TPU v7x, 256 devices: a whole 4x4x8 slice. The times are simulated.
256 devices in a mesh: port: 4 (over z_hi), tile: 64 (over x, z_lo, y, core).
Axes of the slice: x: 4, y: 4, z: 8 (z_hi: 4, z_lo: 2; z = z_hi * 2 + z_lo), core: 2. Of those that a mesh axis runs over, the one named last changes fastest.
Arguments:
- e_start: float32 [4, 3, 1024, 4, 2048], P('port', None, 'tile'), may hold values from -6 to 6
- h_start: float32 [4, 3, 1024, 4, 2048], P('port', None, 'tile'), may hold values from -6 to 6
- forward: bfloat16 [4, 2, 2, 3, 1024, 4, 2048], P('port', None, None, None, 'tile'), may hold values from -6 to 6
- density: float32 [1024, 4, 2048], P('tile'), may hold values from 0 to 10
- material: int32 [1024, 4, 16], P('tile'), may hold values from 0 to 3
- design: int32 [1024, 4, 16], P('tile'), may hold values 0 or 1
- eps_table: float32 [4], replicated, may hold values from 1.5 to 12
- profiles: float32 [4, 2048], replicated, may hold values from -6 to 6
- port_mode: int32 [4], P('port'), may hold values from 0 to 3
Outputs:
- e_final: float32 [4, 3, 1024, 4, 2048], P('port', None, 'tile')
- h_final: float32 [4, 3, 1024, 4, 2048], P('port', None, 'tile')
- gradient: float32 [1024, 4, 2048], P('tile', 'port')
- intersections: float32 [4, 2, 2], P('port')
All inputs are finite; a program needn't handle non-finite values. No bound on the sum of `design` on one device may be relied on, other than what follows from the above.
Results may differ from a plain program's by a relative error of at most 0.0003.
Values sent between devices are 32-bit elements; how exact they have to be, the bound alone decides.
No kernel may reach another device: no remote copies, remote signals or barrier semaphores. Data moves between devices by JAX's collectives and lax.ppermute only.
A program may use at most 128 MiB of HBM per device.

v0:
```python
import math

import jax
import jax.numpy as jnp
from jax import lax
from jax.sharding import PartitionSpec as P

STEPS = 16


OMEGA = 0.7
COEF_H = 0.5
COEF_E = 0.5


def passed_along(x, axis, by):
    devices = lax.axis_size(axis)
    pairs = [(i, i + by) for i in range(devices) if 0 <= i + by < devices]
    return lax.ppermute(x, axis, pairs)


def shifted(field, axis, edge, ahead):
    count = field.shape[axis]
    if ahead:
        return jnp.concatenate([lax.slice_in_dim(field, 1, count, axis=axis), edge], axis=axis)
    return jnp.concatenate([edge, lax.slice_in_dim(field, 0, count - 1, axis=axis)], axis=axis)


def differ(field, axis, edge, ahead):
    axis = field.ndim + axis
    if edge is None:
        edge = jnp.zeros_like(lax.slice_in_dim(field, 0, 1, axis=axis))
    moved = shifted(field, axis, edge, ahead)
    if ahead:
        return moved - field
    return field - moved


def curl(field, edge_x, ahead):
    comp_x = field[..., 0, :, :, :]
    comp_y = field[..., 1, :, :, :]
    comp_z = field[..., 2, :, :, :]
    edge_y = edge_x[..., 0, :, :, :]
    edge_z = edge_x[..., 1, :, :, :]
    curl_x = differ(comp_z, -1, None, ahead) - differ(comp_y, -2, None, ahead)
    curl_y = differ(comp_x, -2, None, ahead) - differ(comp_z, -3, edge_z, ahead)
    curl_z = differ(comp_y, -3, edge_y, ahead) - differ(comp_x, -1, None, ahead)
    return jnp.stack([curl_x, curl_y, curl_z], axis=-4)


def accumulate(acc_re, acc_im, e_now, moment, omegas):
    cosine = jnp.cos(omegas * moment)[None, :, None, None, None, None]
    sine = jnp.sin(omegas * moment)[None, :, None, None, None, None]
    return (acc_re + cosine * e_now[:, None], acc_im - sine * e_now[:, None])


def body(e_start, h_start, forward, density, material, design, eps_table, profiles, port_mode):
    width = e_start.shape[2]
    slab = e_start.shape[3]
    span = e_start.shape[4]
    tiles = lax.axis_size("tile")
    full_x = width * tiles
    freqs = forward.shape[1]
    mat_cells = jnp.repeat(material, 128, axis=2)
    design_cells = jnp.repeat(design, 128, axis=2).astype(jnp.float32)
    base = jnp.zeros(density.shape, jnp.float32)
    for which in range(eps_table.shape[0]):
        base = base + jnp.where(mat_cells == which, eps_table[which], 0.0)
    eps = base + design_cells * density
    omegas = OMEGA * (jnp.arange(freqs) + 1).astype(jnp.float32)
    zeros = jnp.zeros((e_start.shape[0], freqs) + e_start.shape[1:], jnp.float32)

    def advance(step, carry):
        e_now, h_now, acc_re, acc_im = carry
        next_plane = passed_along(e_now[:, 1:3, 0:1], "tile", -1)
        h_now = h_now - COEF_H * curl(e_now, next_plane, True)
        last_plane = passed_along(h_now[:, 1:3, width - 1 : width], "tile", 1)
        e_now = e_now + COEF_E / eps * curl(h_now, last_plane, False)
        moment = (step + 1).astype(jnp.float32)
        acc_re, acc_im = accumulate(acc_re, acc_im, e_now, moment, omegas)
        return (e_now, h_now, acc_re, acc_im)

    e_now, h_now, acc_re, acc_im = lax.fori_loop(
        0, STEPS, advance, (e_start, h_start, zeros, zeros)
    )
    fields = forward.astype(jnp.float32)
    terms = jnp.sum(fields[:, :, 0] * acc_re - fields[:, :, 1] * acc_im, axis=(0, 1, 2))
    local_grad = design_cells * (terms / STEPS)
    gradient = lax.psum_scatter(local_grad, "port", scatter_dimension=1, tiled=True)
    profile = jnp.zeros((port_mode.shape[0], span), jnp.float32)
    for which in range(profiles.shape[0]):
        profile = profile + jnp.where((port_mode == which)[:, None], profiles[which][None, :], 0.0)
    weight = profile[:, None, None, None, :]
    over_re = jnp.sum(acc_re[:, :, 1] * weight, axis=(2, 3, 4))
    over_im = jnp.sum(acc_im[:, :, 1] * weight, axis=(2, 3, 4))
    partial_over = jnp.stack([over_re, over_im], axis=-1)
    intersections = lax.psum(partial_over, "tile") / math.sqrt(full_x * slab * span)
    return (e_now, h_now, gradient, intersections)


def solution(mesh):
    return jax.shard_map(
        body,
        mesh=mesh,
        in_specs=(
            P("port", None, "tile", None, None),
            P("port", None, "tile", None, None),
            P("port", None, None, None, "tile", None, None),
            P("tile", None, None),
            P("tile", None, None),
            P("tile", None, None),
            P(),
            P(),
            P("port"),
        ),
        out_specs=(
            P("port", None, "tile", None, None),
            P("port", None, "tile", None, None),
            P("tile", "port", None),
            P("port", None, None),
        ),
        check_vma=False,
    )
```

profile of v0, /device:TPU:67, one launch (start us, length us, event | category | flops | bytes accessed | tf_op | source)
XLA Modules:
  0.0 670.1 jit_solution(6580197088449681043)
XLA Ops:
  8.5 2.7 select_add_fusion.1
  13.6 5.8 copy_convert_fusion
  21.0 502.5 %while.20 = (s32[]{:T(128)}, f32[1,3,16,4,2048]{4,3,2,1,0:T(4,128)S(1)}, f32[1,3,16,4,2048]{4,3,2,1,0:T(4,128)S(1)}, f32[1,2,3,16,4,2048]{5,4,3,2,1,0:T(4,128)},...) while((s32[]{:T(128)}, ...), condition=%wide.region_1.2_spmd.clone, body=%wide.region_0.1_spmd.clone.sunk | while | flops 12451851 | bytes 109836680 | solution.py:83
  21.0 2.6 collective-permute-start
  31.6 2.8 subtract_bitcast_fusion.4
  35.3 3.1 collective-permute-start.1
  38.6 3.1 collective-permute-done.1
  45.8 2.5 select_subtract_fusion.2
  50.9 7.8 %collective-permute-start = (f32[1,2,1,4,2048]{4,3,2,1,0:T(4,128)S(1)}, f32[1,2,1,4,2048]{4,3,2,1,0:T(4,128)S(1)}, u32[]{:S(2)}, u32[]{:S(2)}) collective-permute-start(f32[1,2,1,4,2048]{4,3,2,1,0:T(4,128)S(1)} %slice.352), channel_id=1, source_target_pairs={{1,0},{2,1},{3,2},{4,3},{5,4},{6,5},{7,6},{8,7},{9,8},{10,9},{11,1... | collective-permute-start | bytes 196616 | tf_op jit(solution)/shard_map/while/body/eval_jaxpr/ppermute | solution.py:19
  66.8 2.8 subtract_bitcast_fusion.4
  77.8 2.5 select_subtract_fusion.2
  83.0 7.3 %collective-permute-start = (f32[1,2,1,4,2048]{4,3,2,1,0:T(4,128)S(1)}, f32[1,2,1,4,2048]{4,3,2,1,0:T(4,128)S(1)}, u32[]{:S(2)}, u32[]{:S(2)}) collective-permute-start(f32[1,2,1,4,2048]{4,3,2,1,0:T(4,128)S(1)} %slice.352), channel_id=1, source_target_pairs={{1,0},{2,1},{3,2},{4,3},{5,4},{6,5},{7,6},{8,7},{9,8},{10,9},{11,1... | collective-permute-start | bytes 196616 | tf_op jit(solution)/shard_map/while/body/eval_jaxpr/ppermute | solution.py:19
  98.3 2.8 subtract_bitcast_fusion.4
  109.3 2.5 select_subtract_fusion.2
  114.4 7.3 %collective-permute-start = (f32[1,2,1,4,2048]{4,3,2,1,0:T(4,128)S(1)}, f32[1,2,1,4,2048]{4,3,2,1,0:T(4,128)S(1)}, u32[]{:S(2)}, u32[]{:S(2)}) collective-permute-start(f32[1,2,1,4,2048]{4,3,2,1,0:T(4,128)S(1)} %slice.352), channel_id=1, source_target_pairs={{1,0},{2,1},{3,2},{4,3},{5,4},{6,5},{7,6},{8,7},{9,8},{10,9},{11,1... | collective-permute-start | bytes 196616 | tf_op jit(solution)/shard_map/while/body/eval_jaxpr/ppermute | solution.py:19
  129.8 2.8 subtract_bitcast_fusion.4
  140.8 2.5 select_subtract_fusion.2
  145.9 7.3 %collective-permute-start = (f32[1,2,1,4,2048]{4,3,2,1,0:T(4,128)S(1)}, f32[1,2,1,4,2048]{4,3,2,1,0:T(4,128)S(1)}, u32[]{:S(2)}, u32[]{:S(2)}) collective-permute-start(f32[1,2,1,4,2048]{4,3,2,1,0:T(4,128)S(1)} %slice.352), channel_id=1, source_target_pairs={{1,0},{2,1},{3,2},{4,3},{5,4},{6,5},{7,6},{8,7},{9,8},{10,9},{11,1... | collective-permute-start | bytes 196616 | tf_op jit(solution)/shard_map/while/body/eval_jaxpr/ppermute | solution.py:19
  161.2 2.8 subtract_bitcast_fusion.4
  172.2 2.5 select_subtract_fusion.2
  177.4 7.3 %collective-permute-start = (f32[1,2,1,4,2048]{4,3,2,1,0:T(4,128)S(1)}, f32[1,2,1,4,2048]{4,3,2,1,0:T(4,128)S(1)}, u32[]{:S(2)}, u32[]{:S(2)}) collective-permute-start(f32[1,2,1,4,2048]{4,3,2,1,0:T(4,128)S(1)} %slice.352), channel_id=1, source_target_pairs={{1,0},{2,1},{3,2},{4,3},{5,4},{6,5},{7,6},{8,7},{9,8},{10,9},{11,1... | collective-permute-start | bytes 196616 | tf_op jit(solution)/shard_map/while/body/eval_jaxpr/ppermute | solution.py:19
  192.7 2.8 subtract_bitcast_fusion.4
  203.7 2.5 select_subtract_fusion.2
  208.8 7.3 %collective-permute-start = (f32[1,2,1,4,2048]{4,3,2,1,0:T(4,128)S(1)}, f32[1,2,1,4,2048]{4,3,2,1,0:T(4,128)S(1)}, u32[]{:S(2)}, u32[]{:S(2)}) collective-permute-start(f32[1,2,1,4,2048]{4,3,2,1,0:T(4,128)S(1)} %slice.352), channel_id=1, source_target_pairs={{1,0},{2,1},{3,2},{4,3},{5,4},{6,5},{7,6},{8,7},{9,8},{10,9},{11,1... | collective-permute-start | bytes 196616 | tf_op jit(solution)/shard_map/while/body/eval_jaxpr/ppermute | solution.py:19
  224.2 2.8 subtract_bitcast_fusion.4
  235.2 2.5 select_subtract_fusion.2
  240.3 7.3 %collective-permute-start = (f32[1,2,1,4,2048]{4,3,2,1,0:T(4,128)S(1)}, f32[1,2,1,4,2048]{4,3,2,1,0:T(4,128)S(1)}, u32[]{:S(2)}, u32[]{:S(2)}) collective-permute-start(f32[1,2,1,4,2048]{4,3,2,1,0:T(4,128)S(1)} %slice.352), channel_id=1, source_target_pairs={{1,0},{2,1},{3,2},{4,3},{5,4},{6,5},{7,6},{8,7},{9,8},{10,9},{11,1... | collective-permute-start | bytes 196616 | tf_op jit(solution)/shard_map/while/body/eval_jaxpr/ppermute | solution.py:19
  255.6 2.8 subtract_bitcast_fusion.4
  271.8 7.3 %collective-permute-start = (f32[1,2,1,4,2048]{4,3,2,1,0:T(4,128)S(1)}, f32[1,2,1,4,2048]{4,3,2,1,0:T(4,128)S(1)}, u32[]{:S(2)}, u32[]{:S(2)}) collective-permute-start(f32[1,2,1,4,2048]{4,3,2,1,0:T(4,128)S(1)} %slice.352), channel_id=1, source_target_pairs={{1,0},{2,1},{3,2},{4,3},{5,4},{6,5},{7,6},{8,7},{9,8},{10,9},{11,1... | collective-permute-start | bytes 196616 | tf_op jit(solution)/shard_map/while/body/eval_jaxpr/ppermute | solution.py:19
  287.1 2.8 subtract_bitcast_fusion.4
  303.2 7.3 %collective-permute-start = (f32[1,2,1,4,2048]{4,3,2,1,0:T(4,128)S(1)}, f32[1,2,1,4,2048]{4,3,2,1,0:T(4,128)S(1)}, u32[]{:S(2)}, u32[]{:S(2)}) collective-permute-start(f32[1,2,1,4,2048]{4,3,2,1,0:T(4,128)S(1)} %slice.352), channel_id=1, source_target_pairs={{1,0},{2,1},{3,2},{4,3},{5,4},{6,5},{7,6},{8,7},{9,8},{10,9},{11,1... | collective-permute-start | bytes 196616 | tf_op jit(solution)/shard_map/while/body/eval_jaxpr/ppermute | solution.py:19
  318.6 2.8 subtract_bitcast_fusion.4
  334.7 7.3 %collective-permute-start = (f32[1,2,1,4,2048]{4,3,2,1,0:T(4,128)S(1)}, f32[1,2,1,4,2048]{4,3,2,1,0:T(4,128)S(1)}, u32[]{:S(2)}, u32[]{:S(2)}) collective-permute-start(f32[1,2,1,4,2048]{4,3,2,1,0:T(4,128)S(1)} %slice.352), channel_id=1, source_target_pairs={{1,0},{2,1},{3,2},{4,3},{5,4},{6,5},{7,6},{8,7},{9,8},{10,9},{11,1... | collective-permute-start | bytes 196616 | tf_op jit(solution)/shard_map/while/body/eval_jaxpr/ppermute | solution.py:19
  350.0 2.8 subtract_bitcast_fusion.4
  366.2 7.3 %collective-permute-start = (f32[1,2,1,4,2048]{4,3,2,1,0:T(4,128)S(1)}, f32[1,2,1,4,2048]{4,3,2,1,0:T(4,128)S(1)}, u32[]{:S(2)}, u32[]{:S(2)}) collective-permute-start(f32[1,2,1,4,2048]{4,3,2,1,0:T(4,128)S(1)} %slice.352), channel_id=1, source_target_pairs={{1,0},{2,1},{3,2},{4,3},{5,4},{6,5},{7,6},{8,7},{9,8},{10,9},{11,1... | collective-permute-start | bytes 196616 | tf_op jit(solution)/shard_map/while/body/eval_jaxpr/ppermute | solution.py:19
  381.5 2.8 subtract_bitcast_fusion.4
  397.6 7.3 %collective-permute-start = (f32[1,2,1,4,2048]{4,3,2,1,0:T(4,128)S(1)}, f32[1,2,1,4,2048]{4,3,2,1,0:T(4,128)S(1)}, u32[]{:S(2)}, u32[]{:S(2)}) collective-permute-start(f32[1,2,1,4,2048]{4,3,2,1,0:T(4,128)S(1)} %slice.352), channel_id=1, source_target_pairs={{1,0},{2,1},{3,2},{4,3},{5,4},{6,5},{7,6},{8,7},{9,8},{10,9},{11,1... | collective-permute-start | bytes 196616 | tf_op jit(solution)/shard_map/while/body/eval_jaxpr/ppermute | solution.py:19
  413.0 2.8 subtract_bitcast_fusion.4
  424.0 2.5 select_subtract_fusion.2
  429.1 7.3 %collective-permute-start = (f32[1,2,1,4,2048]{4,3,2,1,0:T(4,128)S(1)}, f32[1,2,1,4,2048]{4,3,2,1,0:T(4,128)S(1)}, u32[]{:S(2)}, u32[]{:S(2)}) collective-permute-start(f32[1,2,1,4,2048]{4,3,2,1,0:T(4,128)S(1)} %slice.352), channel_id=1, source_target_pairs={{1,0},{2,1},{3,2},{4,3},{5,4},{6,5},{7,6},{8,7},{9,8},{10,9},{11,1... | collective-permute-start | bytes 196616 | tf_op jit(solution)/shard_map/while/body/eval_jaxpr/ppermute | solution.py:19
  444.4 2.8 subtract_bitcast_fusion.4
  460.6 7.3 %collective-permute-start = (f32[1,2,1,4,2048]{4,3,2,1,0:T(4,128)S(1)}, f32[1,2,1,4,2048]{4,3,2,1,0:T(4,128)S(1)}, u32[]{:S(2)}, u32[]{:S(2)}) collective-permute-start(f32[1,2,1,4,2048]{4,3,2,1,0:T(4,128)S(1)} %slice.352), channel_id=1, source_target_pairs={{1,0},{2,1},{3,2},{4,3},{5,4},{6,5},{7,6},{8,7},{9,8},{10,9},{11,1... | collective-permute-start | bytes 196616 | tf_op jit(solution)/shard_map/while/body/eval_jaxpr/ppermute | solution.py:19
  475.9 2.8 subtract_bitcast_fusion.4
  486.9 2.5 select_subtract_fusion.2
  492.0 7.3 %collective-permute-start = (f32[1,2,1,4,2048]{4,3,2,1,0:T(4,128)S(1)}, f32[1,2,1,4,2048]{4,3,2,1,0:T(4,128)S(1)}, u32[]{:S(2)}, u32[]{:S(2)}) collective-permute-start(f32[1,2,1,4,2048]{4,3,2,1,0:T(4,128)S(1)} %slice.352), channel_id=1, source_target_pairs={{1,0},{2,1},{3,2},{4,3},{5,4},{6,5},{7,6},{8,7},{9,8},{10,9},{11,1... | collective-permute-start | bytes 196616 | tf_op jit(solution)/shard_map/while/body/eval_jaxpr/ppermute | solution.py:19
  507.4 2.8 subtract_bitcast_fusion.4
  523.5 7.4 %fusion.16 = f32[16,4,2048]{2,1,0:T(4,128)S(1)} fusion(f32[1,2,3,16,4,2048]{5,4,3,2,1,0:T(4,128)} %get-tuple-element.134, f32[1,2,2,3,16,4,2048]{6,5,4,3,1,2,0:T(4,128)} %copy_convert_fusion, f32[1,2,3,16,4,2048]{5,4,3,2,1,0:T(4,128)} %get-tuple-element.133), kind=kLoop, calls=%fused_computation.38 | loop fusion | flops 3014656 | bytes 13107200 | tf_op jit(solution)/shard_map/reduce_sum | solution.py:87
  535.2 125.7 %psum.7 = f32[1,2,2]{1,2,0:T(2,128)S(1)} all-reduce(f32[1,2,2]{1,2,0:T(2,128)S(1)} %pad_maximum_fusion), channel_id=1, replica_groups=mesh['port'=4,'tile'=64] {'tile'}, use_global_device_ids=true, to_apply=%region_6.7 | all-reduce | flops 4 | bytes 32 | tf_op jit(solution)/shard_map/psum | solution.py:97
  (577 shorter events, 325.4 us)
Async XLA Ops:
  7.2 654.4 %reduce-scatter.2.cloned.1.call-start = ((), (), s32[]{:S(2)}) async-start(), calls=%async_computation.1 | async-start | bytes 655360 | tf_op jit(solution)/shard_map/reduce_scatter | solution.py:89
  7.2 5.1 copy-start.14
  13.6 5.8 copy-start.9
  13.6 5.8 copy-start.11
  13.6 5.8 copy-start.12
  13.6 6.7 copy-start.3
  21.0 10.6 %collective-permute-start = (f32[1,2,1,4,2048]{4,3,2,1,0:T(4,128)S(1)}, f32[1,2,1,4,2048]{4,3,2,1,0:T(4,128)S(1)}, u32[]{:S(2)}, u32[]{:S(2)}) collective-permute-start(f32[1,2,1,4,2048]{4,3,2,1,0:T(4,128)S(1)} %slice.352), channel_id=1, source_target_pairs={{1,0},{2,1},{3,2},{4,3},{5,4},{6,5},{7,6},{8,7},{9,8},{10,9},{11,1... | collective-permute-start | bytes 196616 | tf_op jit(solution)/shard_map/while/body/eval_jaxpr/ppermute | solution.py:19
  35.3 6.4 collective-permute-start.1
  48.3 2.6 copy-start.7
  50.9 15.9 %collective-permute-start = (f32[1,2,1,4,2048]{4,3,2,1,0:T(4,128)S(1)}, f32[1,2,1,4,2048]{4,3,2,1,0:T(4,128)S(1)}, u32[]{:S(2)}, u32[]{:S(2)}) collective-permute-start(f32[1,2,1,4,2048]{4,3,2,1,0:T(4,128)S(1)} %slice.352), channel_id=1, source_target_pairs={{1,0},{2,1},{3,2},{4,3},{5,4},{6,5},{7,6},{8,7},{9,8},{10,9},{11,1... | collective-permute-start | bytes 196616 | tf_op jit(solution)/shard_map/while/body/eval_jaxpr/ppermute | solution.py:19
  70.5 3.2 collective-permute-start.1
  80.4 2.6 copy-start.7
  83.0 15.3 %collective-permute-start = (f32[1,2,1,4,2048]{4,3,2,1,0:T(4,128)S(1)}, f32[1,2,1,4,2048]{4,3,2,1,0:T(4,128)S(1)}, u32[]{:S(2)}, u32[]{:S(2)}) collective-permute-start(f32[1,2,1,4,2048]{4,3,2,1,0:T(4,128)S(1)} %slice.352), channel_id=1, source_target_pairs={{1,0},{2,1},{3,2},{4,3},{5,4},{6,5},{7,6},{8,7},{9,8},{10,9},{11,1... | collective-permute-start | bytes 196616 | tf_op jit(solution)/shard_map/while/body/eval_jaxpr/ppermute | solution.py:19
  102.0 3.2 collective-permute-start.1
  114.4 15.3 %collective-permute-start = (f32[1,2,1,4,2048]{4,3,2,1,0:T(4,128)S(1)}, f32[1,2,1,4,2048]{4,3,2,1,0:T(4,128)S(1)}, u32[]{:S(2)}, u32[]{:S(2)}) collective-permute-start(f32[1,2,1,4,2048]{4,3,2,1,0:T(4,128)S(1)} %slice.352), channel_id=1, source_target_pairs={{1,0},{2,1},{3,2},{4,3},{5,4},{6,5},{7,6},{8,7},{9,8},{10,9},{11,1... | collective-permute-start | bytes 196616 | tf_op jit(solution)/shard_map/while/body/eval_jaxpr/ppermute | solution.py:19
  133.4 3.2 collective-permute-start.1
  145.9 15.3 %collective-permute-start = (f32[1,2,1,4,2048]{4,3,2,1,0:T(4,128)S(1)}, f32[1,2,1,4,2048]{4,3,2,1,0:T(4,128)S(1)}, u32[]{:S(2)}, u32[]{:S(2)}) collective-permute-start(f32[1,2,1,4,2048]{4,3,2,1,0:T(4,128)S(1)} %slice.352), channel_id=1, source_target_pairs={{1,0},{2,1},{3,2},{4,3},{5,4},{6,5},{7,6},{8,7},{9,8},{10,9},{11,1... | collective-permute-start | bytes 196616 | tf_op jit(solution)/shard_map/while/body/eval_jaxpr/ppermute | solution.py:19
  164.9 3.2 collective-permute-start.1
  177.4 15.3 %collective-permute-start = (f32[1,2,1,4,2048]{4,3,2,1,0:T(4,128)S(1)}, f32[1,2,1,4,2048]{4,3,2,1,0:T(4,128)S(1)}, u32[]{:S(2)}, u32[]{:S(2)}) collective-permute-start(f32[1,2,1,4,2048]{4,3,2,1,0:T(4,128)S(1)} %slice.352), channel_id=1, source_target_pairs={{1,0},{2,1},{3,2},{4,3},{5,4},{6,5},{7,6},{8,7},{9,8},{10,9},{11,1... | collective-permute-start | bytes 196616 | tf_op jit(solution)/shard_map/while/body/eval_jaxpr/ppermute | solution.py:19
  196.4 3.2 collective-permute-start.1
  208.8 15.3 %collective-permute-start = (f32[1,2,1,4,2048]{4,3,2,1,0:T(4,128)S(1)}, f32[1,2,1,4,2048]{4,3,2,1,0:T(4,128)S(1)}, u32[]{:S(2)}, u32[]{:S(2)}) collective-permute-start(f32[1,2,1,4,2048]{4,3,2,1,0:T(4,128)S(1)} %slice.352), channel_id=1, source_target_pairs={{1,0},{2,1},{3,2},{4,3},{5,4},{6,5},{7,6},{8,7},{9,8},{10,9},{11,1... | collective-permute-start | bytes 196616 | tf_op jit(solution)/shard_map/while/body/eval_jaxpr/ppermute | solution.py:19
  227.8 3.2 collective-permute-start.1
  237.7 2.6 copy-start.7
  240.3 15.3 %collective-permute-start = (f32[1,2,1,4,2048]{4,3,2,1,0:T(4,128)S(1)}, f32[1,2,1,4,2048]{4,3,2,1,0:T(4,128)S(1)}, u32[]{:S(2)}, u32[]{:S(2)}) collective-permute-start(f32[1,2,1,4,2048]{4,3,2,1,0:T(4,128)S(1)} %slice.352), channel_id=1, source_target_pairs={{1,0},{2,1},{3,2},{4,3},{5,4},{6,5},{7,6},{8,7},{9,8},{10,9},{11,1... | collective-permute-start | bytes 196616 | tf_op jit(solution)/shard_map/while/body/eval_jaxpr/ppermute | solution.py:19
  259.3 3.2 collective-permute-start.1
  271.8 15.3 %collective-permute-start = (f32[1,2,1,4,2048]{4,3,2,1,0:T(4,128)S(1)}, f32[1,2,1,4,2048]{4,3,2,1,0:T(4,128)S(1)}, u32[]{:S(2)}, u32[]{:S(2)}) collective-permute-start(f32[1,2,1,4,2048]{4,3,2,1,0:T(4,128)S(1)} %slice.352), channel_id=1, source_target_pairs={{1,0},{2,1},{3,2},{4,3},{5,4},{6,5},{7,6},{8,7},{9,8},{10,9},{11,1... | collective-permute-start | bytes 196616 | tf_op jit(solution)/shard_map/while/body/eval_jaxpr/ppermute | solution.py:19
  290.8 3.2 collective-permute-start.1
  300.6 2.6 copy-start.7
  303.2 15.3 %collective-permute-start = (f32[1,2,1,4,2048]{4,3,2,1,0:T(4,128)S(1)}, f32[1,2,1,4,2048]{4,3,2,1,0:T(4,128)S(1)}, u32[]{:S(2)}, u32[]{:S(2)}) collective-permute-start(f32[1,2,1,4,2048]{4,3,2,1,0:T(4,128)S(1)} %slice.352), channel_id=1, source_target_pairs={{1,0},{2,1},{3,2},{4,3},{5,4},{6,5},{7,6},{8,7},{9,8},{10,9},{11,1... | collective-permute-start | bytes 196616 | tf_op jit(solution)/shard_map/while/body/eval_jaxpr/ppermute | solution.py:19
  322.2 3.2 collective-permute-start.1
  334.7 15.3 %collective-permute-start = (f32[1,2,1,4,2048]{4,3,2,1,0:T(4,128)S(1)}, f32[1,2,1,4,2048]{4,3,2,1,0:T(4,128)S(1)}, u32[]{:S(2)}, u32[]{:S(2)}) collective-permute-start(f32[1,2,1,4,2048]{4,3,2,1,0:T(4,128)S(1)} %slice.352), channel_id=1, source_target_pairs={{1,0},{2,1},{3,2},{4,3},{5,4},{6,5},{7,6},{8,7},{9,8},{10,9},{11,1... | collective-permute-start | bytes 196616 | tf_op jit(solution)/shard_map/while/body/eval_jaxpr/ppermute | solution.py:19
  353.7 3.2 collective-permute-start.1
  363.5 2.6 copy-start.7
  366.2 15.3 %collective-permute-start = (f32[1,2,1,4,2048]{4,3,2,1,0:T(4,128)S(1)}, f32[1,2,1,4,2048]{4,3,2,1,0:T(4,128)S(1)}, u32[]{:S(2)}, u32[]{:S(2)}) collective-permute-start(f32[1,2,1,4,2048]{4,3,2,1,0:T(4,128)S(1)} %slice.352), channel_id=1, source_target_pairs={{1,0},{2,1},{3,2},{4,3},{5,4},{6,5},{7,6},{8,7},{9,8},{10,9},{11,1... | collective-permute-start | bytes 196616 | tf_op jit(solution)/shard_map/while/body/eval_jaxpr/ppermute | solution.py:19
  385.2 3.2 collective-permute-start.1
  397.6 15.3 %collective-permute-start = (f32[1,2,1,4,2048]{4,3,2,1,0:T(4,128)S(1)}, f32[1,2,1,4,2048]{4,3,2,1,0:T(4,128)S(1)}, u32[]{:S(2)}, u32[]{:S(2)}) collective-permute-start(f32[1,2,1,4,2048]{4,3,2,1,0:T(4,128)S(1)} %slice.352), channel_id=1, source_target_pairs={{1,0},{2,1},{3,2},{4,3},{5,4},{6,5},{7,6},{8,7},{9,8},{10,9},{11,1... | collective-permute-start | bytes 196616 | tf_op jit(solution)/shard_map/while/body/eval_jaxpr/ppermute | solution.py:19
  416.6 3.2 collective-permute-start.1
  426.5 2.6 copy-start.7
  429.1 15.3 %collective-permute-start = (f32[1,2,1,4,2048]{4,3,2,1,0:T(4,128)S(1)}, f32[1,2,1,4,2048]{4,3,2,1,0:T(4,128)S(1)}, u32[]{:S(2)}, u32[]{:S(2)}) collective-permute-start(f32[1,2,1,4,2048]{4,3,2,1,0:T(4,128)S(1)} %slice.352), channel_id=1, source_target_pairs={{1,0},{2,1},{3,2},{4,3},{5,4},{6,5},{7,6},{8,7},{9,8},{10,9},{11,1... | collective-permute-start | bytes 196616 | tf_op jit(solution)/shard_map/while/body/eval_jaxpr/ppermute | solution.py:19
  448.1 3.2 collective-permute-start.1
  460.6 15.3 %collective-permute-start = (f32[1,2,1,4,2048]{4,3,2,1,0:T(4,128)S(1)}, f32[1,2,1,4,2048]{4,3,2,1,0:T(4,128)S(1)}, u32[]{:S(2)}, u32[]{:S(2)}) collective-permute-start(f32[1,2,1,4,2048]{4,3,2,1,0:T(4,128)S(1)} %slice.352), channel_id=1, source_target_pairs={{1,0},{2,1},{3,2},{4,3},{5,4},{6,5},{7,6},{8,7},{9,8},{10,9},{11,1... | collective-permute-start | bytes 196616 | tf_op jit(solution)/shard_map/while/body/eval_jaxpr/ppermute | solution.py:19
  479.6 3.2 collective-permute-start.1
  489.4 2.6 copy-start.7
  492.0 15.3 %collective-permute-start = (f32[1,2,1,4,2048]{4,3,2,1,0:T(4,128)S(1)}, f32[1,2,1,4,2048]{4,3,2,1,0:T(4,128)S(1)}, u32[]{:S(2)}, u32[]{:S(2)}) collective-permute-start(f32[1,2,1,4,2048]{4,3,2,1,0:T(4,128)S(1)} %slice.352), channel_id=1, source_target_pairs={{1,0},{2,1},{3,2},{4,3},{5,4},{6,5},{7,6},{8,7},{9,8},{10,9},{11,1... | collective-permute-start | bytes 196616 | tf_op jit(solution)/shard_map/while/body/eval_jaxpr/ppermute | solution.py:19
  511.0 3.2 collective-permute-start.1
  523.5 7.5 %copy-start = (f32[1,3,16,4,2048]{4,3,2,1,0:T(4,128)}, f32[1,3,16,4,2048]{4,3,2,1,0:T(4,128)S(1)}, u32[]{:S(2)}) copy-start(f32[1,3,16,4,2048]{4,3,2,1,0:T(4,128)S(1)} %get-tuple-element.172) | copy-start | bytes 4718596
  523.5 7.5 %copy-start.2 = (f32[1,3,16,4,2048]{4,3,2,1,0:T(4,128)}, f32[1,3,16,4,2048]{4,3,2,1,0:T(4,128)S(1)}, u32[]{:S(2)}) copy-start(f32[1,3,16,4,2048]{4,3,2,1,0:T(4,128)S(1)} %get-tuple-element.173) | copy-start | bytes 4718596
  523.5 7.5 %copy-start.10 = (f32[16,4,2048]{2,1,0:T(4,128)S(1)}, f32[16,4,2048]{2,1,0:T(4,128)}, u32[]{:S(2)}) copy-start(f32[16,4,2048]{2,1,0:T(4,128)} %convert_element_type.21) | copy-start | bytes 1572868
  (77 other events, 139.3 us)
Sparse Core Ops, SparseCore 0:
  532.4 29.4 reduce-scatter.1
where the time goes:
time: 674 us; the launch traced here: 670 us
  other arithmetic  193 us (29%)
  local copies, waits for them, and re-layouts  172 us (26%)
  starting transfers between devices  144 us (21%)
  blocking collectives  126 us (19%)
  waiting for transfers between devices  18.9 us (3%)
  between operations  14.8 us (2%)
    ppermute x32, starting transfers between devices, passed_along(): return lax.ppermute(x, axis, pairs)  144 us
    psum x1, blocking collectives, body(): lax.psum(partial_over, 'tile') / math.sqrt(full_x * slab * span)  126 us
    slice x96, local copies, waits for them, and re-layouts, shifted(): lax.slice_in_dim(field, 1, count, axis=axis)  94.4 us
    while x160, local copies, waits for them, and re-layouts  63.6 us
    another operation x32, other arithmetic, curl(): return jnp.stack([curl_x, curl_y, curl_z], axis=-4)  61.4 us
    sub x16, other arithmetic, accumulate(): return (acc_re + cosine * e_now[:, None], acc_im - sine * e_now[:, None])  40.1 us
    div x16, other arithmetic, advance(): e_now = e_now + COEF_E / eps * curl(h_now, last_plane, False)  31.7 us
    ppermute x32, waiting for transfers between devices, passed_along(): return lax.ppermute(x, axis, pairs)  18.9 us
  transfers between devices with their start and end apart: 33, of which 16 were waited for; matrix products, arithmetic and copies ran while one was open for 20% of the time, Pallas kernels for 0%

commit v1 on v0

v1 whole, which is shorter than its diff:
```python
import functools
import math

import jax
import jax.numpy as jnp
import numpy as np
from jax import lax
from jax.experimental import pallas as pl
from jax.experimental.pallas import tpu as pltpu
from jax.sharding import PartitionSpec as P

STEPS = 16
OMEGA = 0.7
COEF_H = 0.5
COEF_E = 0.5

WIDTH = 16
SLAB = 4
HALF = 2
DEPTH = STEPS // 2
FREQS = 2
CELLS = (SLAB, HALF, 8, 128)


def rows(x):
    lead = x.shape[:-2]
    x = x.reshape(lead + (SLAB, 16, 128))
    return jnp.swapaxes(x, -3, -2).reshape(lead + (64, 128))


def unrows(x):
    lead = x.shape[:-2]
    x = x.reshape(lead + (16, SLAB, 128))
    return jnp.swapaxes(x, -3, -2).reshape(lead + (SLAB, 2048))


def masks():
    lane = lax.broadcasted_iota(jnp.int32, (8, 128), 1)
    sub = lax.broadcasted_iota(jnp.int32, (8, 128), 0)
    return lane == 127, lane == 0, sub == 7, sub == 0


def ahead_y(pair, m):
    r0 = pltpu.roll(pair[0], 127, 1)
    r1 = pltpu.roll(pair[1], 127, 1)
    rs = jnp.where(m[2], 0.0, pltpu.roll(r0, 7, 0))
    return jnp.where(m[0], r1, r0), jnp.where(m[0], rs, r1)


def behind_y(pair, m):
    r0 = pltpu.roll(pair[0], 1, 1)
    r1 = pltpu.roll(pair[1], 1, 1)
    rs = jnp.where(m[3], 0.0, pltpu.roll(r1, 1, 0))
    return jnp.where(m[1], rs, r0), jnp.where(m[1], r0, r1)


def update_plane(e_old, e_next, h_now, h_prev, coef, e_new, m):
    def pair(ref, comp, z):
        return [ref[comp, z, v] for v in range(HALF)]

    ex, ey = pair(e_old, 0, 0), pair(e_old, 1, 0)
    below = None
    for z in range(SLAB):
        ez = pair(e_old, 2, z)
        ex_up = pair(e_old, 0, z + 1) if z + 1 < SLAB else [0.0, 0.0]
        ey_up = pair(e_old, 1, z + 1) if z + 1 < SLAB else [0.0, 0.0]
        ey_x, ez_x = pair(e_next, 1, z), pair(e_next, 2, z)
        ez_y, ex_y = ahead_y(ez, m), ahead_y(ex, m)
        hx, hy, hz = pair(h_now, 0, z), pair(h_now, 1, z), pair(h_now, 2, z)
        for v in range(HALF):
            hx[v] = hx[v] - ((ez_y[v] - ez[v]) - (ey_up[v] - ey[v]))
            hy[v] = hy[v] - ((ex_up[v] - ex[v]) - (ez_x[v] - ez[v]))
            hz[v] = hz[v] - ((ey_x[v] - ey[v]) - (ex_y[v] - ex[v]))
            h_now[0, z, v] = hx[v]
            h_now[1, z, v] = hy[v]
            h_now[2, z, v] = hz[v]
        hz_y, hx_y = behind_y(hz, m), behind_y(hx, m)
        hy_x, hz_x = pair(h_prev, 1, z), pair(h_prev, 2, z)
        hx_z, hy_z = below if z > 0 else ([0.0, 0.0], [0.0, 0.0])
        for v in range(HALF):
            c = coef[z, v]
            e_new[0, z, v] = ex[v] + c * ((hz[v] - hz_y[v]) - (hy[v] - hy_z[v]))
            e_new[1, z, v] = ey[v] + c * ((hx[v] - hx_z[v]) - (hz[v] - hz_x[v]))
            e_new[2, z, v] = ez[v] + c * ((hy[v] - hy_x[v]) - (hx[v] - hx_y[v]))
        ex, ey, below = ex_up, ey_up, (hx, hy)


def strided(z, v):
    return pl.ds(4 * v + z, 8, stride=8)


def load_rows(src, dst, dst_base, scale):
    def one(x, _):
        for comp in range(3):
            for z in range(SLAB):
                for v in range(HALF):
                    val = src[comp, x, strided(z, v), :]
                    dst[comp, dst_base + x, z, v] = val if scale == 1.0 else val * scale
        return 0

    lax.fori_loop(0, WIDTH, one, 0)


def coef_kernel(table, mat, des, dens, coef, mask):
    kind = mat[...]
    base = jnp.zeros((8, 128), jnp.float32)
    for which in range(table.shape[0]):
        base = base + jnp.where(kind == which, table[which], 0.0)
    flag = des[...].astype(jnp.float32)
    for x in range(WIDTH):
        for z in range(SLAB):
            for v in range(HALF):
                at = (x * SLAB + z) * HALF + v
                b = jnp.broadcast_to(base[:, at : at + 1], (8, 128))
                d = jnp.broadcast_to(flag[:, at : at + 1], (8, 128))
                eps = b + d * dens[x, strided(z, v), :]
                coef[x, z, v] = (COEF_E * COEF_H) / eps
                mask[x, z, v] = d * (1.0 / STEPS)


def free_kernel(e_in, h_in, coef, hist_e, hist_h, e, h):
    m = masks()
    load_rows(e_in, e, 0, 1.0)
    load_rows(h_in, h, 1, 1.0 / COEF_H)
    e[:, WIDTH] = jnp.zeros((3,) + CELLS, jnp.float32)
    h[:, 0] = jnp.zeros((3,) + CELLS, jnp.float32)
    hist_e[0] = e[1:3, 0]

    def sweep(low, high):
        def one(x, _):
            update_plane(e.at[:, x], e.at[:, x + 1], h.at[:, x + 1], h.at[:, x], coef.at[x], e.at[:, x], m)
            return 0

        lax.fori_loop(low, high, one, 0)

    def early(s, _):
        sweep(0, WIDTH)
        hist_e[s] = e[1:3, 0]
        hist_h[s - 1] = h[1:3, WIDTH]
        return 0

    def late(s, _):
        sweep(0, WIDTH - s)
        sweep(s - 1, WIDTH)

        @pl.when(s < STEPS)
        def _():
            hist_e[s] = e[1:3, 0]

        hist_h[s - 1] = h[1:3, WIDTH]
        return 0

    lax.fori_loop(1, DEPTH + 1, early, 0)
    lax.fori_loop(DEPTH + 1, STEPS + 1, late, 0)


def full_kernel(
    info, e_in, h_in, coef, coef_l, coef_r, got_e, got_h, forward, mask, profile,
    e_out, h_out, grad, over,
    e, h, el, hl, er, hr, wide, sums,
):
    m = masks()
    load_rows(e_in, e.at[0], 0, 1.0)
    load_rows(h_in, h, 1, 1.0 / COEF_H)
    for ref in (el, hl, er, hr):
        ref[...] = jnp.zeros(ref.shape, jnp.float32)
    inner = (info[0] > 0).astype(jnp.float32)

    def step(s, _):
        before, after = e.at[s - 1], e.at[s]
        n_left = jnp.minimum(s, STEPS + 1 - s)
        n_right = jnp.minimum(s, STEPS - s)
        el[1:3, DEPTH + 1] = before[1:3, 0]
        before[1:3, WIDTH] = er[1:3, 0] + got_e[s - 1]

        def left(x, _):
            update_plane(el.at[:, x], el.at[:, x + 1], hl.at[:, x], hl.at[:, x - 1], coef_l.at[x - 1], el.at[:, x], m)
            return 0

        lax.fori_loop(DEPTH + 1 - n_left, DEPTH + 1, left, 0)
        h[1:3, 0] = hl[1:3, DEPTH] * inner + got_h[s - 1]

        def own(x, _):
            update_plane(before.at[:, x], before.at[:, x + 1], h.at[:, x + 1], h.at[:, x], coef.at[x], after.at[:, x], m)
            return 0

        lax.fori_loop(0, WIDTH, own, 0)
        hr[1:3, 0] = h[1:3, WIDTH]

        def right(x, _):
            update_plane(er.at[:, x], er.at[:, x + 1], hr.at[:, x + 1], hr.at[:, x], coef_r.at[x], er.at[:, x], m)
            return 0

        lax.fori_loop(0, n_right, right, 0)
        return 0

    lax.fori_loop(1, STEPS + 1, step, 0)

    port = info[1]
    omegas = [OMEGA * (f + 1) for f in range(FREQS)]
    mid = (STEPS + 1) / 2
    ca = [float(np.cos(w * mid)) for w in omegas]
    sa = [float(np.sin(w * mid)) for w in omegas]
    sums[...] = jnp.zeros(sums.shape, jnp.float32)

    def finish(x, _):
        for f in range(FREQS):
            for q in range(2):
                for comp in range(3):
                    wide[(f * 2 + q) * 3 + comp] = forward[f, q, comp, x].astype(jnp.float32)
        for z in range(SLAB):
            for v in range(HALF):
                total = None
                for comp in range(3):
                    plus, minus = [], []
                    for i in range(STEPS // 2):
                        lo = e[STEPS // 2 - i, comp, x, z, v]
                        hi = e[STEPS // 2 + 1 + i, comp, x, z, v]
                        plus.append(hi + lo)
                        minus.append(hi - lo)
                    for f in range(FREQS):
                        even = odd = None
                        for i in range(STEPS // 2):
                            c = float(np.cos(omegas[f] * (i + 0.5)))
                            s = float(np.sin(omegas[f] * (i + 0.5)))
                            even = c * plus[i] if even is None else even + c * plus[i]
                            odd = s * minus[i] if odd is None else odd + s * minus[i]
                        if comp == 1:
                            sums[f, 0, v] += even
                            sums[f, 1, v] += odd
                        re = wide[(f * 2) * 3 + comp, strided(z, v), :]
                        im = wide[(f * 2 + 1) * 3 + comp, strided(z, v), :]
                        term = even * (re * ca[f] + im * sa[f]) + odd * (im * ca[f] - re * sa[f])
                        total = term if total is None else total + term
                grad[lax.rem(z - port + SLAB, SLAB), x, v] = mask[x, z, v] * total
                for comp in range(3):
                    e_out[comp, x, strided(z, v), :] = e[STEPS, comp, x, z, v]
                    h_out[comp, x, strided(z, v), :] = h[comp, x + 1, z, v] * COEF_H
        return 0

    lax.fori_loop(0, WIDTH, finish, 0)
    for f in range(FREQS):
        even = sum(sums[f, 0, v] * profile[info[2], v] for v in range(HALF))
        odd = sum(sums[f, 1, v] * profile[info[2], v] for v in range(HALF))
        re = ca[f] * even - sa[f] * odd
        im = -(sa[f] * even + ca[f] * odd)
        for q, val in enumerate((re, im)):
            val = jnp.sum(jnp.sum(val, axis=0, keepdims=True), axis=1, keepdims=True)
            over[2 * f + q : 2 * f + q + 1, :] = jnp.broadcast_to(val, (1, 128))


def sum_kernel(a, b, c, d, out):
    for x in range(WIDTH):
        for v in range(HALF):
            out[x, pl.ds(v, 8, stride=2), :] = (a[x, v] + b[x, v]) + (c[x, v] + d[x, v])


def f32(*shape):
    return jax.ShapeDtypeStruct(shape, jnp.float32)


VMEM = pl.BlockSpec(memory_space=pltpu.VMEM)
SMEM = pl.BlockSpec(memory_space=pltpu.SMEM)
PARAMS = pltpu.CompilerParams(vmem_limit_bytes=58 * 1024 * 1024)


def body(e_start, h_start, forward, density, material, design, eps_table, profiles, port_mode):
    tiles = lax.axis_size("tile")
    ports = lax.axis_size("port")
    tile = lax.axis_index("tile")
    port = lax.axis_index("port")
    to_right = [(i, i + 1) for i in range(tiles - 1)]
    to_left = [(i + 1, i) for i in range(tiles - 1)]

    def by_sublane(x):
        return x.reshape(WIDTH * SLAB, 8, HALF).transpose(1, 0, 2).reshape(8, 128)

    coef, mask = pl.pallas_call(
        coef_kernel,
        out_shape=(f32(WIDTH, *CELLS), f32(WIDTH, *CELLS)),
        in_specs=[SMEM, VMEM, VMEM, VMEM],
        out_specs=(VMEM, VMEM),
        name="coef",
    )(eps_table, by_sublane(material), by_sublane(design), rows(density))
    coef_l = lax.ppermute(coef[WIDTH - DEPTH :], "tile", to_right)
    coef_r = lax.ppermute(coef[:DEPTH], "tile", to_left)

    e_rows, h_rows = rows(e_start[0]), rows(h_start[0])
    hist_e, hist_h = pl.pallas_call(
        free_kernel,
        out_shape=(f32(STEPS, 2, *CELLS), f32(STEPS, 2, *CELLS)),
        in_specs=[VMEM] * 3,
        out_specs=(VMEM, VMEM),
        scratch_shapes=[pltpu.VMEM((3, WIDTH + 1) + CELLS, jnp.float32)] * 2,
        compiler_params=PARAMS,
        name="free",
    )(e_rows, h_rows, coef)
    got_e = lax.ppermute(hist_e, "tile", to_left)
    got_h = lax.ppermute(hist_h, "tile", to_right)

    info = jnp.stack([tile.astype(jnp.int32), port.astype(jnp.int32), port_mode[0]])
    profile = profiles.reshape(-1, 8, HALF, 128).transpose(0, 2, 1, 3)
    e_out, h_out, grad, over = pl.pallas_call(
        full_kernel,
        out_shape=(
            f32(3, WIDTH, 64, 128),
            f32(3, WIDTH, 64, 128),
            f32(SLAB, WIDTH, HALF, 8, 128),
            f32(2 * FREQS, 128),
        ),
        in_specs=[SMEM] + [VMEM] * 10,
        out_specs=(VMEM,) * 4,
        scratch_shapes=[
            pltpu.VMEM((STEPS + 1, 3, WIDTH + 1) + CELLS, jnp.float32),
            pltpu.VMEM((3, WIDTH + 1) + CELLS, jnp.float32),
            pltpu.VMEM((3, DEPTH + 2) + CELLS, jnp.float32),
            pltpu.VMEM((3, DEPTH + 1) + CELLS, jnp.float32),
            pltpu.VMEM((3, DEPTH + 1) + CELLS, jnp.float32),
            pltpu.VMEM((3, DEPTH + 1) + CELLS, jnp.float32),
            pltpu.VMEM((4 * 3, 64, 128), jnp.float32),
            pltpu.VMEM((FREQS, 2, HALF, 8, 128), jnp.float32),
        ],
        compiler_params=PARAMS,
        name="full",
    )(info, e_rows, h_rows, coef, coef_l, coef_r, got_e, got_h, rows(forward[0]), mask, profile)

    parts = [grad[0]]
    for d in range(1, ports):
        parts.append(lax.ppermute(grad[d], "port", [(i, (i + d) % ports) for i in range(ports)]))
    total = over
    span = 1
    while span < tiles:
        radix = min(4, tiles // span)
        got = []
        for d in range(1, radix):
            pairs = []
            for i in range(tiles):
                digit = i // span % radix
                pairs.append((i, i + ((digit + d) % radix - digit) * span))
            got.append(lax.ppermute(total, "tile", pairs))
        total = total + sum(got[1:], got[0])
        span *= radix
    gradient = pl.pallas_call(
        sum_kernel,
        out_shape=f32(WIDTH, 16, 128),
        in_specs=[VMEM] * 4,
        out_specs=VMEM,
        name="total",
    )(*parts)
    scale = math.sqrt(WIDTH * tiles * SLAB * 2048)
    intersections = (total[:, 0] / scale).reshape(1, FREQS, 2)
    return (
        unrows(e_out)[None],
        unrows(h_out)[None],
        gradient.reshape(WIDTH, 1, 2048),
        intersections,
    )


def solution(mesh):
    return jax.shard_map(
        body,
        mesh=mesh,
        in_specs=(
            P("port", None, "tile", None, None),
            P("port", None, "tile", None, None),
            P("port", None, None, None, "tile", None, None),
            P("tile", None, None),
            P("tile", None, None),
            P("tile", None, None),
            P(),
            P(),
            P("port"),
        ),
        out_specs=(
            P("port", None, "tile", None, None),
            P("port", None, "tile", None, None),
            P("tile", "port", None),
            P("port", None, None),
        ),
        check_vma=False,
    )
```

time: 674 us -> 302 us (0.45)
  the two profiles are of different devices: /device:TPU:67 before, /device:TPU:8 now
where the time goes in v1:
time: 302 us; the launch traced here: 301 us
  Pallas kernels  231 us (76%)
  starting transfers between devices  33.5 us (11%)
  waiting for transfers between devices  24.6 us (8%)
  local copies, waits for them, and re-layouts  8.84 us (3%)
    pallas_call x1, Pallas kernels, body(): pl.pallas_call(full_kernel, out_shape=(f32(3, WIDTH, 64, 128), f32(3, WID...  189 us
    pallas_call x1, Pallas kernels, body(): pl.pallas_call(free_kernel, out_shape=(f32(STEPS, 2, *CELLS), f32(STEPS,...  37.4 us
    ppermute x9, starting transfers between devices, body(): got.append(lax.ppermute(total, 'tile', pairs))  14.3 us
    ppermute x3, starting transfers between devices, body(): lax.ppermute(grad[d], 'port', [(i, (i + d) % ports) for i in range(ports)])  9.22 us
    ppermute x3, waiting for transfers between devices, body(): lax.ppermute(grad[d], 'port', [(i, (i + d) % ports) for i in range(ports)])  8.25 us
    ppermute x9, waiting for transfers between devices, body(): got.append(lax.ppermute(total, 'tile', pairs))  6.66 us
  transfers between devices with their start and end apart: 16, of which 8 were waited for; matrix products, arithmetic and copies ran while one was open for 1% of the time, Pallas kernels for 0%

profile of v1, /device:TPU:8, one launch (start us, length us, event | category | flops | bytes accessed | tf_op | source)
XLA Modules:
  0.0 300.8 jit_solution(7231952446215752114)
XLA Ops:
  0.6 0.9 copy.24
  1.6 0.1 reshape.62
  1.7 0.1 copy.25
  1.8 0.7 copy.29.mat
  2.5 0.9 copy.26
  3.4 0.1 reshape.64
  3.5 0.1 copy.27
  3.6 0.7 copy.30.des
  4.3 2.5 coef.1
  6.8 37.4 %free.1 = (f32[16,2,4,2,8,128]{5,4,3,2,1,0:T(8,128)}, f32[16,2,4,2,8,128]{5,4,3,2,1,0:T(8,128)}) custom-call(f32[3,16,64,128]{3,2,1,0:T(8,128)} %bitcast.52, f32[3,16,64,128]{3,2,1,0:T(8,128)} %bitcast.54, f32[16,4,2,8,128]{4,3,2,1,0:T(8,128)} %get-tuple-element.12.coef), custom_call_target="tpu_custom_call" | custom-call | tf_op jit(solution)/shard_map/free/pallas_call | solution.py:289
  44.2 1.9 collective-permute-start.2
  46.1 2.4 collective-permute-start.3
  48.6 3.7 %collective-permute-start.1 = (f32[8,4,2,8,128]{4,3,2,1,0:T(8,128)S(1)}, f32[8,4,2,8,128]{4,3,2,1,0:T(8,128)S(1)}, u32[]{:S(2)}, u32[]{:S(2)}) collective-permute-start(f32[8,4,2,8,128]{4,3,2,1,0:T(8,128)S(1)} %get-tuple-element.32), channel_id=1, source_target_pairs={{1,0},{2,1},{3,2},{4,3},{5,4},{6,5},{7,6},{8,7},{9,8},{10,9},{11,1... | collective-permute-start | bytes 786440 | tf_op jit(solution)/shard_map/ppermute | solution.py:286
  52.3 1.9 collective-permute-start
  55.0 0.6 copy.37
  55.6 0.6 pad_add_fusion.info
  56.2 5.3 %collective-permute-done.1.coef_r = f32[8,4,2,8,128]{4,3,2,1,0:T(8,128)S(1)} collective-permute-done((f32[8,4,2,8,128]{4,3,2,1,0:T(8,128)S(1)}, f32[8,4,2,8,128]{4,3,2,1,0:T(8,128)S(1)}, u32[]{:S(2)}, u32[]{:S(2)}) %collective-permute-start.1) | collective-permute-done | bytes 262176 | tf_op jit(solution)/shard_map/ppermute | solution.py:286
  61.4 4.4 %collective-permute-done.coef_l = f32[8,4,2,8,128]{4,3,2,1,0:T(8,128)S(1)} collective-permute-done((f32[8,4,2,8,128]{4,3,2,1,0:T(8,128)S(1)}, f32[8,4,2,8,128]{4,3,2,1,0:T(8,128)S(1)}, u32[]{:S(2)}, u32[]{:S(2)}) %collective-permute-start) | collective-permute-done | bytes 262176 | tf_op jit(solution)/shard_map/ppermute | solution.py:285
  65.8 0.0 collective-permute-done.2.got_e
  65.8 0.0 collective-permute-done.3.got_h
  65.9 0.7 copy-done.4
  66.5 0.4 copy-done.1
  66.9 0.3 copy-done.2
  67.2 189.4 %full.1 = (f32[3,16,64,128]{3,2,1,0:T(8,128)}, f32[3,16,64,128]{3,2,1,0:T(8,128)}, f32[4,16,2,8,128]{4,3,2,1,0:T(8,128)}, f32[4,128]{1,0:T(4,128)}) custom-call(s32[3]{0:T(128)} %pad_add_fusion.info, f32[3,16,64,128]{3,2,1,0:T(8,128)} %bitcast.53, f32[3,16,64,128]{3,2,1,0:T(8,128)} %bitcast.55, f32[16,4,2,8,128]{4,3,2,1,0:T(8,128)} %get-tuple-element.12.coef, ...), custom_call_target="tpu_custom_call" | custom-call | tf_op jit(solution)/shard_map/full/pallas_call | solution.py:303
  256.6 0.0 collective-permute-start.9
  256.6 0.3 collective-permute-start.8
  256.9 0.2 collective-permute-start.7
  257.1 1.0 collective-permute-done.9
  258.2 2.4 collective-permute-done.8
  260.5 0.7 add_add_fusion.2
  261.2 6.2 %collective-permute-start.12 = (f32[4,128]{1,0:T(4,128)S(1)}, f32[4,128]{1,0:T(4,128)S(1)}, u32[]{:S(2)}, u32[]{:S(2)}) collective-permute-start(f32[4,128]{1,0:T(4,128)S(1)} %add_add_fusion.2), channel_id=1, source_target_pairs={{0,12},{1,13},{2,14},{3,15},{4,0},{5,1},{6,2},{7,3},{8,4},{9,5},{1... | collective-permute-start | bytes 6152 | tf_op jit(solution)/shard_map/ppermute | solution.py:340
  267.4 2.7 collective-permute-start.10
  270.1 0.9 collective-permute-done.11
  270.9 2.4 collective-permute-done.10
  273.3 3.6 %collective-permute-start.15 = (f32[4,128]{1,0:T(4,128)S(1)}, f32[4,128]{1,0:T(4,128)S(1)}, u32[]{:S(2)}, u32[]{:S(2)}) collective-permute-start(f32[4,128]{1,0:T(4,128)S(1)} %add_add_fusion.1), channel_id=1, source_target_pairs={{0,48},{1,49},{2,50},{3,51},{4,52},{5,53},{6,54},{7,55},{8,56},{9,... | collective-permute-start | bytes 6152 | tf_op jit(solution)/shard_map/ppermute | solution.py:340
  276.9 0.5 collective-permute-start.14
  277.4 0.9 collective-permute-start.13
  278.3 1.8 slice_bitcast_fusion
  280.1 5.4 %collective-permute-start.6 = (f32[16,2,8,128]{3,2,1,0:T(8,128)S(1)}, f32[16,2,8,128]{3,2,1,0:T(8,128)S(1)}, u32[]{:S(2)}, u32[]{:S(2)}) collective-permute-start(f32[16,2,8,128]{3,2,1,0:T(8,128)S(1)} %get-tuple-element.28), channel_id=1, source_target_pairs={{0,192},{64,0},{128,64},{192,128},{1,193},{65,1},{129,65},{193,129... | collective-permute-start | bytes 393224 | tf_op jit(solution)/shard_map/ppermute | solution.py:329
  285.5 1.4 collective-permute-start.5
  286.9 2.4 collective-permute-start.4
  289.3 0.1 multiply_reduce_fusion
  289.4 0.6 div.6
  290.1 2.9 collective-permute-done.6.d
  293.0 5.3 %collective-permute-done.5.c = f32[16,2,8,128]{3,2,1,0:T(8,128)S(1)} collective-permute-done((f32[16,2,8,128]{3,2,1,0:T(8,128)S(1)}, f32[16,2,8,128]{3,2,1,0:T(8,128)S(1)}, u32[]{:S(2)}, u32[]{:S(2)}) %collective-permute-start.5) | collective-permute-done | bytes 131104 | tf_op jit(solution)/shard_map/ppermute | solution.py:329
  298.4 0.6 copy-done.6
  299.0 0.0 copy-done.7
  299.0 1.8 total.1
  (24 shorter events, 0.1 us)
Async XLA Ops:
  6.8 41.7 %copy-start = (f32[16,4,2,8,128]{4,3,2,1,0:T(8,128)S(1)}, f32[16,4,2,8,128]{4,3,2,1,0:T(8,128)}, u32[]{:S(2)}) copy-start(f32[16,4,2,8,128]{4,3,2,1,0:T(8,128)} %get-tuple-element.12.coef) | copy-start | bytes 1572868
  6.8 48.1 %copy-start.8 = (f32[4,2048]{1,0:T(4,128)S(1)}, f32[4,2048]{1,0:T(4,128)}, u32[]{:S(2)}) copy-start(f32[4,2048]{1,0:T(4,128)} %param.16) | copy-start | bytes 98308
  44.2 21.6 %collective-permute-start.2 = (f32[16,2,4,2,8,128]{5,4,3,2,1,0:T(8,128)}, f32[16,2,4,2,8,128]{5,4,3,2,1,0:T(8,128)S(1)}, u32[]{:S(2)}, u32[]{:S(2)}) collective-permute-start(f32[16,2,4,2,8,128]{5,4,3,2,1,0:T(8,128)} %get-tuple-element.13), channel_id=1, source_target_pairs={{1,0},{2,1},{3,2},{4,3},{5,4},{6,5},{7,6},{8,7},{9,8},{10,9},{11,1... | collective-permute-start | bytes 3145736 | tf_op jit(solution)/shard_map/ppermute | solution.py:298
  46.1 19.7 %collective-permute-start.3 = (f32[16,2,4,2,8,128]{5,4,3,2,1,0:T(8,128)}, f32[16,2,4,2,8,128]{5,4,3,2,1,0:T(8,128)S(1)}, u32[]{:S(2)}, u32[]{:S(2)}) collective-permute-start(f32[16,2,4,2,8,128]{5,4,3,2,1,0:T(8,128)} %get-tuple-element.14), channel_id=1, source_target_pairs={{0,1},{1,2},{2,3},{3,4},{4,5},{5,6},{6,7},{7,8},{8,9},{9,10},{10,1... | collective-permute-start | bytes 3145736 | tf_op jit(solution)/shard_map/ppermute | solution.py:299
  48.6 12.8 %collective-permute-start.1 = (f32[8,4,2,8,128]{4,3,2,1,0:T(8,128)S(1)}, f32[8,4,2,8,128]{4,3,2,1,0:T(8,128)S(1)}, u32[]{:S(2)}, u32[]{:S(2)}) collective-permute-start(f32[8,4,2,8,128]{4,3,2,1,0:T(8,128)S(1)} %get-tuple-element.32), channel_id=1, source_target_pairs={{1,0},{2,1},{3,2},{4,3},{5,4},{6,5},{7,6},{8,7},{9,8},{10,9},{11,1... | collective-permute-start | bytes 786440 | tf_op jit(solution)/shard_map/ppermute | solution.py:286
  52.3 13.5 %collective-permute-start = (f32[8,4,2,8,128]{4,3,2,1,0:T(8,128)S(1)}, f32[8,4,2,8,128]{4,3,2,1,0:T(8,128)S(1)}, u32[]{:S(2)}, u32[]{:S(2)}) collective-permute-start(f32[8,4,2,8,128]{4,3,2,1,0:T(8,128)S(1)} %get-tuple-element.33), channel_id=1, source_target_pairs={{0,1},{1,2},{2,3},{3,4},{4,5},{5,6},{6,7},{7,8},{8,9},{9,10},{10,1... | collective-permute-start | bytes 786440 | tf_op jit(solution)/shard_map/ppermute | solution.py:285
  61.4 4.4 %copy-start.3 = (f32[8,4,2,8,128]{4,3,2,1,0:T(8,128)}, f32[8,4,2,8,128]{4,3,2,1,0:T(8,128)S(1)}, u32[]{:S(2)}) copy-start(f32[8,4,2,8,128]{4,3,2,1,0:T(8,128)S(1)} %collective-permute-done.1.coef_r) | copy-start | bytes 786436
  65.8 0.7 copy-start.4
  65.8 1.1 copy-start.1
  65.8 1.4 copy-start.2
  256.6 1.5 collective-permute-start.9
  256.6 3.9 %collective-permute-start.8 = (f32[4,128]{1,0:T(4,128)}, f32[4,128]{1,0:T(4,128)S(1)}, u32[]{:S(2)}, u32[]{:S(2)}) collective-permute-start(f32[4,128]{1,0:T(4,128)} %get-tuple-element.19), channel_id=1, source_target_pairs={{0,2},{1,3},{2,0},{3,1},{4,6},{5,7},{6,4},{7,5},{8,10},{9,11},{10,... | collective-permute-start | bytes 6152 | tf_op jit(solution)/shard_map/ppermute | solution.py:340
  256.9 3.6 %collective-permute-start.7 = (f32[4,128]{1,0:T(4,128)}, f32[4,128]{1,0:T(4,128)S(1)}, u32[]{:S(2)}, u32[]{:S(2)}) collective-permute-start(f32[4,128]{1,0:T(4,128)} %get-tuple-element.19), channel_id=1, source_target_pairs={{0,1},{1,2},{2,3},{3,0},{4,5},{5,6},{6,7},{7,4},{8,9},{9,10},{10,1... | collective-permute-start | bytes 6152 | tf_op jit(solution)/shard_map/ppermute | solution.py:340
  261.2 8.9 %collective-permute-start.12 = (f32[4,128]{1,0:T(4,128)S(1)}, f32[4,128]{1,0:T(4,128)S(1)}, u32[]{:S(2)}, u32[]{:S(2)}) collective-permute-start(f32[4,128]{1,0:T(4,128)S(1)} %add_add_fusion.2), channel_id=1, source_target_pairs={{0,12},{1,13},{2,14},{3,15},{4,0},{5,1},{6,2},{7,3},{8,4},{9,5},{1... | collective-permute-start | bytes 6152 | tf_op jit(solution)/shard_map/ppermute | solution.py:340
  267.4 3.6 %collective-permute-start.11 = (f32[4,128]{1,0:T(4,128)S(1)}, f32[4,128]{1,0:T(4,128)S(1)}, u32[]{:S(2)}, u32[]{:S(2)}) collective-permute-start(f32[4,128]{1,0:T(4,128)S(1)} %add_add_fusion.2), channel_id=1, source_target_pairs={{0,8},{1,9},{2,10},{3,11},{4,12},{5,13},{6,14},{7,15},{8,0},{9,1},... | collective-permute-start | bytes 6152 | tf_op jit(solution)/shard_map/ppermute | solution.py:340
  267.4 6.0 %collective-permute-start.10 = (f32[4,128]{1,0:T(4,128)S(1)}, f32[4,128]{1,0:T(4,128)S(1)}, u32[]{:S(2)}, u32[]{:S(2)}) collective-permute-start(f32[4,128]{1,0:T(4,128)S(1)} %add_add_fusion.2), channel_id=1, source_target_pairs={{0,4},{1,5},{2,6},{3,7},{4,8},{5,9},{6,10},{7,11},{8,12},{9,13},{1... | collective-permute-start | bytes 6152 | tf_op jit(solution)/shard_map/ppermute | solution.py:340
  273.3 13.6 %collective-permute-start.15 = (f32[4,128]{1,0:T(4,128)S(1)}, f32[4,128]{1,0:T(4,128)S(1)}, u32[]{:S(2)}, u32[]{:S(2)}) collective-permute-start(f32[4,128]{1,0:T(4,128)S(1)} %add_add_fusion.1), channel_id=1, source_target_pairs={{0,48},{1,49},{2,50},{3,51},{4,52},{5,53},{6,54},{7,55},{8,56},{9,... | collective-permute-start | bytes 6152 | tf_op jit(solution)/shard_map/ppermute | solution.py:340
  276.9 12.4 %collective-permute-start.14 = (f32[4,128]{1,0:T(4,128)S(1)}, f32[4,128]{1,0:T(4,128)S(1)}, u32[]{:S(2)}, u32[]{:S(2)}) collective-permute-start(f32[4,128]{1,0:T(4,128)S(1)} %add_add_fusion.1), channel_id=1, source_target_pairs={{0,32},{1,33},{2,34},{3,35},{4,36},{5,37},{6,38},{7,39},{8,40},{9,... | collective-permute-start | bytes 6152 | tf_op jit(solution)/shard_map/ppermute | solution.py:340
  277.4 11.9 %collective-permute-start.13 = (f32[4,128]{1,0:T(4,128)S(1)}, f32[4,128]{1,0:T(4,128)S(1)}, u32[]{:S(2)}, u32[]{:S(2)}) collective-permute-start(f32[4,128]{1,0:T(4,128)S(1)} %add_add_fusion.1), channel_id=1, source_target_pairs={{0,16},{1,17},{2,18},{3,19},{4,20},{5,21},{6,22},{7,23},{8,24},{9,... | collective-permute-start | bytes 6152 | tf_op jit(solution)/shard_map/ppermute | solution.py:340
  280.1 12.9 %collective-permute-start.6 = (f32[16,2,8,128]{3,2,1,0:T(8,128)S(1)}, f32[16,2,8,128]{3,2,1,0:T(8,128)S(1)}, u32[]{:S(2)}, u32[]{:S(2)}) collective-permute-start(f32[16,2,8,128]{3,2,1,0:T(8,128)S(1)} %get-tuple-element.28), channel_id=1, source_target_pairs={{0,192},{64,0},{128,64},{192,128},{1,193},{65,1},{129,65},{193,129... | collective-permute-start | bytes 393224 | tf_op jit(solution)/shard_map/ppermute | solution.py:329
  285.5 12.9 %collective-permute-start.5 = (f32[16,2,8,128]{3,2,1,0:T(8,128)S(1)}, f32[16,2,8,128]{3,2,1,0:T(8,128)S(1)}, u32[]{:S(2)}, u32[]{:S(2)}) collective-permute-start(f32[16,2,8,128]{3,2,1,0:T(8,128)S(1)} %get-tuple-element.29), channel_id=1, source_target_pairs={{0,128},{64,192},{128,0},{192,64},{1,129},{65,193},{129,1},{193,65... | collective-permute-start | bytes 393224 | tf_op jit(solution)/shard_map/ppermute | solution.py:329
  286.9 11.4 %collective-permute-start.4 = (f32[16,2,8,128]{3,2,1,0:T(8,128)S(1)}, f32[16,2,8,128]{3,2,1,0:T(8,128)S(1)}, u32[]{:S(2)}, u32[]{:S(2)}) collective-permute-start(f32[16,2,8,128]{3,2,1,0:T(8,128)S(1)} %get-tuple-element.30), channel_id=1, source_target_pairs={{0,64},{64,128},{128,192},{192,0},{1,65},{65,129},{129,193},{193,1... | collective-permute-start | bytes 393224 | tf_op jit(solution)/shard_map/ppermute | solution.py:329
  293.0 5.3 %copy-start.5 = (f32[16,2,8,128]{3,2,1,0:T(8,128)}, f32[16,2,8,128]{3,2,1,0:T(8,128)S(1)}, u32[]{:S(2)}) copy-start(f32[16,2,8,128]{3,2,1,0:T(8,128)S(1)} %collective-permute-done.6.d) | copy-start | bytes 393220
  298.3 0.6 copy-start.6
  298.4 0.7 copy-start.7

commit v2 on v1

--- a/solution.py
+++ b/solution.py
@@ -55,34 +55,50 @@
 
 
 def update_plane(e_old, e_next, h_now, h_prev, coef, e_new, m):
-    def pair(ref, comp, z):
-        return [ref[comp, z, v] for v in range(HALF)]
-
-    ex, ey = pair(e_old, 0, 0), pair(e_old, 1, 0)
-    below = None
+    def plane(ref, comp):
+        return [[ref[comp, z, v] for v in range(HALF)] for z in range(SLAB)]
+
+    ex, ey, ez = (plane(e_old, comp) for comp in range(3))
+    ey_x, ez_x = plane(e_next, 1), plane(e_next, 2)
+    hx, hy, hz = (plane(h_now, comp) for comp in range(3))
+    hy_x, hz_x = plane(h_prev, 1), plane(h_prev, 2)
+    c = [[coef[z, v] for v in range(HALF)] for z in range(SLAB)]
+    edge = [0.0] * HALF
+    new_e = []
     for z in range(SLAB):
-        ez = pair(e_old, 2, z)
-        ex_up = pair(e_old, 0, z + 1) if z + 1 < SLAB else [0.0, 0.0]
-        ey_up = pair(e_old, 1, z + 1) if z + 1 < SLAB else [0.0, 0.0]
-        ey_x, ez_x = pair(e_next, 1, z), pair(e_next, 2, z)
-        ez_y, ex_y = ahead_y(ez, m), ahead_y(ex, m)
-        hx, hy, hz = pair(h_now, 0, z), pair(h_now, 1, z), pair(h_now, 2, z)
+        ex_z, ey_z = (ex[z + 1], ey[z + 1]) if z + 1 < SLAB else (edge, edge)
+        ez_y, ex_y = ahead_y(ez[z], m), ahead_y(ex[z], m)
         for v in range(HALF):
-            hx[v] = hx[v] - ((ez_y[v] - ez[v]) - (ey_up[v] - ey[v]))
-            hy[v] = hy[v] - ((ex_up[v] - ex[v]) - (ez_x[v] - ez[v]))
-            hz[v] = hz[v] - ((ey_x[v] - ey[v]) - (ex_y[v] - ex[v]))
-            h_now[0, z, v] = hx[v]
-            h_now[1, z, v] = hy[v]
-            h_now[2, z, v] = hz[v]
-        hz_y, hx_y = behind_y(hz, m), behind_y(hx, m)
-        hy_x, hz_x = pair(h_prev, 1, z), pair(h_prev, 2, z)
-        hx_z, hy_z = below if z > 0 else ([0.0, 0.0], [0.0, 0.0])
+            hx[z][v] = hx[z][v] - ((ez_y[v] - ez[z][v]) - (ey_z[v] - ey[z][v]))
+            hy[z][v] = hy[z][v] - ((ex_z[v] - ex[z][v]) - (ez_x[z][v] - ez[z][v]))
+            hz[z][v] = hz[z][v] - ((ey_x[z][v] - ey[z][v]) - (ex_y[v] - ex[z][v]))
+        hz_y, hx_y = behind_y(hz[z], m), behind_y(hx[z], m)
+        hx_z, hy_z = (hx[z - 1], hy[z - 1]) if z > 0 else (edge, edge)
         for v in range(HALF):
-            c = coef[z, v]
-            e_new[0, z, v] = ex[v] + c * ((hz[v] - hz_y[v]) - (hy[v] - hy_z[v]))
-            e_new[1, z, v] = ey[v] + c * ((hx[v] - hx_z[v]) - (hz[v] - hz_x[v]))
-            e_new[2, z, v] = ez[v] + c * ((hy[v] - hy_x[v]) - (hx[v] - hx_y[v]))
-        ex, ey, below = ex_up, ey_up, (hx, hy)
+            curl_x = (hz[z][v] - hz_y[v]) - (hy[z][v] - hy_z[v])
+            curl_y = (hx[z][v] - hx_z[v]) - (hz[z][v] - hz_x[z][v])
+            curl_z = (hy[z][v] - hy_x[z][v]) - (hx[z][v] - hx_y[v])
+            new_e.append(
+                (
+                    ex[z][v] + c[z][v] * curl_x,
+                    ey[z][v] + c[z][v] * curl_y,
+                    ez[z][v] + c[z][v] * curl_z,
+                )
+            )
+    for z in range(SLAB):
+        for v in range(HALF):
+            for comp, h in enumerate((hx, hy, hz)):
+                h_now[comp, z, v] = h[z][v]
+                e_new[comp, z, v] = new_e[z * HALF + v][comp]
+
+
+def sweep(first, last, one):
+    def four(i, _):
+        for k in range(4):
+            one(4 * i + k)
+        return 0
+
+    lax.fori_loop(first, last, four, 0)
 
 
 def strided(z, v):
@@ -126,22 +142,18 @@
     h[:, 0] = jnp.zeros((3,) + CELLS, jnp.float32)
     hist_e[0] = e[1:3, 0]
 
-    def sweep(low, high):
-        def one(x, _):
-            update_plane(e.at[:, x], e.at[:, x + 1], h.at[:, x + 1], h.at[:, x], coef.at[x], e.at[:, x], m)
-            return 0
-
-        lax.fori_loop(low, high, one, 0)
+    def one(x):
+        update_plane(e.at[:, x], e.at[:, x + 1], h.at[:, x + 1], h.at[:, x], coef.at[x], e.at[:, x], m)
 
     def early(s, _):
-        sweep(0, WIDTH)
+        sweep(0, WIDTH // 4, one)
         hist_e[s] = e[1:3, 0]
         hist_h[s - 1] = h[1:3, WIDTH]
         return 0
 
     def late(s, _):
-        sweep(0, WIDTH - s)
-        sweep(s - 1, WIDTH)
+        sweep(0, (WIDTH - s + 3) // 4, one)
+        sweep((s - 1) // 4, WIDTH // 4, one)
 
         @pl.when(s < STEPS)
         def _():
@@ -157,7 +169,7 @@
 def full_kernel(
     info, e_in, h_in, coef, coef_l, coef_r, got_e, got_h, forward, mask, profile,
     e_out, h_out, grad, over,
-    e, h, el, hl, er, hr, wide, sums,
+    e, h, el, hl, er, hr, wide,
 ):
     m = masks()
     load_rows(e_in, e.at[0], 0, 1.0)
@@ -173,25 +185,22 @@
         el[1:3, DEPTH + 1] = before[1:3, 0]
         before[1:3, WIDTH] = er[1:3, 0] + got_e[s - 1]
 
-        def left(x, _):
-            update_plane(el.at[:, x], el.at[:, x + 1], hl.at[:, x], hl.at[:, x - 1], coef_l.at[x - 1], el.at[:, x], m)
-            return 0
-
-        lax.fori_loop(DEPTH + 1 - n_left, DEPTH + 1, left, 0)
+        def left(x):
+            update_plane(el.at[:, x + 1], el.at[:, x + 2], hl.at[:, x + 1], hl.at[:, x], coef_l.at[x], el.at[:, x + 1], m)
+
+        sweep((DEPTH - n_left) // 4, DEPTH // 4, left)
         h[1:3, 0] = hl[1:3, DEPTH] * inner + got_h[s - 1]
 
-        def own(x, _):
+        def own(x):
             update_plane(before.at[:, x], before.at[:, x + 1], h.at[:, x + 1], h.at[:, x], coef.at[x], after.at[:, x], m)
-            return 0
-
-        lax.fori_loop(0, WIDTH, own, 0)
+
+        sweep(0, WIDTH // 4, own)
         hr[1:3, 0] = h[1:3, WIDTH]
 
-        def right(x, _):
+        def right(x):
             update_plane(er.at[:, x], er.at[:, x + 1], hr.at[:, x + 1], hr.at[:, x], coef_r.at[x], er.at[:, x], m)
-            return 0
-
-        lax.fori_loop(0, n_right, right, 0)
+
+        sweep(0, (n_right + 3) // 4, right)
         return 0
 
     lax.fori_loop(1, STEPS + 1, step, 0)
@@ -201,14 +210,15 @@
     mid = (STEPS + 1) / 2
     ca = [float(np.cos(w * mid)) for w in omegas]
     sa = [float(np.sin(w * mid)) for w in omegas]
-    sums[...] = jnp.zeros(sums.shape, jnp.float32)
-
-    def finish(x, _):
+
+    def finish(x, acc):
         for f in range(FREQS):
             for q in range(2):
                 for comp in range(3):
                     wide[(f * 2 + q) * 3 + comp] = forward[f, q, comp, x].astype(jnp.float32)
-        for z in range(SLAB):
+
+        def at_z(z, acc):
+            acc = list(acc)
             for v in range(HALF):
                 total = None
                 for comp in range(3):
@@ -226,22 +236,32 @@
                             even = c * plus[i] if even is None else even + c * plus[i]
                             odd = s * minus[i] if odd is None else odd + s * minus[i]
                         if comp == 1:
-                            sums[f, 0, v] += even
-                            sums[f, 1, v] += odd
+                            acc[(f * 2) * HALF + v] += even
+                            acc[(f * 2 + 1) * HALF + v] += odd
                         re = wide[(f * 2) * 3 + comp, strided(z, v), :]
                         im = wide[(f * 2 + 1) * 3 + comp, strided(z, v), :]
                         term = even * (re * ca[f] + im * sa[f]) + odd * (im * ca[f] - re * sa[f])
                         total = term if total is None else total + term
                 grad[lax.rem(z - port + SLAB, SLAB), x, v] = mask[x, z, v] * total
+            return tuple(acc)
+
+        acc = lax.fori_loop(0, SLAB, at_z, acc)
+
+        def put(z, _):
+            for v in range(HALF):
                 for comp in range(3):
                     e_out[comp, x, strided(z, v), :] = e[STEPS, comp, x, z, v]
                     h_out[comp, x, strided(z, v), :] = h[comp, x + 1, z, v] * COEF_H
-        return 0
-
-    lax.fori_loop(0, WIDTH, finish, 0)
+            return 0
+
+        lax.fori_loop(0, SLAB, put, 0)
+        return acc
+
+    zero = jnp.zeros((8, 128), jnp.float32)
+    acc = lax.fori_loop(0, WIDTH, finish, (zero,) * (FREQS * 2 * HALF))
     for f in range(FREQS):
-        even = sum(sums[f, 0, v] * profile[info[2], v] for v in range(HALF))
-        odd = sum(sums[f, 1, v] * profile[info[2], v] for v in range(HALF))
+        even = sum(acc[(f * 2) * HALF + v] * profile[info[2], v] for v in range(HALF))
+        odd = sum(acc[(f * 2 + 1) * HALF + v] * profile[info[2], v] for v in range(HALF))
         re = ca[f] * even - sa[f] * odd
         im = -(sa[f] * even + ca[f] * odd)
         for q, val in enumerate((re, im)):
@@ -318,7 +338,6 @@
             pltpu.VMEM((3, DEPTH + 1) + CELLS, jnp.float32),
             pltpu.VMEM((3, DEPTH + 1) + CELLS, jnp.float32),
             pltpu.VMEM((4 * 3, 64, 128), jnp.float32),
-            pltpu.VMEM((FREQS, 2, HALF, 8, 128), jnp.float32),
         ],
         compiler_params=PARAMS,
         name="full",

time: 302 us -> 169 us (0.56)
  Pallas kernels: 231 us -> 98 us
    pallas_call x1, Pallas kernels: 189 us -> 72.9 us  [body(): pl.pallas_call(full_kernel, out_shape=(f32(3, WIDTH, 64, 128), f32(3, WID...]
    pallas_call x1, Pallas kernels: 37.4 us -> 20.8 us  [body(): pl.pallas_call(free_kernel, out_shape=(f32(STEPS, 2, *CELLS), f32(STEPS,...]
  transfers between devices with their start and end apart: 16 -> 16, of which waited for: 8 -> 8; matrix products, arithmetic and copies ran while one was open for 1% -> 2% of each run, Pallas kernels for 0% -> 0%
where the time goes in v2:
time: 169 us; the launch traced here: 168 us
  Pallas kernels  98 us (58%)
  starting transfers between devices  33.5 us (20%)
  waiting for transfers between devices  24.6 us (15%)
  local copies, waits for them, and re-layouts  8.84 us (5%)
    pallas_call x1, Pallas kernels, body(): pl.pallas_call(full_kernel, out_shape=(f32(3, WIDTH, 64, 128), f32(3, WID...  72.9 us
    pallas_call x1, Pallas kernels, body(): pl.pallas_call(free_kernel, out_shape=(f32(STEPS, 2, *CELLS), f32(STEPS,...  20.8 us
    ppermute x9, starting transfers between devices, body(): got.append(lax.ppermute(total, 'tile', pairs))  14.3 us
    ppermute x3, starting transfers between devices, body(): lax.ppermute(grad[d], 'port', [(i, (i + d) % ports) for i in range(ports)])  9.22 us
    ppermute x3, waiting for transfers between devices, body(): lax.ppermute(grad[d], 'port', [(i, (i + d) % ports) for i in range(ports)])  8.25 us
    ppermute x9, waiting for transfers between devices, body(): got.append(lax.ppermute(total, 'tile', pairs))  6.66 us
    ppermute x1, waiting for transfers between devices, body(): coef_r = lax.ppermute(coef[:DEPTH], 'tile', to_left)  5.26 us
    ppermute x1, waiting for transfers between devices, body(): coef_l = lax.ppermute(coef[WIDTH - DEPTH:], 'tile', to_right)  4.37 us
  transfers between devices with their start and end apart: 16, of which 8 were waited for; matrix products, arithmetic and copies ran while one was open for 2% of the time, Pallas kernels for 0%

profile of v2, /device:TPU:8, one launch (start us, length us, event | category | flops | bytes accessed | tf_op | source)
XLA Modules:
  0.0 167.7 jit_solution(12454629034495389681)
XLA Ops:
  0.6 0.9 copy.24
  1.6 0.1 reshape.62
  1.7 0.1 copy.25
  1.8 0.7 copy.29.mat
  2.5 0.9 copy.26
  3.4 0.1 reshape.64
  3.5 0.1 copy.27
  3.6 0.7 copy.30.des
  4.3 2.5 %coef.1 = (f32[16,4,2,8,128]{4,3,2,1,0:T(8,128)}, f32[16,4,2,8,128]{4,3,2,1,0:T(8,128)}) custom-call(f32[4]{0:T(128)} %table.1, s32[8,128]{1,0:T(8,128)} %copy.29.mat, s32[8,128]{1,0:T(8,128)} %copy.30.des, f32[16,64,128]{2,1,0:T(8,128)} %bitcast.57), custom_call_target="tpu_custom_call" | custom-call | tf_op jit(solution)/shard_map/coef/pallas_call | solution.py:298
  6.8 20.8 %free.1 = (f32[16,2,4,2,8,128]{5,4,3,2,1,0:T(8,128)}, f32[16,2,4,2,8,128]{5,4,3,2,1,0:T(8,128)}) custom-call(f32[3,16,64,128]{3,2,1,0:T(8,128)} %bitcast.52, f32[3,16,64,128]{3,2,1,0:T(8,128)} %bitcast.54, f32[16,4,2,8,128]{4,3,2,1,0:T(8,128)} %get-tuple-element.12.coef), custom_call_target="tpu_custom_call" | custom-call | tf_op jit(solution)/shard_map/free/pallas_call | solution.py:309
  27.6 1.9 %collective-permute-start.2 = (f32[16,2,4,2,8,128]{5,4,3,2,1,0:T(8,128)}, f32[16,2,4,2,8,128]{5,4,3,2,1,0:T(8,128)S(1)}, u32[]{:S(2)}, u32[]{:S(2)}) collective-permute-start(f32[16,2,4,2,8,128]{5,4,3,2,1,0:T(8,128)} %get-tuple-element.13), channel_id=1, source_target_pairs={{1,0},{2,1},{3,2},{4,3},{5,4},{6,5},{7,6},{8,7},{9,8},{10,9},{11,1... | collective-permute-start | bytes 3145736 | tf_op jit(solution)/shard_map/ppermute | solution.py:318
  29.5 2.4 %collective-permute-start.3 = (f32[16,2,4,2,8,128]{5,4,3,2,1,0:T(8,128)}, f32[16,2,4,2,8,128]{5,4,3,2,1,0:T(8,128)S(1)}, u32[]{:S(2)}, u32[]{:S(2)}) collective-permute-start(f32[16,2,4,2,8,128]{5,4,3,2,1,0:T(8,128)} %get-tuple-element.14), channel_id=1, source_target_pairs={{0,1},{1,2},{2,3},{3,4},{4,5},{5,6},{6,7},{7,8},{8,9},{9,10},{10,1... | collective-permute-start | bytes 3145736 | tf_op jit(solution)/shard_map/ppermute | solution.py:319
  32.0 3.7 %collective-permute-start.1 = (f32[8,4,2,8,128]{4,3,2,1,0:T(8,128)S(1)}, f32[8,4,2,8,128]{4,3,2,1,0:T(8,128)S(1)}, u32[]{:S(2)}, u32[]{:S(2)}) collective-permute-start(f32[8,4,2,8,128]{4,3,2,1,0:T(8,128)S(1)} %get-tuple-element.32), channel_id=1, source_target_pairs={{1,0},{2,1},{3,2},{4,3},{5,4},{6,5},{7,6},{8,7},{9,8},{10,9},{11,1... | collective-permute-start | bytes 786440 | tf_op jit(solution)/shard_map/ppermute | solution.py:306
  35.7 1.9 %collective-permute-start = (f32[8,4,2,8,128]{4,3,2,1,0:T(8,128)S(1)}, f32[8,4,2,8,128]{4,3,2,1,0:T(8,128)S(1)}, u32[]{:S(2)}, u32[]{:S(2)}) collective-permute-start(f32[8,4,2,8,128]{4,3,2,1,0:T(8,128)S(1)} %get-tuple-element.33), channel_id=1, source_target_pairs={{0,1},{1,2},{2,3},{3,4},{4,5},{5,6},{6,7},{7,8},{8,9},{9,10},{10,1... | collective-permute-start | bytes 786440 | tf_op jit(solution)/shard_map/ppermute | solution.py:305
  38.3 0.6 copy.37
  38.9 0.6 pad_add_fusion.info
  39.6 5.3 %collective-permute-done.1.coef_r = f32[8,4,2,8,128]{4,3,2,1,0:T(8,128)S(1)} collective-permute-done((f32[8,4,2,8,128]{4,3,2,1,0:T(8,128)S(1)}, f32[8,4,2,8,128]{4,3,2,1,0:T(8,128)S(1)}, u32[]{:S(2)}, u32[]{:S(2)}) %collective-permute-start.1) | collective-permute-done | bytes 262176 | tf_op jit(solution)/shard_map/ppermute | solution.py:306
  44.8 4.4 %collective-permute-done.coef_l = f32[8,4,2,8,128]{4,3,2,1,0:T(8,128)S(1)} collective-permute-done((f32[8,4,2,8,128]{4,3,2,1,0:T(8,128)S(1)}, f32[8,4,2,8,128]{4,3,2,1,0:T(8,128)S(1)}, u32[]{:S(2)}, u32[]{:S(2)}) %collective-permute-start) | collective-permute-done | bytes 262176 | tf_op jit(solution)/shard_map/ppermute | solution.py:305
  49.2 0.0 collective-permute-done.2.got_e
  49.2 0.0 collective-permute-done.3.got_h
  49.2 0.7 copy-done.4
  49.9 0.4 copy-done.1
  50.3 0.3 copy-done.2
  50.6 72.9 %full.1 = (f32[3,16,64,128]{3,2,1,0:T(8,128)}, f32[3,16,64,128]{3,2,1,0:T(8,128)}, f32[4,16,2,8,128]{4,3,2,1,0:T(8,128)}, f32[4,128]{1,0:T(4,128)}) custom-call(s32[3]{0:T(128)} %pad_add_fusion.info, f32[3,16,64,128]{3,2,1,0:T(8,128)} %bitcast.53, f32[3,16,64,128]{3,2,1,0:T(8,128)} %bitcast.55, f32[16,4,2,8,128]{4,3,2,1,0:T(8,128)} %get-tuple-element.12.coef, ...), custom_call_target="tpu_custom_call" | custom-call | tf_op jit(solution)/shard_map/full/pallas_call | solution.py:323
  123.5 0.3 collective-permute-start.8
  123.8 0.2 collective-permute-start.7
  124.1 1.0 collective-permute-done.9
  125.1 2.4 %collective-permute-done.8 = f32[4,128]{1,0:T(4,128)S(1)} collective-permute-done((f32[4,128]{1,0:T(4,128)}, f32[4,128]{1,0:T(4,128)S(1)}, u32[]{:S(2)}, u32[]{:S(2)}) %collective-permute-start.8) | collective-permute-done | bytes 2080 | tf_op jit(solution)/shard_map/ppermute | solution.py:359
  127.4 0.0 collective-permute-done.7
  127.4 0.7 add_add_fusion.2
  128.1 6.2 %collective-permute-start.12 = (f32[4,128]{1,0:T(4,128)S(1)}, f32[4,128]{1,0:T(4,128)S(1)}, u32[]{:S(2)}, u32[]{:S(2)}) collective-permute-start(f32[4,128]{1,0:T(4,128)S(1)} %add_add_fusion.2), channel_id=1, source_target_pairs={{0,12},{1,13},{2,14},{3,15},{4,0},{5,1},{6,2},{7,3},{8,4},{9,5},{1... | collective-permute-start | bytes 6152 | tf_op jit(solution)/shard_map/ppermute | solution.py:359
  134.3 2.7 %collective-permute-start.10 = (f32[4,128]{1,0:T(4,128)S(1)}, f32[4,128]{1,0:T(4,128)S(1)}, u32[]{:S(2)}, u32[]{:S(2)}) collective-permute-start(f32[4,128]{1,0:T(4,128)S(1)} %add_add_fusion.2), channel_id=1, source_target_pairs={{0,4},{1,5},{2,6},{3,7},{4,8},{5,9},{6,10},{7,11},{8,12},{9,13},{1... | collective-permute-start | bytes 6152 | tf_op jit(solution)/shard_map/ppermute | solution.py:359
  137.0 0.9 collective-permute-done.11
  137.8 2.4 %collective-permute-done.10 = f32[4,128]{1,0:T(4,128)S(1)} collective-permute-done((f32[4,128]{1,0:T(4,128)S(1)}, f32[4,128]{1,0:T(4,128)S(1)}, u32[]{:S(2)}, u32[]{:S(2)}) %collective-permute-start.10) | collective-permute-done | bytes 2080 | tf_op jit(solution)/shard_map/ppermute | solution.py:359
  140.3 3.6 %collective-permute-start.15 = (f32[4,128]{1,0:T(4,128)S(1)}, f32[4,128]{1,0:T(4,128)S(1)}, u32[]{:S(2)}, u32[]{:S(2)}) collective-permute-start(f32[4,128]{1,0:T(4,128)S(1)} %add_add_fusion.1), channel_id=1, source_target_pairs={{0,48},{1,49},{2,50},{3,51},{4,52},{5,53},{6,54},{7,55},{8,56},{9,... | collective-permute-start | bytes 6152 | tf_op jit(solution)/shard_map/ppermute | solution.py:359
  143.8 0.5 collective-permute-start.14
  144.3 0.9 collective-permute-start.13
  145.2 1.8 %slice_bitcast_fusion = (f32[16,2,8,128]{3,2,1,0:T(8,128)S(1)}, f32[16,2,8,128]{3,2,1,0:T(8,128)S(1)}, f32[16,2,8,128]{3,2,1,0:T(8,128)S(1)}, f32[16,2,8,128]{3,2,1,0:T(8,128)}) fusion(f32[4,16,2,8,128]{4,3,2,1,0:T(8,128)} %get-tuple-element.18), kind=kLoop, calls=%fused_computation | loop fusion | bytes 1048576 | tf_op jit(solution)/shard_map/squeeze | solution.py:348
  147.0 5.4 %collective-permute-start.6 = (f32[16,2,8,128]{3,2,1,0:T(8,128)S(1)}, f32[16,2,8,128]{3,2,1,0:T(8,128)S(1)}, u32[]{:S(2)}, u32[]{:S(2)}) collective-permute-start(f32[16,2,8,128]{3,2,1,0:T(8,128)S(1)} %get-tuple-element.28), channel_id=1, source_target_pairs={{0,192},{64,0},{128,64},{192,128},{1,193},{65,1},{129,65},{193,129... | collective-permute-start | bytes 393224 | tf_op jit(solution)/shard_map/ppermute | solution.py:348
  152.4 1.4 collective-permute-start.5
  153.8 2.4 %collective-permute-start.4 = (f32[16,2,8,128]{3,2,1,0:T(8,128)S(1)}, f32[16,2,8,128]{3,2,1,0:T(8,128)S(1)}, u32[]{:S(2)}, u32[]{:S(2)}) collective-permute-start(f32[16,2,8,128]{3,2,1,0:T(8,128)S(1)} %get-tuple-element.30), channel_id=1, source_target_pairs={{0,64},{64,128},{128,192},{192,0},{1,65},{65,129},{129,193},{193,1... | collective-permute-start | bytes 393224 | tf_op jit(solution)/shard_map/ppermute | solution.py:348
  156.2 0.1 multiply_reduce_fusion
  156.4 0.6 div.6
  157.0 2.9 %collective-permute-done.6.d = f32[16,2,8,128]{3,2,1,0:T(8,128)S(1)} collective-permute-done((f32[16,2,8,128]{3,2,1,0:T(8,128)S(1)}, f32[16,2,8,128]{3,2,1,0:T(8,128)S(1)}, u32[]{:S(2)}, u32[]{:S(2)}) %collective-permute-start.6) | collective-permute-done | bytes 131104 | tf_op jit(solution)/shard_map/ppermute | solution.py:348
  159.9 5.3 %collective-permute-done.5.c = f32[16,2,8,128]{3,2,1,0:T(8,128)S(1)} collective-permute-done((f32[16,2,8,128]{3,2,1,0:T(8,128)S(1)}, f32[16,2,8,128]{3,2,1,0:T(8,128)S(1)}, u32[]{:S(2)}, u32[]{:S(2)}) %collective-permute-start.5) | collective-permute-done | bytes 131104 | tf_op jit(solution)/shard_map/ppermute | solution.py:348
  165.3 0.6 copy-done.6
  165.9 0.0 copy-done.7
  165.9 1.8 %total.1 = f32[16,16,128]{2,1,0:T(8,128)} custom-call(f32[16,2,8,128]{3,2,1,0:T(8,128)} %get-tuple-element.31.a, f32[16,2,8,128]{3,2,1,0:T(8,128)} %copy-done.7, f32[16,2,8,128]{3,2,1,0:T(8,128)} %copy-done.6, f32[16,2,8,128]{3,2,1,0:T(8,128)} %copy-done.5), custom_call_target="tpu_custom_call" | custom-call | tf_op jit(solution)/shard_map/total/pallas_call | solution.py:362
  (24 shorter events, 0.1 us)
Async XLA Ops:
  6.8 25.1 %copy-start = (f32[16,4,2,8,128]{4,3,2,1,0:T(8,128)S(1)}, f32[16,4,2,8,128]{4,3,2,1,0:T(8,128)}, u32[]{:S(2)}) copy-start(f32[16,4,2,8,128]{4,3,2,1,0:T(8,128)} %get-tuple-element.12.coef) | copy-start | bytes 1572868
  6.8 31.5 %copy-start.8 = (f32[4,2048]{1,0:T(4,128)S(1)}, f32[4,2048]{1,0:T(4,128)}, u32[]{:S(2)}) copy-start(f32[4,2048]{1,0:T(4,128)} %param.16) | copy-start | bytes 98308
  27.6 21.6 %collective-permute-start.2 = (f32[16,2,4,2,8,128]{5,4,3,2,1,0:T(8,128)}, f32[16,2,4,2,8,128]{5,4,3,2,1,0:T(8,128)S(1)}, u32[]{:S(2)}, u32[]{:S(2)}) collective-permute-start(f32[16,2,4,2,8,128]{5,4,3,2,1,0:T(8,128)} %get-tuple-element.13), channel_id=1, source_target_pairs={{1,0},{2,1},{3,2},{4,3},{5,4},{6,5},{7,6},{8,7},{9,8},{10,9},{11,1... | collective-permute-start | bytes 3145736 | tf_op jit(solution)/shard_map/ppermute | solution.py:318
  29.5 19.7 %collective-permute-start.3 = (f32[16,2,4,2,8,128]{5,4,3,2,1,0:T(8,128)}, f32[16,2,4,2,8,128]{5,4,3,2,1,0:T(8,128)S(1)}, u32[]{:S(2)}, u32[]{:S(2)}) collective-permute-start(f32[16,2,4,2,8,128]{5,4,3,2,1,0:T(8,128)} %get-tuple-element.14), channel_id=1, source_target_pairs={{0,1},{1,2},{2,3},{3,4},{4,5},{5,6},{6,7},{7,8},{8,9},{9,10},{10,1... | collective-permute-start | bytes 3145736 | tf_op jit(solution)/shard_map/ppermute | solution.py:319
  32.0 12.8 %collective-permute-start.1 = (f32[8,4,2,8,128]{4,3,2,1,0:T(8,128)S(1)}, f32[8,4,2,8,128]{4,3,2,1,0:T(8,128)S(1)}, u32[]{:S(2)}, u32[]{:S(2)}) collective-permute-start(f32[8,4,2,8,128]{4,3,2,1,0:T(8,128)S(1)} %get-tuple-element.32), channel_id=1, source_target_pairs={{1,0},{2,1},{3,2},{4,3},{5,4},{6,5},{7,6},{8,7},{9,8},{10,9},{11,1... | collective-permute-start | bytes 786440 | tf_op jit(solution)/shard_map/ppermute | solution.py:306
  35.7 13.5 %collective-permute-start = (f32[8,4,2,8,128]{4,3,2,1,0:T(8,128)S(1)}, f32[8,4,2,8,128]{4,3,2,1,0:T(8,128)S(1)}, u32[]{:S(2)}, u32[]{:S(2)}) collective-permute-start(f32[8,4,2,8,128]{4,3,2,1,0:T(8,128)S(1)} %get-tuple-element.33), channel_id=1, source_target_pairs={{0,1},{1,2},{2,3},{3,4},{4,5},{5,6},{6,7},{7,8},{8,9},{9,10},{10,1... | collective-permute-start | bytes 786440 | tf_op jit(solution)/shard_map/ppermute | solution.py:305
  44.8 4.4 %copy-start.3 = (f32[8,4,2,8,128]{4,3,2,1,0:T(8,128)}, f32[8,4,2,8,128]{4,3,2,1,0:T(8,128)S(1)}, u32[]{:S(2)}) copy-start(f32[8,4,2,8,128]{4,3,2,1,0:T(8,128)S(1)} %collective-permute-done.1.coef_r) | copy-start | bytes 786436
  49.2 0.7 copy-start.4
  49.2 1.1 copy-start.1
  49.2 1.4 copy-start.2
  123.5 1.5 collective-permute-start.9
  123.5 3.9 %collective-permute-start.8 = (f32[4,128]{1,0:T(4,128)}, f32[4,128]{1,0:T(4,128)S(1)}, u32[]{:S(2)}, u32[]{:S(2)}) collective-permute-start(f32[4,128]{1,0:T(4,128)} %get-tuple-element.19), channel_id=1, source_target_pairs={{0,2},{1,3},{2,0},{3,1},{4,6},{5,7},{6,4},{7,5},{8,10},{9,11},{10,... | collective-permute-start | bytes 6152 | tf_op jit(solution)/shard_map/ppermute | solution.py:359
  123.8 3.6 %collective-permute-start.7 = (f32[4,128]{1,0:T(4,128)}, f32[4,128]{1,0:T(4,128)S(1)}, u32[]{:S(2)}, u32[]{:S(2)}) collective-permute-start(f32[4,128]{1,0:T(4,128)} %get-tuple-element.19), channel_id=1, source_target_pairs={{0,1},{1,2},{2,3},{3,0},{4,5},{5,6},{6,7},{7,4},{8,9},{9,10},{10,1... | collective-permute-start | bytes 6152 | tf_op jit(solution)/shard_map/ppermute | solution.py:359
  128.1 8.9 %collective-permute-start.12 = (f32[4,128]{1,0:T(4,128)S(1)}, f32[4,128]{1,0:T(4,128)S(1)}, u32[]{:S(2)}, u32[]{:S(2)}) collective-permute-start(f32[4,128]{1,0:T(4,128)S(1)} %add_add_fusion.2), channel_id=1, source_target_pairs={{0,12},{1,13},{2,14},{3,15},{4,0},{5,1},{6,2},{7,3},{8,4},{9,5},{1... | collective-permute-start | bytes 6152 | tf_op jit(solution)/shard_map/ppermute | solution.py:359
  134.3 3.6 %collective-permute-start.11 = (f32[4,128]{1,0:T(4,128)S(1)}, f32[4,128]{1,0:T(4,128)S(1)}, u32[]{:S(2)}, u32[]{:S(2)}) collective-permute-start(f32[4,128]{1,0:T(4,128)S(1)} %add_add_fusion.2), channel_id=1, source_target_pairs={{0,8},{1,9},{2,10},{3,11},{4,12},{5,13},{6,14},{7,15},{8,0},{9,1},... | collective-permute-start | bytes 6152 | tf_op jit(solution)/shard_map/ppermute | solution.py:359
  134.3 6.0 %collective-permute-start.10 = (f32[4,128]{1,0:T(4,128)S(1)}, f32[4,128]{1,0:T(4,128)S(1)}, u32[]{:S(2)}, u32[]{:S(2)}) collective-permute-start(f32[4,128]{1,0:T(4,128)S(1)} %add_add_fusion.2), channel_id=1, source_target_pairs={{0,4},{1,5},{2,6},{3,7},{4,8},{5,9},{6,10},{7,11},{8,12},{9,13},{1... | collective-permute-start | bytes 6152 | tf_op jit(solution)/shard_map/ppermute | solution.py:359
  140.3 13.6 %collective-permute-start.15 = (f32[4,128]{1,0:T(4,128)S(1)}, f32[4,128]{1,0:T(4,128)S(1)}, u32[]{:S(2)}, u32[]{:S(2)}) collective-permute-start(f32[4,128]{1,0:T(4,128)S(1)} %add_add_fusion.1), channel_id=1, source_target_pairs={{0,48},{1,49},{2,50},{3,51},{4,52},{5,53},{6,54},{7,55},{8,56},{9,... | collective-permute-start | bytes 6152 | tf_op jit(solution)/shard_map/ppermute | solution.py:359
  143.8 12.4 %collective-permute-start.14 = (f32[4,128]{1,0:T(4,128)S(1)}, f32[4,128]{1,0:T(4,128)S(1)}, u32[]{:S(2)}, u32[]{:S(2)}) collective-permute-start(f32[4,128]{1,0:T(4,128)S(1)} %add_add_fusion.1), channel_id=1, source_target_pairs={{0,32},{1,33},{2,34},{3,35},{4,36},{5,37},{6,38},{7,39},{8,40},{9,... | collective-permute-start | bytes 6152 | tf_op jit(solution)/shard_map/ppermute | solution.py:359
  144.3 11.9 %collective-permute-start.13 = (f32[4,128]{1,0:T(4,128)S(1)}, f32[4,128]{1,0:T(4,128)S(1)}, u32[]{:S(2)}, u32[]{:S(2)}) collective-permute-start(f32[4,128]{1,0:T(4,128)S(1)} %add_add_fusion.1), channel_id=1, source_target_pairs={{0,16},{1,17},{2,18},{3,19},{4,20},{5,21},{6,22},{7,23},{8,24},{9,... | collective-permute-start | bytes 6152 | tf_op jit(solution)/shard_map/ppermute | solution.py:359
  147.0 12.9 %collective-permute-start.6 = (f32[16,2,8,128]{3,2,1,0:T(8,128)S(1)}, f32[16,2,8,128]{3,2,1,0:T(8,128)S(1)}, u32[]{:S(2)}, u32[]{:S(2)}) collective-permute-start(f32[16,2,8,128]{3,2,1,0:T(8,128)S(1)} %get-tuple-element.28), channel_id=1, source_target_pairs={{0,192},{64,0},{128,64},{192,128},{1,193},{65,1},{129,65},{193,129... | collective-permute-start | bytes 393224 | tf_op jit(solution)/shard_map/ppermute | solution.py:348
  152.4 12.9 %collective-permute-start.5 = (f32[16,2,8,128]{3,2,1,0:T(8,128)S(1)}, f32[16,2,8,128]{3,2,1,0:T(8,128)S(1)}, u32[]{:S(2)}, u32[]{:S(2)}) collective-permute-start(f32[16,2,8,128]{3,2,1,0:T(8,128)S(1)} %get-tuple-element.29), channel_id=1, source_target_pairs={{0,128},{64,192},{128,0},{192,64},{1,129},{65,193},{129,1},{193,65... | collective-permute-start | bytes 393224 | tf_op jit(solution)/shard_map/ppermute | solution.py:348
  153.8 11.4 %collective-permute-start.4 = (f32[16,2,8,128]{3,2,1,0:T(8,128)S(1)}, f32[16,2,8,128]{3,2,1,0:T(8,128)S(1)}, u32[]{:S(2)}, u32[]{:S(2)}) collective-permute-start(f32[16,2,8,128]{3,2,1,0:T(8,128)S(1)} %get-tuple-element.30), channel_id=1, source_target_pairs={{0,64},{64,128},{128,192},{192,0},{1,65},{65,129},{129,193},{193,1... | collective-permute-start | bytes 393224 | tf_op jit(solution)/shard_map/ppermute | solution.py:348
  159.9 5.3 %copy-start.5 = (f32[16,2,8,128]{3,2,1,0:T(8,128)}, f32[16,2,8,128]{3,2,1,0:T(8,128)S(1)}, u32[]{:S(2)}) copy-start(f32[16,2,8,128]{3,2,1,0:T(8,128)S(1)} %collective-permute-done.6.d) | copy-start | bytes 393220
  165.3 0.6 copy-start.6
  165.3 0.7 copy-start.7

commit v3 on v2

--- a/solution.py
+++ b/solution.py
@@ -54,7 +54,7 @@
     return jnp.where(m[1], rs, r0), jnp.where(m[1], r0, r1)
 
 
-def update_plane(e_old, e_next, h_now, h_prev, coef, e_new, m):
+def update_plane(e_old, e_next, h_now, h_prev, coef, e_new, m, keep=None):
     def plane(ref, comp):
         return [[ref[comp, z, v] for v in range(HALF)] for z in range(SLAB)]
 
@@ -90,15 +90,17 @@
             for comp, h in enumerate((hx, hy, hz)):
                 h_now[comp, z, v] = h[z][v]
                 e_new[comp, z, v] = new_e[z * HALF + v][comp]
-
-
-def sweep(first, last, one):
-    def four(i, _):
-        for k in range(4):
-            one(4 * i + k)
+                if keep is not None:
+                    keep[comp, z, v] = new_e[z * HALF + v][comp]
+
+
+def sweep(blocks, planes, one):
+    def block(i, _):
+        for plane in planes(i):
+            one(plane)
         return 0
 
-    lax.fori_loop(first, last, four, 0)
+    lax.fori_loop(0, blocks, block, 0)
 
 
 def strided(z, v):
@@ -117,49 +119,59 @@
     lax.fori_loop(0, WIDTH, one, 0)
 
 
-def coef_kernel(table, mat, des, dens, coef, mask):
-    kind = mat[...]
-    base = jnp.zeros((8, 128), jnp.float32)
-    for which in range(table.shape[0]):
-        base = base + jnp.where(kind == which, table[which], 0.0)
-    flag = des[...].astype(jnp.float32)
-    for x in range(WIDTH):
-        for z in range(SLAB):
-            for v in range(HALF):
-                at = (x * SLAB + z) * HALF + v
+def free_kernel(table, mat, des, dens, e_in, h_in, coef, mask, to_left, to_right, e, h):
+    m = masks()
+    row = lax.broadcasted_iota(jnp.int32, (8, 16), 0)
+    col = lax.broadcasted_iota(jnp.int32, (8, 16), 1)
+    dims = (((1,), (1,)), ((), ()))
+
+    def by_sublane(ref, v):
+        pick = (col == HALF * row + v).astype(jnp.float32)
+        values = ref[...].astype(jnp.float32)
+        return lax.dot_general(pick, values, dims, preferred_element_type=jnp.float32)
+
+    for v in range(HALF):
+        kind = by_sublane(mat, v)
+        flag = by_sublane(des, v)
+        base = jnp.zeros(kind.shape, jnp.float32)
+        for which in range(table.shape[0]):
+            base = base + jnp.where(kind == which, table[which], 0.0)
+        for x in range(WIDTH):
+            for z in range(SLAB):
+                at = x * SLAB + z
                 b = jnp.broadcast_to(base[:, at : at + 1], (8, 128))
                 d = jnp.broadcast_to(flag[:, at : at + 1], (8, 128))
                 eps = b + d * dens[x, strided(z, v), :]
                 coef[x, z, v] = (COEF_E * COEF_H) / eps
                 mask[x, z, v] = d * (1.0 / STEPS)
-
-
-def free_kernel(e_in, h_in, coef, hist_e, hist_h, e, h):
-    m = masks()
+    to_left[2 * STEPS :] = coef[:DEPTH]
+    to_right[2 * STEPS :] = coef[WIDTH - DEPTH :]
+
     load_rows(e_in, e, 0, 1.0)
     load_rows(h_in, h, 1, 1.0 / COEF_H)
     e[:, WIDTH] = jnp.zeros((3,) + CELLS, jnp.float32)
     h[:, 0] = jnp.zeros((3,) + CELLS, jnp.float32)
-    hist_e[0] = e[1:3, 0]
+    to_left[0:2] = e[1:3, 0]
 
     def one(x):
         update_plane(e.at[:, x], e.at[:, x + 1], h.at[:, x + 1], h.at[:, x], coef.at[x], e.at[:, x], m)
 
     def early(s, _):
-        sweep(0, WIDTH // 4, one)
-        hist_e[s] = e[1:3, 0]
-        hist_h[s - 1] = h[1:3, WIDTH]
+        sweep(WIDTH // 4, lambda i: [4 * i + k for k in range(4)], one)
+        to_left[pl.ds(2 * s, 2)] = e[1:3, 0]
+        to_right[pl.ds(2 * s - 2, 2)] = h[1:3, WIDTH]
         return 0
 
     def late(s, _):
-        sweep(0, (WIDTH - s + 3) // 4, one)
-        sweep((s - 1) // 4, WIDTH // 4, one)
+        blocks = (STEPS + 2 - s) // 2
+        high = WIDTH - 2 * blocks
+        sweep(blocks, lambda i: [2 * i, high + 2 * i, 2 * i + 1, high + 2 * i + 1], one)
 
         @pl.when(s < STEPS)
         def _():
-            hist_e[s] = e[1:3, 0]
-
-        hist_h[s - 1] = h[1:3, WIDTH]
+            to_left[pl.ds(2 * s, 2)] = e[1:3, 0]
+
+        to_right[pl.ds(2 * s - 2, 2)] = h[1:3, WIDTH]
         return 0
 
     lax.fori_loop(1, DEPTH + 1, early, 0)
@@ -167,42 +179,55 @@
 
 
 def full_kernel(
-    info, e_in, h_in, coef, coef_l, coef_r, got_e, got_h, forward, mask, profile,
-    e_out, h_out, grad, over,
-    e, h, el, hl, er, hr, wide,
+    scale, info, e_in, h_in, coef, from_left, from_right, forward, mask, profile,
+    e_out, h_out, g0, g1, g2, g3, over,
+    e, now, h, el, hl, er, hr, wide, grad,
 ):
     m = masks()
-    load_rows(e_in, e.at[0], 0, 1.0)
+    load_rows(e_in, now, 0, 1.0)
     load_rows(h_in, h, 1, 1.0 / COEF_H)
     for ref in (el, hl, er, hr):
         ref[...] = jnp.zeros(ref.shape, jnp.float32)
     inner = (info[0] > 0).astype(jnp.float32)
 
+    def left(x):
+        update_plane(
+            el.at[:, x + 1], el.at[:, x + 2], hl.at[:, x + 1], hl.at[:, x],
+            from_left.at[2 * STEPS + x], el.at[:, x + 1], m,
+        )
+
+    def right(x):
+        update_plane(
+            er.at[:, x], er.at[:, x + 1], hr.at[:, x + 1], hr.at[:, x],
+            from_right.at[2 * STEPS + x], er.at[:, x], m,
+        )
+
+    def halos(s):
+        el[1:3, DEPTH + 1] = now[1:3, 0]
+        blocks = (jnp.minimum(s + 1, STEPS - s) + 1) // 2
+        low = DEPTH - 2 * blocks
+        sweep(
+            blocks,
+            lambda i: [(left, low + 2 * i), (right, 2 * i), (left, low + 2 * i + 1), (right, 2 * i + 1)],
+            lambda job: job[0](job[1]),
+        )
+
     def step(s, _):
-        before, after = e.at[s - 1], e.at[s]
-        n_left = jnp.minimum(s, STEPS + 1 - s)
-        n_right = jnp.minimum(s, STEPS - s)
-        el[1:3, DEPTH + 1] = before[1:3, 0]
-        before[1:3, WIDTH] = er[1:3, 0] + got_e[s - 1]
-
-        def left(x):
-            update_plane(el.at[:, x + 1], el.at[:, x + 2], hl.at[:, x + 1], hl.at[:, x], coef_l.at[x], el.at[:, x + 1], m)
-
-        sweep((DEPTH - n_left) // 4, DEPTH // 4, left)
-        h[1:3, 0] = hl[1:3, DEPTH] * inner + got_h[s - 1]
+        now[1:3, WIDTH] = er[1:3, 0] + from_right[pl.ds(2 * s - 2, 2)]
+        h[1:3, 0] = hl[1:3, DEPTH] * inner + from_left[pl.ds(2 * s - 2, 2)]
 
         def own(x):
-            update_plane(before.at[:, x], before.at[:, x + 1], h.at[:, x + 1], h.at[:, x], coef.at[x], after.at[:, x], m)
-
-        sweep(0, WIDTH // 4, own)
+            update_plane(
+                now.at[:, x], now.at[:, x + 1], h.at[:, x + 1], h.at[:, x], coef.at[x], now.at[:, x], m,
+                e.at[s - 1, :, x],
+            )
+
+        sweep(WIDTH // 4, lambda i: [4 * i + k for k in range(4)], own)
         hr[1:3, 0] = h[1:3, WIDTH]
-
-        def right(x):
-            update_plane(er.at[:, x], er.at[:, x + 1], hr.at[:, x + 1], hr.at[:, x], coef_r.at[x], er.at[:, x], m)
-
-        sweep(0, (n_right + 3) // 4, right)
+        halos(s)
         return 0
 
+    halos(0)
     lax.fori_loop(1, STEPS + 1, step, 0)
 
     port = info[1]
@@ -224,8 +249,8 @@
                 for comp in range(3):
                     plus, minus = [], []
                     for i in range(STEPS // 2):
-                        lo = e[STEPS // 2 - i, comp, x, z, v]
-                        hi = e[STEPS // 2 + 1 + i, comp, x, z, v]
+                        lo = e[STEPS // 2 - 1 - i, comp, x, z, v]
+                        hi = e[STEPS // 2 + i, comp, x, z, v]
                         plus.append(hi + lo)
                         minus.append(hi - lo)
                     for f in range(FREQS):
@@ -250,7 +275,7 @@
         def put(z, _):
             for v in range(HALF):
                 for comp in range(3):
-                    e_out[comp, x, strided(z, v), :] = e[STEPS, comp, x, z, v]
+                    e_out[comp, x, strided(z, v), :] = now[comp, x, z, v]
                     h_out[comp, x, strided(z, v), :] = h[comp, x + 1, z, v] * COEF_H
             return 0
 
@@ -266,7 +291,9 @@
         im = -(sa[f] * even + ca[f] * odd)
         for q, val in enumerate((re, im)):
             val = jnp.sum(jnp.sum(val, axis=0, keepdims=True), axis=1, keepdims=True)
-            over[2 * f + q : 2 * f + q + 1, :] = jnp.broadcast_to(val, (1, 128))
+            over[2 * f + q : 2 * f + q + 1, :] = jnp.broadcast_to(val * scale, (1, 128))
+    for d, ref in enumerate((g0, g1, g2, g3)):
+        ref[...] = grad[d]
 
 
 def sum_kernel(a, b, c, d, out):
@@ -289,67 +316,54 @@
     ports = lax.axis_size("port")
     tile = lax.axis_index("tile")
     port = lax.axis_index("port")
-    to_right = [(i, i + 1) for i in range(tiles - 1)]
-    to_left = [(i + 1, i) for i in range(tiles - 1)]
-
-    def by_sublane(x):
-        return x.reshape(WIDTH * SLAB, 8, HALF).transpose(1, 0, 2).reshape(8, 128)
-
-    coef, mask = pl.pallas_call(
-        coef_kernel,
-        out_shape=(f32(WIDTH, *CELLS), f32(WIDTH, *CELLS)),
-        in_specs=[SMEM, VMEM, VMEM, VMEM],
-        out_specs=(VMEM, VMEM),
-        name="coef",
-    )(eps_table, by_sublane(material), by_sublane(design), rows(density))
-    coef_l = lax.ppermute(coef[WIDTH - DEPTH :], "tile", to_right)
-    coef_r = lax.ppermute(coef[:DEPTH], "tile", to_left)
 
     e_rows, h_rows = rows(e_start[0]), rows(h_start[0])
-    hist_e, hist_h = pl.pallas_call(
+    sent = f32(2 * STEPS + DEPTH, *CELLS)
+    coef, mask, to_left, to_right = pl.pallas_call(
         free_kernel,
-        out_shape=(f32(STEPS, 2, *CELLS), f32(STEPS, 2, *CELLS)),
-        in_specs=[VMEM] * 3,
-        out_specs=(VMEM, VMEM),
+        out_shape=(f32(WIDTH, *CELLS), f32(WIDTH, *CELLS), sent, sent),
+        in_specs=[SMEM] + [VMEM] * 5,
+        out_specs=(VMEM,) * 4,
         scratch_shapes=[pltpu.VMEM((3, WIDTH + 1) + CELLS, jnp.float32)] * 2,
         compiler_params=PARAMS,
         name="free",
-    )(e_rows, h_rows, coef)
-    got_e = lax.ppermute(hist_e, "tile", to_left)
-    got_h = lax.ppermute(hist_h, "tile", to_right)
+    )(eps_table, material.reshape(64, 16), design.reshape(64, 16), rows(density), e_rows, h_rows)
+    from_right = lax.ppermute(to_left, "tile", [(i + 1, i) for i in range(tiles - 1)])
+    from_left = lax.ppermute(to_right, "tile", [(i, i + 1) for i in range(tiles - 1)])
 
     info = jnp.stack([tile.astype(jnp.int32), port.astype(jnp.int32), port_mode[0]])
     profile = profiles.reshape(-1, 8, HALF, 128).transpose(0, 2, 1, 3)
-    e_out, h_out, grad, over = pl.pallas_call(
-        full_kernel,
-        out_shape=(
-            f32(3, WIDTH, 64, 128),
-            f32(3, WIDTH, 64, 128),
-            f32(SLAB, WIDTH, HALF, 8, 128),
-            f32(2 * FREQS, 128),
-        ),
-        in_specs=[SMEM] + [VMEM] * 10,
-        out_specs=(VMEM,) * 4,
+    scale = 1.0 / math.sqrt(WIDTH * tiles * SLAB * 2048)
+    e_out, h_out, *parts, over = pl.pallas_call(
+        functools.partial(full_kernel, scale),
+        out_shape=(f32(3, WIDTH, 64, 128), f32(3, WIDTH, 64, 128))
+        + (f32(WIDTH, HALF, 8, 128),) * SLAB
+        + (f32(2 * FREQS, 128),),
+        in_specs=[SMEM] + [VMEM] * 8,
+        out_specs=(VMEM,) * (3 + SLAB),
         scratch_shapes=[
-            pltpu.VMEM((STEPS + 1, 3, WIDTH + 1) + CELLS, jnp.float32),
+            pltpu.VMEM((STEPS, 3, WIDTH) + CELLS, jnp.float32),
+            pltpu.VMEM((3, WIDTH + 1) + CELLS, jnp.float32),
             pltpu.VMEM((3, WIDTH + 1) + CELLS, jnp.float32),
             pltpu.VMEM((3, DEPTH + 2) + CELLS, jnp.float32),
             pltpu.VMEM((3, DEPTH + 1) + CELLS, jnp.float32),
             pltpu.VMEM((3, DEPTH + 1) + CELLS, jnp.float32),
             pltpu.VMEM((3, DEPTH + 1) + CELLS, jnp.float32),
             pltpu.VMEM((4 * 3, 64, 128), jnp.float32),
+            pltpu.VMEM((SLAB, WIDTH, HALF, 8, 128), jnp.float32),
         ],
         compiler_params=PARAMS,
         name="full",
-    )(info, e_rows, h_rows, coef, coef_l, coef_r, got_e, got_h, rows(forward[0]), mask, profile)
-
-    parts = [grad[0]]
+    )(info, e_rows, h_rows, coef, from_left, from_right, rows(forward[0]), mask, profile)
+
     for d in range(1, ports):
-        parts.append(lax.ppermute(grad[d], "port", [(i, (i + d) % ports) for i in range(ports)]))
+        parts[d] = lax.ppermute(parts[d], "port", [(i, (i + d) % ports) for i in range(ports)])
     total = over
     span = 1
     while span < tiles:
         radix = min(4, tiles // span)
+        if span * radix >= tiles:
+            total, *parts = lax.optimization_barrier((total, *parts))
         got = []
         for d in range(1, radix):
             pairs = []
@@ -366,13 +380,11 @@
         out_specs=VMEM,
         name="total",
     )(*parts)
-    scale = math.sqrt(WIDTH * tiles * SLAB * 2048)
-    intersections = (total[:, 0] / scale).reshape(1, FREQS, 2)
     return (
         unrows(e_out)[None],
         unrows(h_out)[None],
         gradient.reshape(WIDTH, 1, 2048),
-        intersections,
+        total[:, 0].reshape(1, FREQS, 2),
     )
 
 

time: 169 us -> 142 us (0.84)
  the two profiles are of different devices: /device:TPU:8 before, /device:TPU:16 now
where the time goes in v3:
time: 142 us
  Pallas kernels  77.5 us (55%)
  starting transfers between devices  32.3 us (23%)
  waiting for transfers between devices  27.1 us (19%)
  local copies, waits for them, and re-layouts  2.49 us (2%)
    pallas_call x1, Pallas kernels, body(): pl.pallas_call(functools.partial(full_kernel, scale), out_shape=(f32(3, W...  46.6 us
    pallas_call x1, Pallas kernels, body(): pl.pallas_call(free_kernel, out_shape=(f32(WIDTH, *CELLS), f32(WIDTH, *CE...  29.1 us
    ppermute x9, starting transfers between devices, body(): got.append(lax.ppermute(total, 'tile', pairs))  15.5 us
    ppermute x1, waiting for transfers between devices, body(): lax.ppermute(to_right, 'tile', [(i, i + 1) for i in range(tiles - 1)])  11.7 us
    ppermute x3, starting transfers between devices, body(): lax.ppermute(parts[d], 'port', [(i, (i + d) % ports) for i in range(ports)])  11.3 us
    ppermute x3, waiting for transfers between devices, body(): lax.ppermute(parts[d], 'port', [(i, (i + d) % ports) for i in range(ports)])  7.51 us
    ppermute x9, waiting for transfers between devices, body(): got.append(lax.ppermute(total, 'tile', pairs))  6.03 us
    ppermute x1, starting transfers between devices, body(): lax.ppermute(to_left, 'tile', [(i + 1, i) for i in range(tiles - 1)])  3.64 us
  transfers between devices with their start and end apart: 14, of which 8 were waited for; matrix products, arithmetic and copies ran while one was open for 1% of the time, Pallas kernels for 1%

profile of v3, /device:TPU:16, one launch (start us, length us, event | category | flops | bytes accessed | tf_op | source)
XLA Modules:
  0.0 142.0 jit_solution(14432866552744618667)
XLA Ops:
  0.6 0.0 copy-start.5
  0.6 29.1 %free.1 = (f32[16,4,2,8,128]{4,3,2,1,0:T(8,128)}, f32[16,4,2,8,128]{4,3,2,1,0:T(8,128)}, f32[40,4,2,8,128]{4,3,2,1,0:T(8,128)}, f32[40,4,2,8,128]{4,3,2,1,0:T(8,128)}) custom-call(f32[4]{0:T(128)} %table.1, s32[64,16]{1,0:T(8,128)} %bitcast.46, s32[64,16]{1,0:T(8,128)} %bitcast.47, f32[16,64,128]{2,1,0:T(8,128)} %bitcast.43, f32[3,16,64,128]{3,2,1,0:T(8,128)} %bitcast.38, ...), custom_call_target="tpu_custom_call" | custom-call | tf_op jit(solution)/shard_map/free/pallas_call | solution.py:322
  29.7 1.9 %collective-permute-start = (f32[40,4,2,8,128]{4,3,2,1,0:T(8,128)}, f32[40,4,2,8,128]{4,3,2,1,0:T(8,128)S(1)}, u32[]{:S(2)}, u32[]{:S(2)}) collective-permute-start(f32[40,4,2,8,128]{4,3,2,1,0:T(8,128)} %get-tuple-element.21), channel_id=1, source_target_pairs={{0,1},{1,2},{2,3},{3,4},{4,5},{5,6},{6,7},{7,8},{8,9},{9,10},{10,1... | collective-permute-start | bytes 3932168 | tf_op jit(solution)/shard_map/ppermute | solution.py:332
  31.6 3.6 %collective-permute-start.1 = (f32[40,4,2,8,128]{4,3,2,1,0:T(8,128)}, f32[40,4,2,8,128]{4,3,2,1,0:T(8,128)S(1)}, u32[]{:S(2)}, u32[]{:S(2)}) collective-permute-start(f32[40,4,2,8,128]{4,3,2,1,0:T(8,128)} %get-tuple-element.22), channel_id=1, source_target_pairs={{1,0},{2,1},{3,2},{4,3},{5,4},{6,5},{7,6},{8,7},{9,8},{10,9},{11,1... | collective-permute-start | bytes 3932168 | tf_op jit(solution)/shard_map/ppermute | solution.py:331
  35.9 0.0 copy-done.5
  36.0 0.6 copy.29
  36.6 0.6 pad_add_fusion.info
  37.2 11.7 %collective-permute-done.from_left = f32[40,4,2,8,128]{4,3,2,1,0:T(8,128)S(1)} collective-permute-done((f32[40,4,2,8,128]{4,3,2,1,0:T(8,128)}, f32[40,4,2,8,128]{4,3,2,1,0:T(8,128)S(1)}, u32[]{:S(2)}, u32[]{:S(2)}) %collective-permute-start) | collective-permute-done | bytes 1310752 | tf_op jit(solution)/shard_map/ppermute | solution.py:332
  48.9 0.0 copy-start
  48.9 1.9 %collective-permute-done.1.from_right = f32[40,4,2,8,128]{4,3,2,1,0:T(8,128)S(1)} collective-permute-done((f32[40,4,2,8,128]{4,3,2,1,0:T(8,128)}, f32[40,4,2,8,128]{4,3,2,1,0:T(8,128)S(1)}, u32[]{:S(2)}, u32[]{:S(2)}) %collective-permute-start.1) | collective-permute-done | bytes 1310752 | tf_op jit(solution)/shard_map/ppermute | solution.py:331
  50.7 0.0 copy-start.1
  50.7 0.0 copy-done
  50.7 1.1 copy-done.1
  51.8 46.6 %full.1 = (f32[3,16,64,128]{3,2,1,0:T(8,128)}, f32[3,16,64,128]{3,2,1,0:T(8,128)}, f32[16,2,8,128]{3,2,1,0:T(8,128)}, f32[16,2,8,128]{3,2,1,0:T(8,128)}, f32[16,...) custom-call(s32[3]{0:T(128)} %pad_add_fusion.info, f32[3,16,64,128]{3,2,1,0:T(8,128)} %bitcast.39, ...), custom_call_target="tpu_custom_call" | custom-call | tf_op jit(solution)/shard_map/full/pallas_call | solution.py:337
  98.4 4.7 %collective-permute-start.4 = (f32[4,128]{1,0:T(4,128)}, f32[4,128]{1,0:T(4,128)S(1)}, u32[]{:S(2)}, u32[]{:S(2)}) collective-permute-start(f32[4,128]{1,0:T(4,128)} %get-tuple-element.26), channel_id=1, source_target_pairs={{0,3},{1,0},{2,1},{3,2},{4,7},{5,4},{6,5},{7,6},{8,11},{9,8},{10,9... | collective-permute-start | bytes 6152 | tf_op jit(solution)/shard_map/ppermute | solution.py:373
  103.2 0.0 collective-permute-start.3
  103.2 0.2 collective-permute-start.2
  103.4 1.3 collective-permute-done.4
  104.7 2.3 %collective-permute-done.3 = f32[4,128]{1,0:T(4,128)S(1)} collective-permute-done((f32[4,128]{1,0:T(4,128)}, f32[4,128]{1,0:T(4,128)S(1)}, u32[]{:S(2)}, u32[]{:S(2)}) %collective-permute-start.3) | collective-permute-done | bytes 2080 | tf_op jit(solution)/shard_map/ppermute | solution.py:373
  107.0 0.0 collective-permute-done.2
  107.0 0.7 add_add_fusion.2
  107.6 0.0 collective-permute-start.7
  107.6 1.9 %collective-permute-start.6 = (f32[4,128]{1,0:T(4,128)S(1)}, f32[4,128]{1,0:T(4,128)S(1)}, u32[]{:S(2)}, u32[]{:S(2)}) collective-permute-start(f32[4,128]{1,0:T(4,128)S(1)} %add_add_fusion.2), channel_id=1, source_target_pairs={{0,8},{1,9},{2,10},{3,11},{4,12},{5,13},{6,14},{7,15},{8,0},{9,1},... | collective-permute-start | bytes 6152 | tf_op jit(solution)/shard_map/ppermute | solution.py:373
  109.6 4.4 %collective-permute-start.5 = (f32[4,128]{1,0:T(4,128)S(1)}, f32[4,128]{1,0:T(4,128)S(1)}, u32[]{:S(2)}, u32[]{:S(2)}) collective-permute-start(f32[4,128]{1,0:T(4,128)S(1)} %add_add_fusion.2), channel_id=1, source_target_pairs={{0,4},{1,5},{2,6},{3,7},{4,8},{5,9},{6,10},{7,11},{8,12},{9,13},{1... | collective-permute-start | bytes 6152 | tf_op jit(solution)/shard_map/ppermute | solution.py:373
  114.0 3.3 %collective-permute-start.8 = (f32[16,2,8,128]{3,2,1,0:T(8,128)}, f32[16,2,8,128]{3,2,1,0:T(8,128)S(1)}, u32[]{:S(2)}, u32[]{:S(2)}) collective-permute-start(f32[16,2,8,128]{3,2,1,0:T(8,128)} %get-tuple-element.28), channel_id=1, source_target_pairs={{0,64},{64,128},{128,192},{192,0},{1,65},{65,129},{129,193},{193,1... | collective-permute-start | bytes 393224 | tf_op jit(solution)/shard_map/ppermute | solution.py:360
  117.3 5.4 %collective-permute-start.9 = (f32[16,2,8,128]{3,2,1,0:T(8,128)}, f32[16,2,8,128]{3,2,1,0:T(8,128)S(1)}, u32[]{:S(2)}, u32[]{:S(2)}) collective-permute-start(f32[16,2,8,128]{3,2,1,0:T(8,128)} %get-tuple-element.29), channel_id=1, source_target_pairs={{0,128},{64,192},{128,0},{192,64},{1,129},{65,193},{129,1},{193,65... | collective-permute-start | bytes 393224 | tf_op jit(solution)/shard_map/ppermute | solution.py:360
  122.7 0.0 collective-permute-done.7
  122.7 2.7 %collective-permute-start.10 = (f32[16,2,8,128]{3,2,1,0:T(8,128)}, f32[16,2,8,128]{3,2,1,0:T(8,128)S(1)}, u32[]{:S(2)}, u32[]{:S(2)}) collective-permute-start(f32[16,2,8,128]{3,2,1,0:T(8,128)} %get-tuple-element.30), channel_id=1, source_target_pairs={{0,192},{64,0},{128,64},{192,128},{1,193},{65,1},{129,65},{193,129... | collective-permute-start | bytes 393224 | tf_op jit(solution)/shard_map/ppermute | solution.py:360
  125.3 0.0 collective-permute-done.6
  125.3 0.0 collective-permute-done.5
  125.4 1.3 collective-permute-done.8.b
  126.6 0.0 copy-start.2
  126.6 3.7 %collective-permute-done.9.c = f32[16,2,8,128]{3,2,1,0:T(8,128)S(1)} collective-permute-done((f32[16,2,8,128]{3,2,1,0:T(8,128)}, f32[16,2,8,128]{3,2,1,0:T(8,128)S(1)}, u32[]{:S(2)}, u32[]{:S(2)}) %collective-permute-start.9) | collective-permute-done | bytes 131104 | tf_op jit(solution)/shard_map/ppermute | solution.py:360
  130.3 0.0 copy-start.3
  130.3 2.5 %collective-permute-done.10.d = f32[16,2,8,128]{3,2,1,0:T(8,128)S(1)} collective-permute-done((f32[16,2,8,128]{3,2,1,0:T(8,128)}, f32[16,2,8,128]{3,2,1,0:T(8,128)S(1)}, u32[]{:S(2)}, u32[]{:S(2)}) %collective-permute-start.10) | collective-permute-done | bytes 131104 | tf_op jit(solution)/shard_map/ppermute | solution.py:360
  132.9 0.0 copy-start.4
  132.9 0.0 collective-permute-start.13
  132.9 3.6 %collective-permute-start.12 = (f32[4,128]{1,0:T(4,128)S(1)}, f32[4,128]{1,0:T(4,128)S(1)}, u32[]{:S(2)}, u32[]{:S(2)}) collective-permute-start(f32[4,128]{1,0:T(4,128)S(1)} %add_add_fusion.1), channel_id=1, source_target_pairs={{0,32},{1,33},{2,34},{3,35},{4,36},{5,37},{6,38},{7,39},{8,40},{9,... | collective-permute-start | bytes 6152 | tf_op jit(solution)/shard_map/ppermute | solution.py:373
  136.4 0.6 collective-permute-start.11
  137.0 0.0 copy-done.2
  137.0 0.0 copy-done.3
  137.0 0.0 copy-done.4
  137.0 1.8 %total.1 = f32[16,16,128]{2,1,0:T(8,128)} custom-call(f32[16,2,8,128]{3,2,1,0:T(8,128)} %get-tuple-element.31.a, f32[16,2,8,128]{3,2,1,0:T(8,128)} %copy-done.2, f32[16,2,8,128]{3,2,1,0:T(8,128)} %copy-done.3, f32[16,2,8,128]{3,2,1,0:T(8,128)} %copy-done.4), custom_call_target="tpu_custom_call" | custom-call | tf_op jit(solution)/shard_map/total/pallas_call | solution.py:376
  138.8 0.0 collective-permute-done.13
  138.8 0.0 collective-permute-done.12
  138.8 2.4 %collective-permute-done.11 = f32[4,128]{1,0:T(4,128)S(1)} collective-permute-done((f32[4,128]{1,0:T(4,128)S(1)}, f32[4,128]{1,0:T(4,128)S(1)}, u32[]{:S(2)}, u32[]{:S(2)}) %collective-permute-start.11) | collective-permute-done | bytes 2080 | tf_op jit(solution)/shard_map/ppermute | solution.py:373
  141.2 0.1 slice_reduce_fusion
  141.3 0.6 reshape_squeeze.15
  (3 shorter events, 0.1 us)
Async XLA Ops:
  0.6 35.3 %copy-start.5 = (f32[4,2048]{1,0:T(4,128)S(1)}, f32[4,2048]{1,0:T(4,128)}, u32[]{:S(2)}) copy-start(f32[4,2048]{1,0:T(4,128)} %param.16) | copy-start | bytes 98308
  29.7 19.1 %collective-permute-start = (f32[40,4,2,8,128]{4,3,2,1,0:T(8,128)}, f32[40,4,2,8,128]{4,3,2,1,0:T(8,128)S(1)}, u32[]{:S(2)}, u32[]{:S(2)}) collective-permute-start(f32[40,4,2,8,128]{4,3,2,1,0:T(8,128)} %get-tuple-element.21), channel_id=1, source_target_pairs={{0,1},{1,2},{2,3},{3,4},{4,5},{5,6},{6,7},{7,8},{8,9},{9,10},{10,1... | collective-permute-start | bytes 3932168 | tf_op jit(solution)/shard_map/ppermute | solution.py:332
  31.6 19.1 %collective-permute-start.1 = (f32[40,4,2,8,128]{4,3,2,1,0:T(8,128)}, f32[40,4,2,8,128]{4,3,2,1,0:T(8,128)S(1)}, u32[]{:S(2)}, u32[]{:S(2)}) collective-permute-start(f32[40,4,2,8,128]{4,3,2,1,0:T(8,128)} %get-tuple-element.22), channel_id=1, source_target_pairs={{1,0},{2,1},{3,2},{4,3},{5,4},{6,5},{7,6},{8,7},{9,8},{10,9},{11,1... | collective-permute-start | bytes 3932168 | tf_op jit(solution)/shard_map/ppermute | solution.py:331
  48.9 1.9 %copy-start = (f32[40,4,2,8,128]{4,3,2,1,0:T(8,128)}, f32[40,4,2,8,128]{4,3,2,1,0:T(8,128)S(1)}, u32[]{:S(2)}) copy-start(f32[40,4,2,8,128]{4,3,2,1,0:T(8,128)S(1)} %collective-permute-done.from_left) | copy-start | bytes 3932164
  50.7 1.1 copy-start.1
  98.4 6.3 %collective-permute-start.4 = (f32[4,128]{1,0:T(4,128)}, f32[4,128]{1,0:T(4,128)S(1)}, u32[]{:S(2)}, u32[]{:S(2)}) collective-permute-start(f32[4,128]{1,0:T(4,128)} %get-tuple-element.26), channel_id=1, source_target_pairs={{0,3},{1,0},{2,1},{3,2},{4,7},{5,4},{6,5},{7,6},{8,11},{9,8},{10,9... | collective-permute-start | bytes 6152 | tf_op jit(solution)/shard_map/ppermute | solution.py:373
  103.2 3.8 %collective-permute-start.3 = (f32[4,128]{1,0:T(4,128)}, f32[4,128]{1,0:T(4,128)S(1)}, u32[]{:S(2)}, u32[]{:S(2)}) collective-permute-start(f32[4,128]{1,0:T(4,128)} %get-tuple-element.26), channel_id=1, source_target_pairs={{0,2},{1,3},{2,0},{3,1},{4,6},{5,7},{6,4},{7,5},{8,10},{9,11},{10,... | collective-permute-start | bytes 6152 | tf_op jit(solution)/shard_map/ppermute | solution.py:373
  103.2 3.8 %collective-permute-start.2 = (f32[4,128]{1,0:T(4,128)}, f32[4,128]{1,0:T(4,128)S(1)}, u32[]{:S(2)}, u32[]{:S(2)}) collective-permute-start(f32[4,128]{1,0:T(4,128)} %get-tuple-element.26), channel_id=1, source_target_pairs={{0,1},{1,2},{2,3},{3,0},{4,5},{5,6},{6,7},{7,4},{8,9},{9,10},{10,1... | collective-permute-start | bytes 6152 | tf_op jit(solution)/shard_map/ppermute | solution.py:373
  107.6 15.0 %collective-permute-start.7 = (f32[4,128]{1,0:T(4,128)S(1)}, f32[4,128]{1,0:T(4,128)S(1)}, u32[]{:S(2)}, u32[]{:S(2)}) collective-permute-start(f32[4,128]{1,0:T(4,128)S(1)} %add_add_fusion.2), channel_id=1, source_target_pairs={{0,12},{1,13},{2,14},{3,15},{4,0},{5,1},{6,2},{7,3},{8,4},{9,5},{1... | collective-permute-start | bytes 6152 | tf_op jit(solution)/shard_map/ppermute | solution.py:373
  107.6 17.7 %collective-permute-start.6 = (f32[4,128]{1,0:T(4,128)S(1)}, f32[4,128]{1,0:T(4,128)S(1)}, u32[]{:S(2)}, u32[]{:S(2)}) collective-permute-start(f32[4,128]{1,0:T(4,128)S(1)} %add_add_fusion.2), channel_id=1, source_target_pairs={{0,8},{1,9},{2,10},{3,11},{4,12},{5,13},{6,14},{7,15},{8,0},{9,1},... | collective-permute-start | bytes 6152 | tf_op jit(solution)/shard_map/ppermute | solution.py:373
  109.6 15.8 %collective-permute-start.5 = (f32[4,128]{1,0:T(4,128)S(1)}, f32[4,128]{1,0:T(4,128)S(1)}, u32[]{:S(2)}, u32[]{:S(2)}) collective-permute-start(f32[4,128]{1,0:T(4,128)S(1)} %add_add_fusion.2), channel_id=1, source_target_pairs={{0,4},{1,5},{2,6},{3,7},{4,8},{5,9},{6,10},{7,11},{8,12},{9,13},{1... | collective-permute-start | bytes 6152 | tf_op jit(solution)/shard_map/ppermute | solution.py:373
  114.0 12.6 %collective-permute-start.8 = (f32[16,2,8,128]{3,2,1,0:T(8,128)}, f32[16,2,8,128]{3,2,1,0:T(8,128)S(1)}, u32[]{:S(2)}, u32[]{:S(2)}) collective-permute-start(f32[16,2,8,128]{3,2,1,0:T(8,128)} %get-tuple-element.28), channel_id=1, source_target_pairs={{0,64},{64,128},{128,192},{192,0},{1,65},{65,129},{129,193},{193,1... | collective-permute-start | bytes 393224 | tf_op jit(solution)/shard_map/ppermute | solution.py:360
  117.3 13.0 %collective-permute-start.9 = (f32[16,2,8,128]{3,2,1,0:T(8,128)}, f32[16,2,8,128]{3,2,1,0:T(8,128)S(1)}, u32[]{:S(2)}, u32[]{:S(2)}) collective-permute-start(f32[16,2,8,128]{3,2,1,0:T(8,128)} %get-tuple-element.29), channel_id=1, source_target_pairs={{0,128},{64,192},{128,0},{192,64},{1,129},{65,193},{129,1},{193,65... | collective-permute-start | bytes 393224 | tf_op jit(solution)/shard_map/ppermute | solution.py:360
  122.7 10.2 %collective-permute-start.10 = (f32[16,2,8,128]{3,2,1,0:T(8,128)}, f32[16,2,8,128]{3,2,1,0:T(8,128)S(1)}, u32[]{:S(2)}, u32[]{:S(2)}) collective-permute-start(f32[16,2,8,128]{3,2,1,0:T(8,128)} %get-tuple-element.30), channel_id=1, source_target_pairs={{0,192},{64,0},{128,64},{192,128},{1,193},{65,1},{129,65},{193,129... | collective-permute-start | bytes 393224 | tf_op jit(solution)/shard_map/ppermute | solution.py:360
  126.6 10.4 %copy-start.2 = (f32[16,2,8,128]{3,2,1,0:T(8,128)}, f32[16,2,8,128]{3,2,1,0:T(8,128)S(1)}, u32[]{:S(2)}) copy-start(f32[16,2,8,128]{3,2,1,0:T(8,128)S(1)} %collective-permute-done.8.b) | copy-start | bytes 393220
  130.3 6.7 %copy-start.3 = (f32[16,2,8,128]{3,2,1,0:T(8,128)}, f32[16,2,8,128]{3,2,1,0:T(8,128)S(1)}, u32[]{:S(2)}) copy-start(f32[16,2,8,128]{3,2,1,0:T(8,128)S(1)} %collective-permute-done.9.c) | copy-start | bytes 393220
  132.9 4.2 %copy-start.4 = (f32[16,2,8,128]{3,2,1,0:T(8,128)}, f32[16,2,8,128]{3,2,1,0:T(8,128)S(1)}, u32[]{:S(2)}) copy-start(f32[16,2,8,128]{3,2,1,0:T(8,128)S(1)} %collective-permute-done.10.d) | copy-start | bytes 393220
  132.9 5.9 %collective-permute-start.13 = (f32[4,128]{1,0:T(4,128)S(1)}, f32[4,128]{1,0:T(4,128)S(1)}, u32[]{:S(2)}, u32[]{:S(2)}) collective-permute-start(f32[4,128]{1,0:T(4,128)S(1)} %add_add_fusion.1), channel_id=1, source_target_pairs={{0,48},{1,49},{2,50},{3,51},{4,52},{5,53},{6,54},{7,55},{8,56},{9,... | collective-permute-start | bytes 6152 | tf_op jit(solution)/shard_map/ppermute | solution.py:373
  132.9 5.9 %collective-permute-start.12 = (f32[4,128]{1,0:T(4,128)S(1)}, f32[4,128]{1,0:T(4,128)S(1)}, u32[]{:S(2)}, u32[]{:S(2)}) collective-permute-start(f32[4,128]{1,0:T(4,128)S(1)} %add_add_fusion.1), channel_id=1, source_target_pairs={{0,32},{1,33},{2,34},{3,35},{4,36},{5,37},{6,38},{7,39},{8,40},{9,... | collective-permute-start | bytes 6152 | tf_op jit(solution)/shard_map/ppermute | solution.py:373
  136.4 4.8 %collective-permute-start.11 = (f32[4,128]{1,0:T(4,128)S(1)}, f32[4,128]{1,0:T(4,128)S(1)}, u32[]{:S(2)}, u32[]{:S(2)}) collective-permute-start(f32[4,128]{1,0:T(4,128)S(1)} %add_add_fusion.1), channel_id=1, source_target_pairs={{0,16},{1,17},{2,18},{3,19},{4,20},{5,21},{6,22},{7,23},{8,24},{9,... | collective-permute-start | bytes 6152 | tf_op jit(solution)/shard_map/ppermute | solution.py:373

commit v4 on v3

v4 whole, which is shorter than its diff:
```python
import functools
import math

import jax
import jax.numpy as jnp
import numpy as np
from jax import lax
from jax.experimental import pallas as pl
from jax.experimental.pallas import tpu as pltpu
from jax.sharding import PartitionSpec as P

STEPS = 16
OMEGA = 0.7
COEF_H = 0.5
COEF_E = 0.5

WIDTH = 16
SLAB = 4
HALF = 2
DEPTH = STEPS // 2
FREQS = 2
CELLS = (SLAB, HALF, 8, 128)


def rows(x):
    lead = x.shape[:-2]
    x = x.reshape(lead + (SLAB, 16, 128))
    return jnp.swapaxes(x, -3, -2).reshape(lead + (64, 128))


def unrows(x):
    lead = x.shape[:-2]
    x = x.reshape(lead + (16, SLAB, 128))
    return jnp.swapaxes(x, -3, -2).reshape(lead + (SLAB, 2048))


def masks():
    lane = lax.broadcasted_iota(jnp.int32, (8, 128), 1)
    sub = lax.broadcasted_iota(jnp.int32, (8, 128), 0)
    return lane == 127, lane == 0, sub == 7, sub == 0


def ahead_y(pair, m):
    r0 = pltpu.roll(pair[0], 127, 1)
    r1 = pltpu.roll(pair[1], 127, 1)
    rs = jnp.where(m[2], 0.0, pltpu.roll(r0, 7, 0))
    return jnp.where(m[0], r1, r0), jnp.where(m[0], rs, r1)


def behind_y(pair, m):
    r0 = pltpu.roll(pair[0], 1, 1)
    r1 = pltpu.roll(pair[1], 1, 1)
    rs = jnp.where(m[3], 0.0, pltpu.roll(r1, 1, 0))
    return jnp.where(m[1], rs, r0), jnp.where(m[1], r0, r1)


def update_plane(e_old, e_next, h_now, h_prev, coef, e_new, m, keep=None, sums=None):
    def plane(ref, comp):
        return [[ref[comp, z, v] for v in range(HALF)] for z in range(SLAB)]

    ex, ey, ez = (plane(e_old, comp) for comp in range(3))
    ey_x, ez_x = plane(e_next, 1), plane(e_next, 2)
    hx, hy, hz = (plane(h_now, comp) for comp in range(3))
    hy_x, hz_x = plane(h_prev, 1), plane(h_prev, 2)
    c = [[coef[z, v] for v in range(HALF)] for z in range(SLAB)]
    edge = [0.0] * HALF
    new_e = []
    for z in range(SLAB):
        ex_z, ey_z = (ex[z + 1], ey[z + 1]) if z + 1 < SLAB else (edge, edge)
        ez_y, ex_y = ahead_y(ez[z], m), ahead_y(ex[z], m)
        for v in range(HALF):
            hx[z][v] = hx[z][v] - ((ez_y[v] - ez[z][v]) - (ey_z[v] - ey[z][v]))
            hy[z][v] = hy[z][v] - ((ex_z[v] - ex[z][v]) - (ez_x[z][v] - ez[z][v]))
            hz[z][v] = hz[z][v] - ((ey_x[z][v] - ey[z][v]) - (ex_y[v] - ex[z][v]))
        hz_y, hx_y = behind_y(hz[z], m), behind_y(hx[z], m)
        hx_z, hy_z = (hx[z - 1], hy[z - 1]) if z > 0 else (edge, edge)
        for v in range(HALF):
            curl_x = (hz[z][v] - hz_y[v]) - (hy[z][v] - hy_z[v])
            curl_y = (hx[z][v] - hx_z[v]) - (hz[z][v] - hz_x[z][v])
            curl_z = (hy[z][v] - hy_x[z][v]) - (hx[z][v] - hx_y[v])
            new_e.append(
                (
                    ex[z][v] + c[z][v] * curl_x,
                    ey[z][v] + c[z][v] * curl_y,
                    ez[z][v] + c[z][v] * curl_z,
                )
            )
    for z in range(SLAB):
        for v in range(HALF):
            for comp, h in enumerate((hx, hy, hz)):
                h_now[comp, z, v] = h[z][v]
                e_new[comp, z, v] = new_e[z * HALF + v][comp]
                if keep is not None:
                    keep[comp, z, v] = new_e[z * HALF + v][comp]
    if sums is not None:
        for v in range(HALF):
            sums[v] += sum(new_e[z * HALF + v][1] for z in range(SLAB))


def sweep(blocks, planes, one):
    def block(i, _):
        for plane in planes(i):
            one(plane)
        return 0

    lax.fori_loop(0, blocks, block, 0)


def strided(z, v):
    return pl.ds(4 * v + z, 8, stride=8)


def load_rows(src, dst, scale, first=0, count=WIDTH, base=0):
    def one(x, _):
        for comp in range(3):
            for z in range(SLAB):
                for v in range(HALF):
                    val = src[comp, first + x, strided(z, v), :]
                    dst[comp, base + x, z, v] = val if scale == 1.0 else val * scale
        return 0

    lax.fori_loop(0, count, one, 0)


def by_sublane(ref, v):
    row = lax.broadcasted_iota(jnp.int32, (8, 16), 0)
    col = lax.broadcasted_iota(jnp.int32, (8, 16), 1)
    pick = (col == HALF * row + v).astype(jnp.float32)
    values = ref[...].astype(jnp.float32)
    return lax.dot_general(pick, values, (((1,), (1,)), ((), ())), preferred_element_type=jnp.float32)


def free_kernel(
    info, table, mat_far, des_far, dens_far, e_far, h_far,
    coef_far, inter_far, intra_far,
    ea, ha, eb, hb, coef, mat, des, dens, e_in, h_in, faces, sems, sent,
):
    m = masks()
    to_left, to_right = faces.at[0], faces.at[1]
    odd = lax.rem(info[0], 2)
    pairs = ((mat_far, mat), (des_far, des), (dens_far, dens), (e_far, e_in), (h_far, h_in))
    fetch = [pltpu.make_async_copy(src, dst, sems.at[i]) for i, (src, dst) in enumerate(pairs)]
    for copy in fetch:
        copy.start()
    for copy in fetch[:3]:
        copy.wait()
    for v in range(HALF):
        kind = by_sublane(mat, v)
        flag = by_sublane(des, v)
        base = jnp.zeros(kind.shape, jnp.float32)
        for which in range(table.shape[0]):
            base = base + jnp.where(kind == which, table[which], 0.0)
        for x in range(WIDTH):
            for z in range(SLAB):
                at = x * SLAB + z
                b = jnp.broadcast_to(base[:, at : at + 1], (8, 128))
                d = jnp.broadcast_to(flag[:, at : at + 1], (8, 128))
                eps = b + d * dens[x, strided(z, v), :]
                coef[x, z, v] = (COEF_E * COEF_H) / eps
    coef_out = pltpu.make_async_copy(coef, coef_far, sent.at[4])
    coef_out.start()
    to_left[2 * STEPS :] = coef[:DEPTH]
    to_right[2 * STEPS :] = coef[WIDTH - DEPTH :]

    half = WIDTH // 2
    fetch[3].wait()
    fetch[4].wait()
    load_rows(e_in, ea, 1.0, 0, half)
    load_rows(e_in, eb, 1.0, half, half)
    load_rows(h_in, ha, 1.0 / COEF_H, 0, half, 1)
    load_rows(h_in, hb, 1.0 / COEF_H, half, half, 1)
    eb[:, half] = jnp.zeros((3,) + CELLS, jnp.float32)
    ha[:, 0] = jnp.zeros((3,) + CELLS, jnp.float32)
    to_left[0:2] = ea[1:3, 0]

    def low(x):
        update_plane(ea.at[:, x], ea.at[:, x + 1], ha.at[:, x + 1], ha.at[:, x], coef.at[x], ea.at[:, x], m)

    def high(x):
        update_plane(eb.at[:, x], eb.at[:, x + 1], hb.at[:, x + 1], hb.at[:, x], coef.at[half + x], eb.at[:, x], m)

    def early(s, _):
        ea[1:3, half] = eb[1:3, 0]
        sweep(half // 4, lambda i: [4 * i + k for k in range(4)], low)
        hb[1:3, 0] = ha[1:3, half]
        sweep(half // 4, lambda i: [4 * i + k for k in range(4)], high)
        to_left[pl.ds(2 * s, 2)] = ea[1:3, 0]
        to_right[pl.ds(2 * s - 2, 2)] = hb[1:3, half]
        return 0

    def late(s, _):
        blocks = (STEPS + 2 - s) // 2
        first = half - 2 * blocks
        sweep(
            blocks,
            lambda i: [(low, 2 * i), (high, first + 2 * i), (low, 2 * i + 1), (high, first + 2 * i + 1)],
            lambda job: job[0](job[1]),
        )

        @pl.when(s < STEPS)
        def _():
            to_left[pl.ds(2 * s, 2)] = ea[1:3, 0]

        to_right[pl.ds(2 * s - 2, 2)] = hb[1:3, half]
        return 0

    lax.fori_loop(1, DEPTH + 1, early, 0)
    cut = 2 * DEPTH
    sends = []
    for first, count in ((0, cut), (cut, 2 * STEPS + DEPTH - cut)):
        for side, far in ((odd, inter_far), (1 - odd, intra_far)):
            part = pl.ds(first, count)
            sends.append(pltpu.make_async_copy(faces.at[side, part], far.at[part], sent.at[len(sends)]))
    sends[0].start()
    sends[1].start()
    lax.fori_loop(DEPTH + 1, STEPS + 1, late, 0)
    sends[2].start()
    sends[3].start()
    for copy in sends + [coef_out]:
        copy.wait()


def angles():
    omegas = [OMEGA * (f + 1) for f in range(FREQS)]
    mid = (STEPS + 1) / 2
    return omegas, [float(np.cos(w * mid)) for w in omegas], [float(np.sin(w * mid)) for w in omegas]


def wide_kernel(forward, des, profile_in, e_in, h_in, turned, profile, e_all, h_all, wide, mask):
    _, ca, sa = angles()
    profile[...] = profile_in[...]
    for v in range(HALF):
        flag = by_sublane(des, v)
        for x in range(WIDTH):
            for z in range(SLAB):
                at = x * SLAB + z
                mask[x, z, v] = jnp.broadcast_to(flag[:, at : at + 1], (8, 128)) * (1.0 / STEPS)
    load_rows(e_in, e_all, 1.0)
    load_rows(h_in, h_all, 1.0 / COEF_H)

    def one(x, _):
        for f in range(FREQS):
            for q in range(2):
                for comp in range(3):
                    wide[(f * 2 + q) * 3 + comp] = forward[f, q, comp, x].astype(jnp.float32)

        def at_z(z, _):
            for v in range(HALF):
                keep = mask[x, z, v]
                for f in range(FREQS):
                    for comp in range(3):
                        re = wide[(f * 2) * 3 + comp, strided(z, v), :]
                        im = wide[(f * 2 + 1) * 3 + comp, strided(z, v), :]
                        turned[f, 0, comp, z, x, v] = keep * (re * ca[f] + im * sa[f])
                        turned[f, 1, comp, z, x, v] = keep * (im * ca[f] - re * sa[f])
            return 0

        return lax.fori_loop(0, SLAB, at_z, 0)

    lax.fori_loop(0, WIDTH, one, 0)


def terms(away, info, e, turned, grad):
    omegas, _, _ = angles()
    z = lax.rem(info[1] + away, SLAB)

    def one(x, _):
        for v in range(HALF):
            total = None
            for comp in range(3):
                plus, minus = [], []
                for i in range(STEPS // 2):
                    lo = e[STEPS // 2 - 1 - i, comp, x, z, v]
                    hi = e[STEPS // 2 + i, comp, x, z, v]
                    plus.append(hi + lo)
                    minus.append(hi - lo)
                for f in range(FREQS):
                    even = odd = None
                    for i in range(STEPS // 2):
                        c = float(np.cos(omegas[f] * (i + 0.5)))
                        s = float(np.sin(omegas[f] * (i + 0.5)))
                        even = c * plus[i] if even is None else even + c * plus[i]
                        odd = s * minus[i] if odd is None else odd + s * minus[i]
                    term = even * turned[f, 0, comp, z, x, v] + odd * turned[f, 1, comp, z, x, v]
                    total = term if total is None else total + term
            grad[x, v] = total
        return 0

    lax.fori_loop(0, WIDTH, one, 0)


def out_kernel(e, h, e_out, h_out):
    def one(x, _):
        for z in range(SLAB):
            for v in range(HALF):
                for comp in range(3):
                    e_out[comp, x, strided(z, v), :] = e[comp, x, z, v]
                    h_out[comp, x, strided(z, v), :] = h[comp, x + 1, z, v] * COEF_H
        return 0

    lax.fori_loop(0, WIDTH, one, 0)


def steps_kernel(
    scale, info, e_all, h_all, coef, inter, intra, profile, turned,
    now, h, over, *rest,
):
    grads_far, (e, el, hl, er, hr, sums, *grads, got, sems) = rest[:SLAB], rest[SLAB:]
    m = masks()
    odd = lax.rem(info[0], 2)
    fetch = [
        pltpu.make_async_copy(far, got.at[side], sems.at[SLAB + i])
        for i, (side, far) in enumerate(((odd, inter), (1 - odd, intra)))
    ]
    for copy in fetch:
        copy.start()
    from_left, from_right = got.at[0], got.at[1]

    def place(x, _):
        for comp in range(3):
            now[comp, x] = e_all[comp, x]
            h[comp, x + 1] = h_all[comp, x]
        return 0

    lax.fori_loop(0, WIDTH, place, 0)
    sums[...] = jnp.zeros(sums.shape, jnp.float32)
    for ref in (el, hl, er, hr):
        ref[...] = jnp.zeros(ref.shape, jnp.float32)
    inner = (info[0] > 0).astype(jnp.float32)

    def left(x):
        update_plane(
            el.at[:, x + 1], el.at[:, x + 2], hl.at[:, x + 1], hl.at[:, x],
            from_left.at[2 * STEPS + x], el.at[:, x + 1], m,
        )

    def right(x):
        update_plane(
            er.at[:, x], er.at[:, x + 1], hr.at[:, x + 1], hr.at[:, x],
            from_right.at[2 * STEPS + x], er.at[:, x], m,
        )

    def halos(s):
        el[1:3, DEPTH + 1] = now[1:3, 0]
        blocks = (jnp.minimum(s + 1, STEPS - s) + 1) // 2
        low = DEPTH - 2 * blocks
        sweep(
            blocks,
            lambda i: [(left, low + 2 * i), (right, 2 * i), (left, low + 2 * i + 1), (right, 2 * i + 1)],
            lambda job: job[0](job[1]),
        )

    def step(s, _):
        now[1:3, WIDTH] = er[1:3, 0] + from_right[pl.ds(2 * s - 2, 2)]
        h[1:3, 0] = hl[1:3, DEPTH] * inner + from_left[pl.ds(2 * s - 2, 2)]

        def own(x):
            update_plane(
                now.at[:, x], now.at[:, x + 1], h.at[:, x + 1], h.at[:, x], coef.at[x], now.at[:, x], m,
                e.at[s - 1, :, x], sums.at[s - 1],
            )

        sweep(WIDTH // 4, lambda i: [4 * i + k for k in range(4)], own)
        hr[1:3, 0] = h[1:3, WIDTH]
        halos(s)
        return 0

    for copy in fetch:
        copy.wait()
    halos(0)
    lax.fori_loop(1, STEPS + 1, step, 0)

    omegas = [OMEGA * (f + 1) for f in range(FREQS)]
    profiled = [sum(sums[t, v] * profile[strided(info[2], v), :] for v in range(HALF)) for t in range(STEPS)]
    for f in range(FREQS):
        for q in range(2):
            turn = [float(np.cos(omegas[f] * (t + 1))) if q == 0 else -float(np.sin(omegas[f] * (t + 1))) for t in range(STEPS)]
            val = sum(turn[t] * profiled[t] for t in range(STEPS))
            val = jnp.sum(jnp.sum(val, axis=0, keepdims=True), axis=1, keepdims=True)
            over[2 * f + q : 2 * f + q + 1, :] = jnp.broadcast_to(val * scale, (1, 128))
    copies = []
    for away in (1, 2, 3, 0):
        terms(away, info, e, turned, grads[away])
        copies.append(pltpu.make_async_copy(grads[away], grads_far[away], sems.at[away]))
        copies[-1].start()
    for copy in copies:
        copy.wait()


def sum_kernel(a, b, c, d, out):
    for x in range(WIDTH):
        for v in range(HALF):
            out[x, pl.ds(v, 8, stride=2), :] = (a[x, v] + b[x, v]) + (c[x, v] + d[x, v])


def add_kernel(*refs):
    total = refs[0][...]
    for ref in refs[1:-1]:
        total = total + ref[...]
    refs[-1][...] = total


def f32(*shape):
    return jax.ShapeDtypeStruct(shape, jnp.float32)


VMEM = pl.BlockSpec(memory_space=pltpu.VMEM)
SMEM = pl.BlockSpec(memory_space=pltpu.SMEM)
FAR = pl.BlockSpec(memory_space=pltpu.HBM)
ANY = pl.BlockSpec(memory_space=pl.ANY)


def room(mib):
    return pltpu.CompilerParams(vmem_limit_bytes=mib * 1024 * 1024)


def held(*shape):
    return pltpu.VMEM(shape, jnp.float32)


def here(x):
    return pltpu.with_memory_space_constraint(x, pltpu.VMEM)


def far(x):
    return pltpu.with_memory_space_constraint(x, pltpu.HBM)


def body(e_start, h_start, forward, density, material, design, eps_table, profiles, port_mode):
    tiles = lax.axis_size("tile")
    ports = lax.axis_size("port")
    tile = lax.axis_index("tile")
    port = lax.axis_index("port")

    e_rows, h_rows = rows(e_start[0]), rows(h_start[0])
    planes = 2 * STEPS + DEPTH
    sent = pltpu.HBM((planes, *CELLS), jnp.float32)
    half = (3, WIDTH // 2 + 1) + CELLS
    info = jnp.stack([tile.astype(jnp.int32), port.astype(jnp.int32), port_mode[0]])
    coef, inter, intra = pl.pallas_call(
        free_kernel,
        out_shape=(pltpu.HBM((WIDTH, *CELLS), jnp.float32), sent, sent),
        in_specs=[SMEM] * 2 + [FAR] * 5,
        out_specs=(FAR,) * 3,
        scratch_shapes=[held(*half)] * 4
        + [
            held(WIDTH, *CELLS),
            pltpu.VMEM((64, 16), jnp.int32),
            pltpu.VMEM((64, 16), jnp.int32),
            held(WIDTH, 64, 128),
            held(3, WIDTH, 64, 128),
            held(3, WIDTH, 64, 128),
            held(2, planes, *CELLS),
            pltpu.SemaphoreType.DMA((5,)),
            pltpu.SemaphoreType.DMA((5,)),
        ],
        compiler_params=room(14),
        name="free",
    )(
        info, eps_table, far(material.reshape(64, 16)), far(design.reshape(64, 16)), far(rows(density)),
        far(e_rows), far(h_rows),
    )
    across = [(i, i + 1) for i in range(1, tiles - 1, 2)]
    inter = lax.ppermute(inter, "tile", across + [(j, i) for i, j in across])
    intra = lax.ppermute(intra, "tile", [(i, i ^ 1) for i in range(tiles)])

    fields = held(3, WIDTH, *CELLS)
    turned, profile, e_all, h_all = pl.pallas_call(
        wide_kernel,
        out_shape=(held(FREQS, 2, 3, SLAB, WIDTH, HALF, 8, 128), f32(64, 128), fields, fields),
        in_specs=[VMEM] * 5,
        out_specs=(VMEM,) * 4,
        scratch_shapes=[held(4 * 3, 64, 128), held(WIDTH, *CELLS)],
        compiler_params=room(4),
        name="wide",
    )(rows(forward[0]), design.reshape(64, 16), rows(profiles), e_rows, h_rows)

    scale = 1.0 / math.sqrt(WIDTH * tiles * SLAB * 2048)
    edge = (3, DEPTH + 1) + CELLS
    wider = held(3, WIDTH + 1, *CELLS)
    e_last, h_last, over, *parts = pl.pallas_call(
        functools.partial(steps_kernel, scale),
        out_shape=(wider, wider, f32(2 * FREQS, 128)) + (pltpu.HBM((WIDTH, HALF, 8, 128), jnp.float32),) * SLAB,
        in_specs=[SMEM] + [VMEM] * 3 + [ANY] * 2 + [VMEM] * 2,
        out_specs=(VMEM,) * 3 + (FAR,) * SLAB,
        scratch_shapes=[
            held(STEPS, 3, WIDTH, *CELLS),
            held(3, DEPTH + 2, *CELLS),
            held(*edge),
            held(*edge),
            held(*edge),
            held(STEPS, HALF, 8, 128),
        ]
        + [held(WIDTH, HALF, 8, 128)] * SLAB
        + [held(2, planes, *CELLS), pltpu.SemaphoreType.DMA((SLAB + 2,))],
        compiler_params=room(39),
        name="steps",
    )(info, here(e_all), here(h_all), coef, inter, intra, profile, here(turned))

    def to_port(x, d):
        return lax.ppermute(x, "port", [(i, (i + d) % ports) for i in range(ports)])

    def stage(total, steps):
        got = []
        for mask in range(1, 1 << len(steps)):
            flip = sum(by for bit, by in enumerate(steps) if mask >> bit & 1)
            got.append(lax.ppermute(total, "tile", [(i, i ^ flip) for i in range(tiles)]))
        return pl.pallas_call(
            add_kernel,
            out_shape=f32(*total.shape),
            in_specs=[VMEM] * (1 + len(got)),
            out_specs=VMEM,
            compiler_params=room(1),
            name="add",
        )(total, *got)

    e_out, h_out = pl.pallas_call(
        out_kernel,
        out_shape=(f32(3, WIDTH, 64, 128), f32(3, WIDTH, 64, 128)),
        in_specs=[VMEM] * 2,
        out_specs=(VMEM,) * 2,
        compiler_params=room(4),
        name="out",
    )(here(e_last), here(h_last))
    total = stage(over, (1, 8))
    total, e_out, h_out, *parts = lax.optimization_barrier((total, e_out, h_out, *parts))
    for d in range(1, ports):
        parts[d] = to_port(parts[d], d)
    total = stage(total, (2, 4))
    total, *parts = lax.optimization_barrier((total, *parts))
    total = stage(total, (16, 32))
    gradient = pl.pallas_call(
        sum_kernel,
        out_shape=f32(WIDTH, 16, 128),
        in_specs=[VMEM] * 4,
        out_specs=VMEM,
        name="total",
    )(*parts)
    return (
        unrows(e_out)[None],
        unrows(h_out)[None],
        gradient.reshape(WIDTH, 1, 2048),
        total[:, 0].reshape(1, FREQS, 2),
    )


def solution(mesh):
    return jax.shard_map(
        body,
        mesh=mesh,
        in_specs=(
            P("port", None, "tile", None, None),
            P("port", None, "tile", None, None),
            P("port", None, None, None, "tile", None, None),
            P("tile", None, None),
            P("tile", None, None),
            P("tile", None, None),
            P(),
            P(),
            P("port"),
        ),
        out_specs=(
            P("port", None, "tile", None, None),
            P("port", None, "tile", None, None),
            P("tile", "port", None),
            P("port", None, None),
        ),
        check_vma=False,
    )
```

time: 142 us -> 121 us (0.85)
  the two profiles are of different devices: /device:TPU:16 before, /device:TPU:8 now
where the time goes in v4:
time: 121 us; the launch traced here: 119 us
  Pallas kernels  70.3 us (58%)
  starting transfers between devices  28.1 us (23%)
  waiting for transfers between devices  14.6 us (12%)
  local copies, waits for them, and re-layouts  4.4 us (4%)
  between operations  1.39 us (1%)
    pallas_call x1, Pallas kernels, body(): pl.pallas_call(functools.partial(steps_kernel, scale), out_shape=(wider,...  41.5 us
    pallas_call x1, Pallas kernels, body(): pl.pallas_call(free_kernel, out_shape=(pltpu.HBM((WIDTH, *CELLS), jnp.flo...  20.8 us
    ppermute x9, starting transfers between devices, stage(): lax.ppermute(total, 'tile', [(i, i ^ flip) for i in range(tiles)])  13.9 us
    ppermute x3, starting transfers between devices, to_port(): return lax.ppermute(x, 'port', [(i, (i + d) % ports) for i in range(ports)])  10.5 us
    ppermute x1, waiting for transfers between devices, body(): inter = lax.ppermute(inter, 'tile', across + [(j, i) for i, j in across])  9.5 us
    ppermute x9, waiting for transfers between devices, stage(): lax.ppermute(total, 'tile', [(i, i ^ flip) for i in range(tiles)])  4.49 us
    pallas_call x1, Pallas kernels, body(): pl.pallas_call(wide_kernel, out_shape=(held(FREQS, 2, 3, SLAB, WIDTH, HAL...  4.02 us
    unnamed x28, local copies, waits for them, and re-layouts  3.64 us
  transfers between devices with their start and end apart: 14, of which 5 were waited for; matrix products, arithmetic and copies ran while one was open for 0% of the time, Pallas kernels for 7%

profile of v4, /device:TPU:8, one launch (start us, length us, event | category | flops | bytes accessed | tf_op | source)
XLA Modules:
  0.0 118.9 jit_solution(12786734146810154049)
XLA Ops:
  1.3 0.1 pad_add_fusion.info
  1.4 0.7 copy-done.6
  2.0 20.8 %free.1 = (f32[16,4,2,8,128]{4,3,2,1,0:T(8,128)}, f32[40,4,2,8,128]{4,3,2,1,0:T(8,128)}, f32[40,4,2,8,128]{4,3,2,1,0:T(8,128)}) custom-call(s32[3]{0:T(128)S(1)} %pad_add_fusion.info, f32[4]{0:T(128)S(1)} %copy-done.6, s32[64,16]{1,0:T(8,128)} %bitcast.50, s32[64,16]{1,0:T(8,128)} %bitcast.45, f32[16,64,128]{2,1,0:T(8,128)} %bitcast.48, ...), custom_call_target="tpu_custom_call" | custom-call | tf_op jit(solution)/shard_map/free/pallas_call | solution.py:440
  22.8 1.9 %collective-permute-start = (f32[40,4,2,8,128]{4,3,2,1,0:T(8,128)}, f32[40,4,2,8,128]{4,3,2,1,0:T(8,128)S(1)}, u32[]{:S(2)}, u32[]{:S(2)}) collective-permute-start(f32[40,4,2,8,128]{4,3,2,1,0:T(8,128)} %get-tuple-element.35), channel_id=1, source_target_pairs={{1,2},{3,4},{5,6},{7,8},{9,10},{11,12},{13,14},{15,16},{17,18},{19... | collective-permute-start | bytes 3932168 | tf_op jit(solution)/shard_map/ppermute | solution.py:464
  24.7 1.8 %collective-permute-start.1 = (f32[40,4,2,8,128]{4,3,2,1,0:T(8,128)}, f32[40,4,2,8,128]{4,3,2,1,0:T(8,128)S(1)}, u32[]{:S(2)}, u32[]{:S(2)}) collective-permute-start(f32[40,4,2,8,128]{4,3,2,1,0:T(8,128)} %get-tuple-element.36), channel_id=1, source_target_pairs={{0,1},{1,0},{2,3},{3,2},{4,5},{5,4},{6,7},{7,6},{8,9},{9,8},{10,11... | collective-permute-start | bytes 3932168 | tf_op jit(solution)/shard_map/ppermute | solution.py:465
  26.5 0.0 copy-done
  26.5 0.0 copy-done.1
  26.5 0.0 copy-done.4
  26.5 0.0 copy-done.5
  26.5 0.0 copy-start.2
  26.5 1.9 %copy-done.2 = bf16[1,2,2,3,16,4,2048]{6,5,4,3,2,1,0:T(4,128)(2,1)S(1)} copy-done((bf16[1,2,2,3,16,4,2048]{6,5,4,3,2,1,0:T(4,128)(2,1)S(1)}, bf16[1,2,2,3,16,4,2048]{6,5,4,3,2,1,0:T(4,128)(2,1)}, u32[]{:S(2)}) %copy-start.2) | copy-done | bytes 3145752
  28.4 4.0 %wide.1 = (f32[2,2,3,4,16,2,8,128]{7,6,5,4,3,2,1,0:T(8,128)S(1)}, f32[64,128]{1,0:T(8,128)S(1)}, f32[3,16,4,2,8,128]{5,4,3,2,1,0:T(8,128)S(1)}, f32[3,16,4,2,8,128]{5,4,3,2,1,0:T(8,128)S(1)}) custom-call(bf16[2,2,3,16,64,128]{5,4,3,2,1,0:T(8,128)(2,1)S(1)} %bitcast.44, s32[64,16]{1,0:T(8,128)S(1)} %bitcast.46, f32[64,128]{1,0:T(8,128)S(1)} %bitcast.47, ...), custom_call_target="tpu_custom_call" | custom-call | tf_op jit(solution)/shard_map/wide/pallas_call | solution.py:468
  32.4 9.5 %collective-permute-done.inter = f32[40,4,2,8,128]{4,3,2,1,0:T(8,128)S(1)} collective-permute-done((f32[40,4,2,8,128]{4,3,2,1,0:T(8,128)}, f32[40,4,2,8,128]{4,3,2,1,0:T(8,128)S(1)}, u32[]{:S(2)}, u32[]{:S(2)}) %collective-permute-start) | collective-permute-done | bytes 1310752 | tf_op jit(solution)/shard_map/ppermute | solution.py:464
  41.9 0.0 collective-permute-done.1.intra
  41.9 1.1 copy-done.7
  43.0 0.0 copy-done.3
  43.0 41.5 %steps.1 = (f32[3,17,4,2,8,128]{5,4,3,2,1,0:T(8,128)S(1)}, f32[3,17,4,2,8,128]{5,4,3,2,1,0:T(8,128)S(1)}, f32[4,128]{1,0:T(4,128)S(1)}, f32[16,2,8,128]{3,2,1,0:...) custom-call(s32[3]{0:T(128)S(1)} %pad_add_fusion.info, ...), custom_call_target="tpu_custom_call" | custom-call | tf_op jit(solution)/shard_map/steps/pallas_call | solution.py:481
  84.5 1.7 %collective-permute-start.4 = (f32[4,128]{1,0:T(4,128)S(1)}, f32[4,128]{1,0:T(4,128)S(1)}, u32[]{:S(2)}, u32[]{:S(2)}) collective-permute-start(f32[4,128]{1,0:T(4,128)S(1)} %get-tuple-element.39.refs_0_), channel_id=1, source_target_pairs={{0,9},{1,8},{2,11},{3,10},{4,13},{5,12},{6,15},{7,14},{8,1},{9,0},... | collective-permute-start | bytes 6152 | tf_op jit(solution)/shard_map/ppermute | solution.py:507
  86.2 0.4 collective-permute-start.3
  86.6 0.0 collective-permute-start.2
  86.6 2.3 %out.1 = (f32[3,16,64,128]{3,2,1,0:T(8,128)}, f32[3,16,64,128]{3,2,1,0:T(8,128)}) custom-call(f32[3,17,4,2,8,128]{5,4,3,2,1,0:T(8,128)S(1)} %get-tuple-element.40.e, f32[3,17,4,2,8,128]{5,4,3,2,1,0:T(8,128)S(1)} %get-tuple-element.41.h), custom_call_target="tpu_custom_call" | custom-call | tf_op jit(solution)/shard_map/out/pallas_call | solution.py:517
  88.9 0.0 collective-permute-done.4.refs_3_
  88.9 1.0 collective-permute-done.3.refs_2_
  89.8 0.0 collective-permute-done.2.refs_1_
  89.8 3.3 %collective-permute-start.8 = (f32[16,2,8,128]{3,2,1,0:T(8,128)S(1)}, f32[16,2,8,128]{3,2,1,0:T(8,128)S(1)}, u32[]{:S(2)}, u32[]{:S(2)}) collective-permute-start(f32[16,2,8,128]{3,2,1,0:T(8,128)S(1)} %copy-done.13), channel_id=1, source_target_pairs={{0,64},{64,128},{128,192},{192,0},{1,65},{65,129},{129,193},{193,1... | collective-permute-start | bytes 393224 | tf_op jit(solution)/shard_map/ppermute | solution.py:501
  93.2 4.5 %collective-permute-start.9 = (f32[16,2,8,128]{3,2,1,0:T(8,128)S(1)}, f32[16,2,8,128]{3,2,1,0:T(8,128)S(1)}, u32[]{:S(2)}, u32[]{:S(2)}) collective-permute-start(f32[16,2,8,128]{3,2,1,0:T(8,128)S(1)} %copy-done.12), channel_id=1, source_target_pairs={{0,128},{64,192},{128,0},{192,64},{1,129},{65,193},{129,1},{193,65... | collective-permute-start | bytes 393224 | tf_op jit(solution)/shard_map/ppermute | solution.py:501
  97.7 2.7 %collective-permute-start.10 = (f32[16,2,8,128]{3,2,1,0:T(8,128)S(1)}, f32[16,2,8,128]{3,2,1,0:T(8,128)S(1)}, u32[]{:S(2)}, u32[]{:S(2)}) collective-permute-start(f32[16,2,8,128]{3,2,1,0:T(8,128)S(1)} %copy-done.11), channel_id=1, source_target_pairs={{0,192},{64,0},{128,64},{192,128},{1,193},{65,1},{129,65},{193,129... | collective-permute-start | bytes 393224 | tf_op jit(solution)/shard_map/ppermute | solution.py:501
  100.3 1.6 %collective-permute-start.7 = (f32[4,128]{1,0:T(4,128)S(1)}, f32[4,128]{1,0:T(4,128)S(1)}, u32[]{:S(2)}, u32[]{:S(2)}) collective-permute-start(f32[4,128]{1,0:T(4,128)S(1)} %add.8.refs_0_), channel_id=1, source_target_pairs={{0,6},{1,7},{2,4},{3,5},{4,2},{5,3},{6,0},{7,1},{8,14},{9,15},{10,... | collective-permute-start | bytes 6152 | tf_op jit(solution)/shard_map/ppermute | solution.py:507
  101.9 3.4 %collective-permute-start.6 = (f32[4,128]{1,0:T(4,128)S(1)}, f32[4,128]{1,0:T(4,128)S(1)}, u32[]{:S(2)}, u32[]{:S(2)}) collective-permute-start(f32[4,128]{1,0:T(4,128)S(1)} %add.8.refs_0_), channel_id=1, source_target_pairs={{0,4},{1,5},{2,6},{3,7},{4,0},{5,1},{6,2},{7,3},{8,12},{9,13},{10,... | collective-permute-start | bytes 6152 | tf_op jit(solution)/shard_map/ppermute | solution.py:507
  105.3 0.0 collective-permute-done.7.refs_3_
  105.3 2.7 %collective-permute-start.5 = (f32[4,128]{1,0:T(4,128)S(1)}, f32[4,128]{1,0:T(4,128)S(1)}, u32[]{:S(2)}, u32[]{:S(2)}) collective-permute-start(f32[4,128]{1,0:T(4,128)S(1)} %add.8.refs_0_), channel_id=1, source_target_pairs={{0,2},{1,3},{2,0},{3,1},{4,6},{5,7},{6,4},{7,5},{8,10},{9,11},{10,... | collective-permute-start | bytes 6152 | tf_op jit(solution)/shard_map/ppermute | solution.py:507
  108.1 0.0 collective-permute-done.6.refs_2_
  108.1 1.6 %collective-permute-done.5.refs_1_ = f32[4,128]{1,0:T(4,128)S(1)} collective-permute-done((f32[4,128]{1,0:T(4,128)S(1)}, f32[4,128]{1,0:T(4,128)S(1)}, u32[]{:S(2)}, u32[]{:S(2)}) %collective-permute-start.5) | collective-permute-done | bytes 2080 | tf_op jit(solution)/shard_map/ppermute | solution.py:507
  109.6 0.0 collective-permute-done.8.b
  109.6 0.0 copy-start.8
  109.6 0.0 collective-permute-done.9.c
  109.7 0.6 collective-permute-done.10.d
  110.3 2.8 %collective-permute-start.13 = (f32[4,128]{1,0:T(4,128)S(1)}, f32[4,128]{1,0:T(4,128)S(1)}, u32[]{:S(2)}, u32[]{:S(2)}) collective-permute-start(f32[4,128]{1,0:T(4,128)S(1)} %add.9.refs_0_), channel_id=1, source_target_pairs={{0,48},{1,49},{2,50},{3,51},{4,52},{5,53},{6,54},{7,55},{8,56},{9,... | collective-permute-start | bytes 6152 | tf_op jit(solution)/shard_map/ppermute | solution.py:507
  113.0 0.8 collective-permute-start.12
  113.8 0.5 collective-permute-start.11
  114.3 0.0 copy-done.8
  114.4 0.0 copy-done.10
  114.4 1.8 %total.1 = f32[16,16,128]{2,1,0:T(8,128)} custom-call(f32[16,2,8,128]{3,2,1,0:T(8,128)} %get-tuple-element.55.a, f32[16,2,8,128]{3,2,1,0:T(8,128)} %copy-done.8, f32[16,2,8,128]{3,2,1,0:T(8,128)} %copy-done.9, f32[16,2,8,128]{3,2,1,0:T(8,128)} %copy-done.10), custom_call_target="tpu_custom_call" | custom-call | tf_op jit(solution)/shard_map/total/pallas_call | solution.py:532
  116.1 0.0 collective-permute-done.13.refs_3_
  116.1 2.0 %collective-permute-done.12.refs_2_ = f32[4,128]{1,0:T(4,128)S(1)} collective-permute-done((f32[4,128]{1,0:T(4,128)S(1)}, f32[4,128]{1,0:T(4,128)S(1)}, u32[]{:S(2)}, u32[]{:S(2)}) %collective-permute-start.12) | collective-permute-done | bytes 2080 | tf_op jit(solution)/shard_map/ppermute | solution.py:507
  118.1 0.0 collective-permute-done.11.refs_1_
  118.1 0.1 slice_reduce_fusion
  118.2 0.6 reshape_squeeze.15
  (19 shorter events, 0.0 us)
Async XLA Ops:
  1.4 0.7 copy-start.6
  2.0 24.5 %copy-start = (f32[1,3,16,4,2048]{4,3,2,1,0:T(4,128)S(1)}, f32[1,3,16,4,2048]{4,3,2,1,0:T(4,128)}, u32[]{:S(2)}) copy-start(f32[1,3,16,4,2048]{4,3,2,1,0:T(4,128)} %param.9) | copy-start | bytes 4718596
  2.0 24.5 %copy-start.1 = (f32[1,3,16,4,2048]{4,3,2,1,0:T(4,128)S(1)}, f32[1,3,16,4,2048]{4,3,2,1,0:T(4,128)}, u32[]{:S(2)}) copy-start(f32[1,3,16,4,2048]{4,3,2,1,0:T(4,128)} %param.10) | copy-start | bytes 4718596
  2.0 24.5 %copy-start.4 = (s32[16,4,16]{2,1,0:T(4,128)S(1)}, s32[16,4,16]{2,1,0:T(4,128)}, u32[]{:S(2)}) copy-start(s32[16,4,16]{2,1,0:T(4,128)} %param.14) | copy-start | bytes 12292
  2.0 24.5 %copy-start.5 = (f32[4,2048]{1,0:T(4,128)S(1)}, f32[4,2048]{1,0:T(4,128)}, u32[]{:S(2)}) copy-start(f32[4,2048]{1,0:T(4,128)} %param.16) | copy-start | bytes 98308
  22.8 19.1 %collective-permute-start = (f32[40,4,2,8,128]{4,3,2,1,0:T(8,128)}, f32[40,4,2,8,128]{4,3,2,1,0:T(8,128)S(1)}, u32[]{:S(2)}, u32[]{:S(2)}) collective-permute-start(f32[40,4,2,8,128]{4,3,2,1,0:T(8,128)} %get-tuple-element.35), channel_id=1, source_target_pairs={{1,2},{3,4},{5,6},{7,8},{9,10},{11,12},{13,14},{15,16},{17,18},{19... | collective-permute-start | bytes 3932168 | tf_op jit(solution)/shard_map/ppermute | solution.py:464
  24.7 17.2 %collective-permute-start.1 = (f32[40,4,2,8,128]{4,3,2,1,0:T(8,128)}, f32[40,4,2,8,128]{4,3,2,1,0:T(8,128)S(1)}, u32[]{:S(2)}, u32[]{:S(2)}) collective-permute-start(f32[40,4,2,8,128]{4,3,2,1,0:T(8,128)} %get-tuple-element.36), channel_id=1, source_target_pairs={{0,1},{1,0},{2,3},{3,2},{4,5},{5,4},{6,7},{7,6},{8,9},{9,8},{10,11... | collective-permute-start | bytes 3932168 | tf_op jit(solution)/shard_map/ppermute | solution.py:465
  26.5 1.9 %copy-start.2 = (bf16[1,2,2,3,16,4,2048]{6,5,4,3,2,1,0:T(4,128)(2,1)S(1)}, bf16[1,2,2,3,16,4,2048]{6,5,4,3,2,1,0:T(4,128)(2,1)}, u32[]{:S(2)}) copy-start(bf16[1,2,2,3,16,4,2048]{6,5,4,3,2,1,0:T(4,128)(2,1)} %param.11) | copy-start | bytes 9437188
  28.4 14.6 %copy-start.3 = (f32[16,4,2,8,128]{4,3,2,1,0:T(8,128)S(1)}, f32[16,4,2,8,128]{4,3,2,1,0:T(8,128)}, u32[]{:S(2)}) copy-start(f32[16,4,2,8,128]{4,3,2,1,0:T(8,128)} %get-tuple-element.34.coef) | copy-start | bytes 1572868
  41.9 1.1 copy-start.7
  84.5 4.4 %collective-permute-start.4 = (f32[4,128]{1,0:T(4,128)S(1)}, f32[4,128]{1,0:T(4,128)S(1)}, u32[]{:S(2)}, u32[]{:S(2)}) collective-permute-start(f32[4,128]{1,0:T(4,128)S(1)} %get-tuple-element.39.refs_0_), channel_id=1, source_target_pairs={{0,9},{1,8},{2,11},{3,10},{4,13},{5,12},{6,15},{7,14},{8,1},{9,0},... | collective-permute-start | bytes 6152 | tf_op jit(solution)/shard_map/ppermute | solution.py:507
  86.2 3.6 %collective-permute-start.3 = (f32[4,128]{1,0:T(4,128)S(1)}, f32[4,128]{1,0:T(4,128)S(1)}, u32[]{:S(2)}, u32[]{:S(2)}) collective-permute-start(f32[4,128]{1,0:T(4,128)S(1)} %get-tuple-element.39.refs_0_), channel_id=1, source_target_pairs={{0,8},{1,9},{2,10},{3,11},{4,12},{5,13},{6,14},{7,15},{8,0},{9,1},... | collective-permute-start | bytes 6152 | tf_op jit(solution)/shard_map/ppermute | solution.py:507
  86.6 3.2 %collective-permute-start.2 = (f32[4,128]{1,0:T(4,128)S(1)}, f32[4,128]{1,0:T(4,128)S(1)}, u32[]{:S(2)}, u32[]{:S(2)}) collective-permute-start(f32[4,128]{1,0:T(4,128)S(1)} %get-tuple-element.39.refs_0_), channel_id=1, source_target_pairs={{0,1},{1,0},{2,3},{3,2},{4,5},{5,4},{6,7},{7,6},{8,9},{9,8},{10,11... | collective-permute-start | bytes 6152 | tf_op jit(solution)/shard_map/ppermute | solution.py:507
  86.6 3.2 %copy-start.13 = (f32[16,2,8,128]{3,2,1,0:T(8,128)S(1)}, f32[16,2,8,128]{3,2,1,0:T(8,128)}, u32[]{:S(2)}) copy-start(f32[16,2,8,128]{3,2,1,0:T(8,128)} %get-tuple-element.52) | copy-start | bytes 393220
  86.6 6.6 %copy-start.12 = (f32[16,2,8,128]{3,2,1,0:T(8,128)S(1)}, f32[16,2,8,128]{3,2,1,0:T(8,128)}, u32[]{:S(2)}) copy-start(f32[16,2,8,128]{3,2,1,0:T(8,128)} %get-tuple-element.53) | copy-start | bytes 393220
  86.6 11.1 %copy-start.11 = (f32[16,2,8,128]{3,2,1,0:T(8,128)S(1)}, f32[16,2,8,128]{3,2,1,0:T(8,128)}, u32[]{:S(2)}) copy-start(f32[16,2,8,128]{3,2,1,0:T(8,128)} %get-tuple-element.54) | copy-start | bytes 393220
  89.8 19.8 %collective-permute-start.8 = (f32[16,2,8,128]{3,2,1,0:T(8,128)S(1)}, f32[16,2,8,128]{3,2,1,0:T(8,128)S(1)}, u32[]{:S(2)}, u32[]{:S(2)}) collective-permute-start(f32[16,2,8,128]{3,2,1,0:T(8,128)S(1)} %copy-done.13), channel_id=1, source_target_pairs={{0,64},{64,128},{128,192},{192,0},{1,65},{65,129},{129,193},{193,1... | collective-permute-start | bytes 393224 | tf_op jit(solution)/shard_map/ppermute | solution.py:501
  93.2 16.5 %collective-permute-start.9 = (f32[16,2,8,128]{3,2,1,0:T(8,128)S(1)}, f32[16,2,8,128]{3,2,1,0:T(8,128)S(1)}, u32[]{:S(2)}, u32[]{:S(2)}) collective-permute-start(f32[16,2,8,128]{3,2,1,0:T(8,128)S(1)} %copy-done.12), channel_id=1, source_target_pairs={{0,128},{64,192},{128,0},{192,64},{1,129},{65,193},{129,1},{193,65... | collective-permute-start | bytes 393224 | tf_op jit(solution)/shard_map/ppermute | solution.py:501
  97.7 12.6 %collective-permute-start.10 = (f32[16,2,8,128]{3,2,1,0:T(8,128)S(1)}, f32[16,2,8,128]{3,2,1,0:T(8,128)S(1)}, u32[]{:S(2)}, u32[]{:S(2)}) collective-permute-start(f32[16,2,8,128]{3,2,1,0:T(8,128)S(1)} %copy-done.11), channel_id=1, source_target_pairs={{0,192},{64,0},{128,64},{192,128},{1,193},{65,1},{129,65},{193,129... | collective-permute-start | bytes 393224 | tf_op jit(solution)/shard_map/ppermute | solution.py:501
  100.3 5.0 %collective-permute-start.7 = (f32[4,128]{1,0:T(4,128)S(1)}, f32[4,128]{1,0:T(4,128)S(1)}, u32[]{:S(2)}, u32[]{:S(2)}) collective-permute-start(f32[4,128]{1,0:T(4,128)S(1)} %add.8.refs_0_), channel_id=1, source_target_pairs={{0,6},{1,7},{2,4},{3,5},{4,2},{5,3},{6,0},{7,1},{8,14},{9,15},{10,... | collective-permute-start | bytes 6152 | tf_op jit(solution)/shard_map/ppermute | solution.py:507
  101.9 6.1 %collective-permute-start.6 = (f32[4,128]{1,0:T(4,128)S(1)}, f32[4,128]{1,0:T(4,128)S(1)}, u32[]{:S(2)}, u32[]{:S(2)}) collective-permute-start(f32[4,128]{1,0:T(4,128)S(1)} %add.8.refs_0_), channel_id=1, source_target_pairs={{0,4},{1,5},{2,6},{3,7},{4,0},{5,1},{6,2},{7,3},{8,12},{9,13},{10,... | collective-permute-start | bytes 6152 | tf_op jit(solution)/shard_map/ppermute | solution.py:507
  105.3 4.3 %collective-permute-start.5 = (f32[4,128]{1,0:T(4,128)S(1)}, f32[4,128]{1,0:T(4,128)S(1)}, u32[]{:S(2)}, u32[]{:S(2)}) collective-permute-start(f32[4,128]{1,0:T(4,128)S(1)} %add.8.refs_0_), channel_id=1, source_target_pairs={{0,2},{1,3},{2,0},{3,1},{4,6},{5,7},{6,4},{7,5},{8,10},{9,11},{10,... | collective-permute-start | bytes 6152 | tf_op jit(solution)/shard_map/ppermute | solution.py:507
  109.6 4.7 %copy-start.8 = (f32[16,2,8,128]{3,2,1,0:T(8,128)}, f32[16,2,8,128]{3,2,1,0:T(8,128)S(1)}, u32[]{:S(2)}) copy-start(f32[16,2,8,128]{3,2,1,0:T(8,128)S(1)} %collective-permute-done.8.b) | copy-start | bytes 393220
  109.7 4.7 %copy-start.9 = (f32[16,2,8,128]{3,2,1,0:T(8,128)}, f32[16,2,8,128]{3,2,1,0:T(8,128)S(1)}, u32[]{:S(2)}) copy-start(f32[16,2,8,128]{3,2,1,0:T(8,128)S(1)} %collective-permute-done.9.c) | copy-start | bytes 393220
  110.2 4.1 %copy-start.10 = (f32[16,2,8,128]{3,2,1,0:T(8,128)}, f32[16,2,8,128]{3,2,1,0:T(8,128)S(1)}, u32[]{:S(2)}) copy-start(f32[16,2,8,128]{3,2,1,0:T(8,128)S(1)} %collective-permute-done.10.d) | copy-start | bytes 393220
  110.3 5.9 %collective-permute-start.13 = (f32[4,128]{1,0:T(4,128)S(1)}, f32[4,128]{1,0:T(4,128)S(1)}, u32[]{:S(2)}, u32[]{:S(2)}) collective-permute-start(f32[4,128]{1,0:T(4,128)S(1)} %add.9.refs_0_), channel_id=1, source_target_pairs={{0,48},{1,49},{2,50},{3,51},{4,52},{5,53},{6,54},{7,55},{8,56},{9,... | collective-permute-start | bytes 6152 | tf_op jit(solution)/shard_map/ppermute | solution.py:507
  113.0 5.1 %collective-permute-start.12 = (f32[4,128]{1,0:T(4,128)S(1)}, f32[4,128]{1,0:T(4,128)S(1)}, u32[]{:S(2)}, u32[]{:S(2)}) collective-permute-start(f32[4,128]{1,0:T(4,128)S(1)} %add.9.refs_0_), channel_id=1, source_target_pairs={{0,32},{1,33},{2,34},{3,35},{4,36},{5,37},{6,38},{7,39},{8,40},{9,... | collective-permute-start | bytes 6152 | tf_op jit(solution)/shard_map/ppermute | solution.py:507
  113.8 4.3 %collective-permute-start.11 = (f32[4,128]{1,0:T(4,128)S(1)}, f32[4,128]{1,0:T(4,128)S(1)}, u32[]{:S(2)}, u32[]{:S(2)}) collective-permute-start(f32[4,128]{1,0:T(4,128)S(1)} %add.9.refs_0_), channel_id=1, source_target_pairs={{0,16},{1,17},{2,18},{3,19},{4,20},{5,21},{6,22},{7,23},{8,24},{9,... | collective-permute-start | bytes 6152 | tf_op jit(solution)/shard_map/ppermute | solution.py:507

commit v5 on v4

--- a/solution.py
+++ b/solution.py
@@ -130,14 +130,33 @@
     return lax.dot_general(pick, values, (((1,), (1,)), ((), ())), preferred_element_type=jnp.float32)
 
 
+def free_planes(ea, ha, eb, hb, coef):
+    m = masks()
+    half = WIDTH // 2
+
+    def low(x):
+        update_plane(ea.at[:, x], ea.at[:, x + 1], ha.at[:, x + 1], ha.at[:, x], coef.at[x], ea.at[:, x], m)
+
+    def high(x):
+        update_plane(eb.at[:, x], eb.at[:, x + 1], hb.at[:, x + 1], hb.at[:, x], coef.at[half + x], eb.at[:, x], m)
+
+    return low, high
+
+
+def swaps(info, faces, inter_far, intra_far, sems):
+    odd = lax.rem(info[0], 2)
+    return [
+        pltpu.make_async_copy(faces.at[side], far, sems.at[i])
+        for i, (side, far) in enumerate(((odd, inter_far), (1 - odd, intra_far)))
+    ]
+
+
 def free_kernel(
     info, table, mat_far, des_far, dens_far, e_far, h_far,
-    coef_far, inter_far, intra_far,
-    ea, ha, eb, hb, coef, mat, des, dens, e_in, h_in, faces, sems, sent,
+    coef, inter_far, intra_far, ea, ha, eb, hb,
+    mat, des, dens, e_in, h_in, faces, sems, sent,
 ):
-    m = masks()
     to_left, to_right = faces.at[0], faces.at[1]
-    odd = lax.rem(info[0], 2)
     pairs = ((mat_far, mat), (des_far, des), (dens_far, dens), (e_far, e_in), (h_far, h_in))
     fetch = [pltpu.make_async_copy(src, dst, sems.at[i]) for i, (src, dst) in enumerate(pairs)]
     for copy in fetch:
@@ -157,10 +176,8 @@
                 d = jnp.broadcast_to(flag[:, at : at + 1], (8, 128))
                 eps = b + d * dens[x, strided(z, v), :]
                 coef[x, z, v] = (COEF_E * COEF_H) / eps
-    coef_out = pltpu.make_async_copy(coef, coef_far, sent.at[4])
-    coef_out.start()
-    to_left[2 * STEPS :] = coef[:DEPTH]
-    to_right[2 * STEPS :] = coef[WIDTH - DEPTH :]
+    to_left[STEPS:] = coef[:DEPTH]
+    to_right[STEPS:] = coef[WIDTH - DEPTH :]
 
     half = WIDTH // 2
     fetch[3].wait()
@@ -171,24 +188,44 @@
     load_rows(h_in, hb, 1.0 / COEF_H, half, half, 1)
     eb[:, half] = jnp.zeros((3,) + CELLS, jnp.float32)
     ha[:, 0] = jnp.zeros((3,) + CELLS, jnp.float32)
-    to_left[0:2] = ea[1:3, 0]
-
-    def low(x):
-        update_plane(ea.at[:, x], ea.at[:, x + 1], ha.at[:, x + 1], ha.at[:, x], coef.at[x], ea.at[:, x], m)
-
-    def high(x):
-        update_plane(eb.at[:, x], eb.at[:, x + 1], hb.at[:, x + 1], hb.at[:, x], coef.at[half + x], eb.at[:, x], m)
+    low, high = free_planes(ea, ha, eb, hb, coef)
 
     def early(s, _):
+        to_left[pl.ds(2 * s - 2, 2)] = ea[1:3, 0]
         ea[1:3, half] = eb[1:3, 0]
         sweep(half // 4, lambda i: [4 * i + k for k in range(4)], low)
         hb[1:3, 0] = ha[1:3, half]
         sweep(half // 4, lambda i: [4 * i + k for k in range(4)], high)
-        to_left[pl.ds(2 * s, 2)] = ea[1:3, 0]
         to_right[pl.ds(2 * s - 2, 2)] = hb[1:3, half]
         return 0
 
+    lax.fori_loop(1, DEPTH + 1, early, 0)
+    sends = swaps(info, faces, inter_far, intra_far, sent)
+    for copy in sends:
+        copy.start()
+    for copy in sends:
+        copy.wait()
+
+
+def late_kernel(
+    info, coef, ea_in, ha_in, eb_in, hb_in,
+    inter_far, intra_far,
+    ea, ha, eb, hb, faces, sent,
+):
+    to_left, to_right = faces.at[0], faces.at[1]
+    half = WIDTH // 2
+
+    def place(x, _):
+        for comp in range(3):
+            for src, dst in ((ea_in, ea), (ha_in, ha), (eb_in, eb), (hb_in, hb)):
+                dst[comp, x] = src[comp, x]
+        return 0
+
+    lax.fori_loop(0, half + 1, place, 0)
+    low, high = free_planes(ea, ha, eb, hb, coef)
+
     def late(s, _):
+        to_left[pl.ds(2 * (s - DEPTH - 1), 2)] = ea[1:3, 0]
         blocks = (STEPS + 2 - s) // 2
         first = half - 2 * blocks
         sweep(
@@ -196,27 +233,14 @@
             lambda i: [(low, 2 * i), (high, first + 2 * i), (low, 2 * i + 1), (high, first + 2 * i + 1)],
             lambda job: job[0](job[1]),
         )
-
-        @pl.when(s < STEPS)
-        def _():
-            to_left[pl.ds(2 * s, 2)] = ea[1:3, 0]
-
-        to_right[pl.ds(2 * s - 2, 2)] = hb[1:3, half]
-        return 0
-
-    lax.fori_loop(1, DEPTH + 1, early, 0)
-    cut = 2 * DEPTH
-    sends = []
-    for first, count in ((0, cut), (cut, 2 * STEPS + DEPTH - cut)):
-        for side, far in ((odd, inter_far), (1 - odd, intra_far)):
-            part = pl.ds(first, count)
-            sends.append(pltpu.make_async_copy(faces.at[side, part], far.at[part], sent.at[len(sends)]))
-    sends[0].start()
-    sends[1].start()
+        to_right[pl.ds(2 * (s - DEPTH - 1), 2)] = hb[1:3, half]
+        return 0
+
     lax.fori_loop(DEPTH + 1, STEPS + 1, late, 0)
-    sends[2].start()
-    sends[3].start()
-    for copy in sends + [coef_out]:
+    sends = swaps(info, faces, inter_far, intra_far, sent)
+    for copy in sends:
+        copy.start()
+    for copy in sends:
         copy.wait()
 
 
@@ -302,16 +326,21 @@
 
 
 def steps_kernel(
-    scale, info, e_all, h_all, coef, inter, intra, profile, turned,
-    now, h, over, *rest,
+    scale, info, e_all, h_all, coef, inter, intra, late_inter, late_intra, profile,
+    e, now, h, over,
+    el, hl, er, hr, sums, got, sems,
 ):
-    grads_far, (e, el, hl, er, hr, sums, *grads, got, sems) = rest[:SLAB], rest[SLAB:]
     m = masks()
     odd = lax.rem(info[0], 2)
-    fetch = [
-        pltpu.make_async_copy(far, got.at[side], sems.at[SLAB + i])
-        for i, (side, far) in enumerate(((odd, inter), (1 - odd, intra)))
-    ]
+    hist, tail = pl.ds(0, STEPS), pl.ds(STEPS, DEPTH)
+    fetch = []
+    for side, early, late in ((odd, inter, late_inter), (1 - odd, intra, late_intra)):
+        for src, dst in (
+            (early.at[hist], got.at[side, hist]),
+            (early.at[tail], got.at[side, pl.ds(2 * STEPS, DEPTH)]),
+            (late, got.at[side, pl.ds(STEPS, STEPS)]),
+        ):
+            fetch.append(pltpu.make_async_copy(src, dst, sems.at[len(fetch)]))
     for copy in fetch:
         copy.start()
     from_left, from_right = got.at[0], got.at[1]
@@ -378,6 +407,10 @@
             val = sum(turn[t] * profiled[t] for t in range(STEPS))
             val = jnp.sum(jnp.sum(val, axis=0, keepdims=True), axis=1, keepdims=True)
             over[2 * f + q : 2 * f + q + 1, :] = jnp.broadcast_to(val * scale, (1, 128))
+
+
+def finish_kernel(info, e, turned, g0, g1, g2, g3, *scratch):
+    grads_far, (*grads, sems) = (g0, g1, g2, g3), scratch
     copies = []
     for away in (1, 2, 3, 0):
         terms(away, info, e, turned, grads[away])
@@ -434,35 +467,53 @@
 
     e_rows, h_rows = rows(e_start[0]), rows(h_start[0])
     planes = 2 * STEPS + DEPTH
-    sent = pltpu.HBM((planes, *CELLS), jnp.float32)
     half = (3, WIDTH // 2 + 1) + CELLS
+
+    def sent(count):
+        return (pltpu.HBM((count, *CELLS), jnp.float32),) * 2
+
     info = jnp.stack([tile.astype(jnp.int32), port.astype(jnp.int32), port_mode[0]])
-    coef, inter, intra = pl.pallas_call(
+    coef, inter, intra, *state = pl.pallas_call(
         free_kernel,
-        out_shape=(pltpu.HBM((WIDTH, *CELLS), jnp.float32), sent, sent),
+        out_shape=(held(WIDTH, *CELLS),) + sent(STEPS + DEPTH) + (held(*half),) * 4,
         in_specs=[SMEM] * 2 + [FAR] * 5,
-        out_specs=(FAR,) * 3,
-        scratch_shapes=[held(*half)] * 4
-        + [
-            held(WIDTH, *CELLS),
+        out_specs=(VMEM,) + (FAR,) * 2 + (VMEM,) * 4,
+        scratch_shapes=[
             pltpu.VMEM((64, 16), jnp.int32),
             pltpu.VMEM((64, 16), jnp.int32),
             held(WIDTH, 64, 128),
             held(3, WIDTH, 64, 128),
             held(3, WIDTH, 64, 128),
-            held(2, planes, *CELLS),
+            held(2, STEPS + DEPTH, *CELLS),
             pltpu.SemaphoreType.DMA((5,)),
-            pltpu.SemaphoreType.DMA((5,)),
+            pltpu.SemaphoreType.DMA((2,)),
         ],
-        compiler_params=room(14),
+        compiler_params=room(10),
         name="free",
     )(
-        info, eps_table, far(material.reshape(64, 16)), far(design.reshape(64, 16)), far(rows(density)),
+        info, far(eps_table), far(material.reshape(64, 16)), far(design.reshape(64, 16)), far(rows(density)),
         far(e_rows), far(h_rows),
     )
     across = [(i, i + 1) for i in range(1, tiles - 1, 2)]
-    inter = lax.ppermute(inter, "tile", across + [(j, i) for i, j in across])
-    intra = lax.ppermute(intra, "tile", [(i, i ^ 1) for i in range(tiles)])
+
+    def swap(inter, intra):
+        return (
+            lax.ppermute(inter, "tile", across + [(j, i) for i, j in across]),
+            lax.ppermute(intra, "tile", [(i, i ^ 1) for i in range(tiles)]),
+        )
+
+    inter, intra = swap(inter, intra)
+    late_inter, late_intra = pl.pallas_call(
+        late_kernel,
+        out_shape=sent(STEPS),
+        in_specs=[SMEM] + [VMEM] * 5,
+        out_specs=(FAR,) * 2,
+        scratch_shapes=[held(*half)] * 4 + [held(2, STEPS, *CELLS), pltpu.SemaphoreType.DMA((2,))],
+        compiler_params=room(8),
+        name="late",
+    )(info, here(coef), *[here(x) for x in state])
+    blocks, late_inter, late_intra = lax.optimization_barrier((design.reshape(64, 16), late_inter, late_intra))
+    late_inter, late_intra = swap(late_inter, late_intra)
 
     fields = held(3, WIDTH, *CELLS)
     turned, profile, e_all, h_all = pl.pallas_call(
@@ -473,29 +524,37 @@
         scratch_shapes=[held(4 * 3, 64, 128), held(WIDTH, *CELLS)],
         compiler_params=room(4),
         name="wide",
-    )(rows(forward[0]), design.reshape(64, 16), rows(profiles), e_rows, h_rows)
+    )(rows(forward[0]), blocks, rows(profiles), e_rows, h_rows)
 
     scale = 1.0 / math.sqrt(WIDTH * tiles * SLAB * 2048)
     edge = (3, DEPTH + 1) + CELLS
     wider = held(3, WIDTH + 1, *CELLS)
-    e_last, h_last, over, *parts = pl.pallas_call(
+    e_hist, e_last, h_last, over = pl.pallas_call(
         functools.partial(steps_kernel, scale),
-        out_shape=(wider, wider, f32(2 * FREQS, 128)) + (pltpu.HBM((WIDTH, HALF, 8, 128), jnp.float32),) * SLAB,
-        in_specs=[SMEM] + [VMEM] * 3 + [ANY] * 2 + [VMEM] * 2,
-        out_specs=(VMEM,) * 3 + (FAR,) * SLAB,
+        out_shape=(held(STEPS, 3, WIDTH, *CELLS), wider, wider, f32(2 * FREQS, 128)),
+        in_specs=[SMEM] + [VMEM] * 3 + [ANY] * 4 + [VMEM],
+        out_specs=(VMEM,) * 4,
         scratch_shapes=[
-            held(STEPS, 3, WIDTH, *CELLS),
             held(3, DEPTH + 2, *CELLS),
             held(*edge),
             held(*edge),
             held(*edge),
             held(STEPS, HALF, 8, 128),
-        ]
-        + [held(WIDTH, HALF, 8, 128)] * SLAB
-        + [held(2, planes, *CELLS), pltpu.SemaphoreType.DMA((SLAB + 2,))],
-        compiler_params=room(39),
+            held(2, planes, *CELLS),
+            pltpu.SemaphoreType.DMA((6,)),
+        ],
+        compiler_params=room(9),
         name="steps",
-    )(info, here(e_all), here(h_all), coef, inter, intra, profile, here(turned))
+    )(info, here(e_all), here(h_all), here(coef), inter, intra, late_inter, late_intra, profile)
+    parts = pl.pallas_call(
+        finish_kernel,
+        out_shape=(pltpu.HBM((WIDTH, HALF, 8, 128), jnp.float32),) * SLAB,
+        in_specs=[SMEM, VMEM, VMEM],
+        out_specs=(FAR,) * SLAB,
+        scratch_shapes=[held(WIDTH, HALF, 8, 128)] * SLAB + [pltpu.SemaphoreType.DMA((SLAB,))],
+        compiler_params=room(4),
+        name="finish",
+    )(info, here(e_hist), here(turned))
 
     def to_port(x, d):
         return lax.ppermute(x, "port", [(i, (i + d) % ports) for i in range(ports)])
@@ -523,11 +582,11 @@
         name="out",
     )(here(e_last), here(h_last))
     total = stage(over, (1, 8))
-    total, e_out, h_out, *parts = lax.optimization_barrier((total, e_out, h_out, *parts))
+    total, *parts = lax.optimization_barrier((total, *parts))
     for d in range(1, ports):
         parts[d] = to_port(parts[d], d)
     total = stage(total, (2, 4))
-    total, *parts = lax.optimization_barrier((total, *parts))
+    total, e_out, h_out, *parts = lax.optimization_barrier((total, e_out, h_out, *parts))
     total = stage(total, (16, 32))
     gradient = pl.pallas_call(
         sum_kernel,

time: 121 us -> 117 us (0.967)
  waiting for transfers between devices: 14.6 us -> 5.81 us
  starting transfers between devices: 28.1 us -> 33.9 us
  local copies, waits for them, and re-layouts: 4.4 us -> 0.8 us
  Pallas kernels: 70.3 us -> 72.9 us
    ppermute x2 -> x4, waiting for transfers between devices: 9.51 us -> 3.26 us  [the longest x2 3.25 us: swap(): lax.ppermute(inter, 'tile', across + [(j, i) for i, j in across])]
    unnamed x28 -> x16, local copies, waits for them, and re-layouts: 3.64 us -> 0.03 us
    ppermute x2 -> x4, starting transfers between devices: 3.69 us -> 7.08 us  [the longest x2 3.93 us: swap(): lax.ppermute(inter, 'tile', across + [(j, i) for i, j in across])]
    pallas_call x2 -> x4, Pallas kernels: 62.2 us -> 64.9 us  [the longest x1 35.2 us: body(): pl.pallas_call(functools.partial(steps_kernel, scale), out_shape=(held(ST...]
    ppermute x9, waiting for transfers between devices: 4.49 us -> 2.36 us  [stage(): lax.ppermute(total, 'tile', [(i, i ^ flip) for i in range(tiles)])]
    ppermute x9, starting transfers between devices: 13.9 us -> 15.5 us  [stage(): lax.ppermute(total, 'tile', [(i, i ^ flip) for i in range(tiles)])]
  transfers between devices with their start and end apart: 14 -> 16, of which waited for: 5 -> 3; matrix products, arithmetic and copies ran while one was open for 0% -> 0% of each run, Pallas kernels for 7% -> 19%
where the time goes in v5:
time: 117 us; the launch traced here: 115 us
  Pallas kernels  72.9 us (62%)
  starting transfers between devices  33.9 us (29%)
  waiting for transfers between devices  5.81 us (5%)
  between operations  1.44 us (1%)
    pallas_call x1, Pallas kernels, body(): pl.pallas_call(functools.partial(steps_kernel, scale), out_shape=(held(ST...  35.2 us
    ppermute x9, starting transfers between devices, stage(): lax.ppermute(total, 'tile', [(i, i ^ flip) for i in range(tiles)])  15.5 us
    pallas_call x1, Pallas kernels, body(): pl.pallas_call(free_kernel, out_shape=(held(WIDTH, *CELLS),) + sent(STEPS...  15.5 us
    ppermute x3, starting transfers between devices, to_port(): return lax.ppermute(x, 'port', [(i, (i + d) % ports) for i in range(ports)])  11.2 us
    pallas_call x1, Pallas kernels, body(): pl.pallas_call(late_kernel, out_shape=sent(STEPS), in_specs=[SMEM] + [VME...  8.02 us
    pallas_call x1, Pallas kernels, body(): pl.pallas_call(finish_kernel, out_shape=(pltpu.HBM((WIDTH, HALF, 8, 128),...  6.15 us
    pallas_call x1, Pallas kernels, body(): pl.pallas_call(wide_kernel, out_shape=(held(FREQS, 2, 3, SLAB, WIDTH, HAL...  4.03 us
    ppermute x2, starting transfers between devices, swap(): lax.ppermute(inter, 'tile', across + [(j, i) for i, j in across])  3.93 us
  transfers between devices with their start and end apart: 16, of which 3 were waited for; matrix products, arithmetic and copies ran while one was open for 0% of the time, Pallas kernels for 19%

profile of v5, /device:TPU:8, one launch (start us, length us, event | category | flops | bytes accessed | tf_op | source)
XLA Modules:
  0.0 114.9 jit_solution(547818855137922501)
XLA Ops:
  1.3 0.1 pad_add_fusion.info
  1.4 15.5 %free.1 = (f32[16,4,2,8,128]{4,3,2,1,0:T(8,128)S(1)}, f32[24,4,2,8,128]{4,3,2,1,0:T(8,128)}, f32[24,4,2,8,128]{4,3,2,1,0:T(8,128)}, f32[3,9,4,2,8,128]{5,4,3,2,1...) custom-call(s32[3]{0:T(128)S(1)} %pad_add_fusion.info, ...), custom_call_target="tpu_custom_call" | custom-call | tf_op jit(solution)/shard_map/free/pallas_call | solution.py:476
  16.9 1.9 %collective-permute-start = (f32[24,4,2,8,128]{4,3,2,1,0:T(8,128)}, f32[24,4,2,8,128]{4,3,2,1,0:T(8,128)S(1)}, u32[]{:S(2)}, u32[]{:S(2)}) collective-permute-start(f32[24,4,2,8,128]{4,3,2,1,0:T(8,128)} %get-tuple-element.52), channel_id=1, source_target_pairs={{1,2},{3,4},{5,6},{7,8},{9,10},{11,12},{13,14},{15,16},{17,18},{19... | collective-permute-start | bytes 2359304 | tf_op jit(solution)/shard_map/ppermute | solution.py:501
  18.8 1.8 %collective-permute-start.1 = (f32[24,4,2,8,128]{4,3,2,1,0:T(8,128)}, f32[24,4,2,8,128]{4,3,2,1,0:T(8,128)S(1)}, u32[]{:S(2)}, u32[]{:S(2)}) collective-permute-start(f32[24,4,2,8,128]{4,3,2,1,0:T(8,128)} %get-tuple-element.53), channel_id=1, source_target_pairs={{0,1},{1,0},{2,3},{3,2},{4,5},{5,4},{6,7},{7,6},{8,9},{9,8},{10,11... | collective-permute-start | bytes 2359304 | tf_op jit(solution)/shard_map/ppermute | solution.py:502
  20.6 8.0 %late.1 = (f32[16,4,2,8,128]{4,3,2,1,0:T(8,128)}, f32[16,4,2,8,128]{4,3,2,1,0:T(8,128)}) custom-call(s32[3]{0:T(128)S(1)} %pad_add_fusion.info, f32[16,4,2,8,128]{4,3,2,1,0:T(8,128)S(1)} %get-tuple-element.42.coef, f32[3,9,4,2,8,128]{5,4,3,2,1,0:T(8,128)S(1)} %get-tuple-element.43.ea_in, f32[3,9,4,2,8,128]{5,4,3,2,1,0:T(8,128)S(1)} %get-tuple-element.44.ha_in, ...), custom_call_target="tpu_custom_call" | custom-call | tf_op jit(solution)/shard_map/late/pallas_call | solution.py:506
  28.6 2.0 %collective-permute-start.2 = (f32[16,4,2,8,128]{4,3,2,1,0:T(8,128)}, f32[16,4,2,8,128]{4,3,2,1,0:T(8,128)S(1)}, u32[]{:S(2)}, u32[]{:S(2)}) collective-permute-start(f32[16,4,2,8,128]{4,3,2,1,0:T(8,128)} %get-tuple-element.54), channel_id=1, source_target_pairs={{1,2},{3,4},{5,6},{7,8},{9,10},{11,12},{13,14},{15,16},{17,18},{19... | collective-permute-start | bytes 1572872 | tf_op jit(solution)/shard_map/ppermute | solution.py:501
  30.6 1.4 %collective-permute-start.3 = (f32[16,4,2,8,128]{4,3,2,1,0:T(8,128)}, f32[16,4,2,8,128]{4,3,2,1,0:T(8,128)S(1)}, u32[]{:S(2)}, u32[]{:S(2)}) collective-permute-start(f32[16,4,2,8,128]{4,3,2,1,0:T(8,128)} %get-tuple-element.55), channel_id=1, source_target_pairs={{0,1},{1,0},{2,3},{3,2},{4,5},{5,4},{6,7},{7,6},{8,9},{9,8},{10,11... | collective-permute-start | bytes 1572872 | tf_op jit(solution)/shard_map/ppermute | solution.py:502
  32.0 0.0 copy-done.2
  32.0 0.0 copy-done
  32.0 0.0 copy-done.1
  32.0 0.0 copy-done.3
  32.0 4.0 %wide.1 = (f32[2,2,3,4,16,2,8,128]{7,6,5,4,3,2,1,0:T(8,128)S(1)}, f32[64,128]{1,0:T(8,128)S(1)}, f32[3,16,4,2,8,128]{5,4,3,2,1,0:T(8,128)S(1)}, f32[3,16,4,2,8,128]{5,4,3,2,1,0:T(8,128)S(1)}) custom-call(bf16[2,2,3,16,64,128]{5,4,3,2,1,0:T(8,128)(2,1)S(1)} %bitcast.44, s32[64,16]{1,0:T(8,128)S(1)} %bitcast.46, f32[64,128]{1,0:T(8,128)S(1)} %bitcast.47, ...), custom_call_target="tpu_custom_call" | custom-call | tf_op jit(solution)/shard_map/wide/pallas_call | solution.py:519
  36.1 3.3 %collective-permute-done.2.late_inter = f32[16,4,2,8,128]{4,3,2,1,0:T(8,128)S(1)} collective-permute-done((f32[16,4,2,8,128]{4,3,2,1,0:T(8,128)}, f32[16,4,2,8,128]{4,3,2,1,0:T(8,128)S(1)}, u32[]{:S(2)}, u32[]{:S(2)}) %collective-permute-start.2) | collective-permute-done | bytes 524320 | tf_op jit(solution)/shard_map/ppermute | solution.py:501
  39.3 0.0 collective-permute-done.3.late_intra
  39.3 0.0 collective-permute-done.inter
  39.3 0.0 collective-permute-done.1.intra
  39.3 35.2 %steps.1 = (f32[16,3,16,4,2,8,128]{6,5,4,3,2,1,0:T(8,128)S(1)}, f32[3,17,4,2,8,128]{5,4,3,2,1,0:T(8,128)S(1)}, f32[3,17,4,2,8,128]{5,4,3,2,1,0:T(8,128)S(1)}, f32[4,128]{1,0:T(4,128)S(1)}) custom-call(s32[3]{0:T(128)S(1)} %pad_add_fusion.info, f32[3,16,4,2,8,128]{5,4,3,2,1,0:T(8,128)S(1)} %get-tuple-element.50.e_all, ...), custom_call_target="tpu_custom_call" | custom-call | tf_op jit(solution)/shard_map/steps/pallas_call | solution.py:532
  74.5 1.7 %collective-permute-start.6 = (f32[4,128]{1,0:T(4,128)S(1)}, f32[4,128]{1,0:T(4,128)S(1)}, u32[]{:S(2)}, u32[]{:S(2)}) collective-permute-start(f32[4,128]{1,0:T(4,128)S(1)} %get-tuple-element.57.refs_0_), channel_id=1, source_target_pairs={{0,9},{1,8},{2,11},{3,10},{4,13},{5,12},{6,15},{7,14},{8,1},{9,0},... | collective-permute-start | bytes 6152 | tf_op jit(solution)/shard_map/ppermute | solution.py:566
  76.2 0.4 collective-permute-start.5
  76.6 0.0 collective-permute-start.4
  76.6 6.2 %finish.1 = (f32[16,2,8,128]{3,2,1,0:T(8,128)}, f32[16,2,8,128]{3,2,1,0:T(8,128)}, f32[16,2,8,128]{3,2,1,0:T(8,128)}, f32[16,2,8,128]{3,2,1,0:T(8,128)}) custom-call(s32[3]{0:T(128)S(1)} %pad_add_fusion.info, f32[16,3,16,4,2,8,128]{6,5,4,3,2,1,0:T(8,128)S(1)} %get-tuple-element.58.e, f32[2,2,3,4,16,2,8,128]{7,6,5,4,3,2,1,0:T(8,128)S(1)} %get-tuple-element.59.turned), custom_call_target="tpu_custom_call" | custom-call | tf_op jit(solution)/shard_map/finish/pallas_call | solution.py:549
  82.8 0.0 collective-permute-done.6.refs_3_
  82.8 0.0 collective-permute-done.5.refs_2_
  82.8 0.0 collective-permute-done.4.refs_1_
  82.8 3.3 %collective-permute-start.10 = (f32[16,2,8,128]{3,2,1,0:T(8,128)}, f32[16,2,8,128]{3,2,1,0:T(8,128)S(1)}, u32[]{:S(2)}, u32[]{:S(2)}) collective-permute-start(f32[16,2,8,128]{3,2,1,0:T(8,128)} %get-tuple-element.70), channel_id=1, source_target_pairs={{0,64},{64,128},{128,192},{192,0},{1,65},{65,129},{129,193},{193,1... | collective-permute-start | bytes 393224 | tf_op jit(solution)/shard_map/ppermute | solution.py:560
  86.2 5.2 %collective-permute-start.11 = (f32[16,2,8,128]{3,2,1,0:T(8,128)}, f32[16,2,8,128]{3,2,1,0:T(8,128)S(1)}, u32[]{:S(2)}, u32[]{:S(2)}) collective-permute-start(f32[16,2,8,128]{3,2,1,0:T(8,128)} %get-tuple-element.71), channel_id=1, source_target_pairs={{0,128},{64,192},{128,0},{192,64},{1,129},{65,193},{129,1},{193,65... | collective-permute-start | bytes 393224 | tf_op jit(solution)/shard_map/ppermute | solution.py:560
  91.4 2.7 %collective-permute-start.12 = (f32[16,2,8,128]{3,2,1,0:T(8,128)}, f32[16,2,8,128]{3,2,1,0:T(8,128)S(1)}, u32[]{:S(2)}, u32[]{:S(2)}) collective-permute-start(f32[16,2,8,128]{3,2,1,0:T(8,128)} %get-tuple-element.72), channel_id=1, source_target_pairs={{0,192},{64,0},{128,64},{192,128},{1,193},{65,1},{129,65},{193,129... | collective-permute-start | bytes 393224 | tf_op jit(solution)/shard_map/ppermute | solution.py:560
  94.1 1.3 %collective-permute-start.9 = (f32[4,128]{1,0:T(4,128)S(1)}, f32[4,128]{1,0:T(4,128)S(1)}, u32[]{:S(2)}, u32[]{:S(2)}) collective-permute-start(f32[4,128]{1,0:T(4,128)S(1)} %add.8.refs_0_), channel_id=1, source_target_pairs={{0,6},{1,7},{2,4},{3,5},{4,2},{5,3},{6,0},{7,1},{8,14},{9,15},{10,... | collective-permute-start | bytes 6152 | tf_op jit(solution)/shard_map/ppermute | solution.py:566
  95.4 3.9 %collective-permute-start.8 = (f32[4,128]{1,0:T(4,128)S(1)}, f32[4,128]{1,0:T(4,128)S(1)}, u32[]{:S(2)}, u32[]{:S(2)}) collective-permute-start(f32[4,128]{1,0:T(4,128)S(1)} %add.8.refs_0_), channel_id=1, source_target_pairs={{0,4},{1,5},{2,6},{3,7},{4,0},{5,1},{6,2},{7,3},{8,12},{9,13},{10,... | collective-permute-start | bytes 6152 | tf_op jit(solution)/shard_map/ppermute | solution.py:566
  99.2 0.0 collective-permute-done.9.refs_3_
  99.2 2.7 %collective-permute-start.7 = (f32[4,128]{1,0:T(4,128)S(1)}, f32[4,128]{1,0:T(4,128)S(1)}, u32[]{:S(2)}, u32[]{:S(2)}) collective-permute-start(f32[4,128]{1,0:T(4,128)S(1)} %add.8.refs_0_), channel_id=1, source_target_pairs={{0,2},{1,3},{2,0},{3,1},{4,6},{5,7},{6,4},{7,5},{8,10},{9,11},{10,... | collective-permute-start | bytes 6152 | tf_op jit(solution)/shard_map/ppermute | solution.py:566
  102.0 2.3 %out.1 = (f32[3,16,64,128]{3,2,1,0:T(8,128)}, f32[3,16,64,128]{3,2,1,0:T(8,128)}) custom-call(f32[3,17,4,2,8,128]{5,4,3,2,1,0:T(8,128)S(1)} %get-tuple-element.65.e, f32[3,17,4,2,8,128]{5,4,3,2,1,0:T(8,128)S(1)} %get-tuple-element.66.h), custom_call_target="tpu_custom_call" | custom-call | tf_op jit(solution)/shard_map/out/pallas_call | solution.py:576
  104.2 0.0 collective-permute-done.8.refs_2_
  104.2 0.0 collective-permute-done.7.refs_1_
  104.2 0.0 collective-permute-done.10.b
  104.3 0.0 collective-permute-done.11.c
  104.3 0.2 collective-permute-done.12.d
  104.5 4.6 %collective-permute-start.15 = (f32[4,128]{1,0:T(4,128)S(1)}, f32[4,128]{1,0:T(4,128)S(1)}, u32[]{:S(2)}, u32[]{:S(2)}) collective-permute-start(f32[4,128]{1,0:T(4,128)S(1)} %add.9.refs_0_), channel_id=1, source_target_pairs={{0,48},{1,49},{2,50},{3,51},{4,52},{5,53},{6,54},{7,55},{8,56},{9,... | collective-permute-start | bytes 6152 | tf_op jit(solution)/shard_map/ppermute | solution.py:566
  109.0 0.5 collective-permute-start.14
  109.5 0.5 collective-permute-start.13
  110.0 0.0 copy-done.5
  110.0 0.0 copy-done.7
  110.0 1.8 %total.1 = f32[16,16,128]{2,1,0:T(8,128)} custom-call(f32[16,2,8,128]{3,2,1,0:T(8,128)} %get-tuple-element.75.a, f32[16,2,8,128]{3,2,1,0:T(8,128)} %copy-done.5, f32[16,2,8,128]{3,2,1,0:T(8,128)} %copy-done.6, f32[16,2,8,128]{3,2,1,0:T(8,128)} %copy-done.7), custom_call_target="tpu_custom_call" | custom-call | tf_op jit(solution)/shard_map/total/pallas_call | solution.py:591
  111.8 0.0 collective-permute-done.15.refs_3_
  111.8 2.3 %collective-permute-done.14.refs_2_ = f32[4,128]{1,0:T(4,128)S(1)} collective-permute-done((f32[4,128]{1,0:T(4,128)S(1)}, f32[4,128]{1,0:T(4,128)S(1)}, u32[]{:S(2)}, u32[]{:S(2)}) %collective-permute-start.14) | collective-permute-done | bytes 2080 | tf_op jit(solution)/shard_map/ppermute | solution.py:566
  114.1 0.0 collective-permute-done.13.refs_1_
  114.1 0.1 slice_reduce_fusion
  114.3 0.6 reshape_squeeze.15
  (13 shorter events, 0.0 us)
Async XLA Ops:
  1.4 30.7 %copy-start.2 = (bf16[1,2,2,3,16,4,2048]{6,5,4,3,2,1,0:T(4,128)(2,1)S(1)}, bf16[1,2,2,3,16,4,2048]{6,5,4,3,2,1,0:T(4,128)(2,1)}, u32[]{:S(2)}) copy-start(bf16[1,2,2,3,16,4,2048]{6,5,4,3,2,1,0:T(4,128)(2,1)} %param.11) | copy-start | bytes 9437188
  16.9 22.4 %collective-permute-start = (f32[24,4,2,8,128]{4,3,2,1,0:T(8,128)}, f32[24,4,2,8,128]{4,3,2,1,0:T(8,128)S(1)}, u32[]{:S(2)}, u32[]{:S(2)}) collective-permute-start(f32[24,4,2,8,128]{4,3,2,1,0:T(8,128)} %get-tuple-element.52), channel_id=1, source_target_pairs={{1,2},{3,4},{5,6},{7,8},{9,10},{11,12},{13,14},{15,16},{17,18},{19... | collective-permute-start | bytes 2359304 | tf_op jit(solution)/shard_map/ppermute | solution.py:501
  18.8 20.5 %collective-permute-start.1 = (f32[24,4,2,8,128]{4,3,2,1,0:T(8,128)}, f32[24,4,2,8,128]{4,3,2,1,0:T(8,128)S(1)}, u32[]{:S(2)}, u32[]{:S(2)}) collective-permute-start(f32[24,4,2,8,128]{4,3,2,1,0:T(8,128)} %get-tuple-element.53), channel_id=1, source_target_pairs={{0,1},{1,0},{2,3},{3,2},{4,5},{5,4},{6,7},{7,6},{8,9},{9,8},{10,11... | collective-permute-start | bytes 2359304 | tf_op jit(solution)/shard_map/ppermute | solution.py:502
  20.6 11.4 %copy-start = (f32[1,3,16,4,2048]{4,3,2,1,0:T(4,128)S(1)}, f32[1,3,16,4,2048]{4,3,2,1,0:T(4,128)}, u32[]{:S(2)}) copy-start(f32[1,3,16,4,2048]{4,3,2,1,0:T(4,128)} %param.9) | copy-start | bytes 4718596
  20.6 11.4 %copy-start.1 = (f32[1,3,16,4,2048]{4,3,2,1,0:T(4,128)S(1)}, f32[1,3,16,4,2048]{4,3,2,1,0:T(4,128)}, u32[]{:S(2)}) copy-start(f32[1,3,16,4,2048]{4,3,2,1,0:T(4,128)} %param.10) | copy-start | bytes 4718596
  20.6 11.4 %copy-start.3 = (s32[16,4,16]{2,1,0:T(4,128)S(1)}, s32[16,4,16]{2,1,0:T(4,128)}, u32[]{:S(2)}) copy-start(s32[16,4,16]{2,1,0:T(4,128)} %param.14) | copy-start | bytes 12292
  20.6 11.4 %copy-start.4 = (f32[4,2048]{1,0:T(4,128)S(1)}, f32[4,2048]{1,0:T(4,128)}, u32[]{:S(2)}) copy-start(f32[4,2048]{1,0:T(4,128)} %param.16) | copy-start | bytes 98308
  28.6 10.7 %collective-permute-start.2 = (f32[16,4,2,8,128]{4,3,2,1,0:T(8,128)}, f32[16,4,2,8,128]{4,3,2,1,0:T(8,128)S(1)}, u32[]{:S(2)}, u32[]{:S(2)}) collective-permute-start(f32[16,4,2,8,128]{4,3,2,1,0:T(8,128)} %get-tuple-element.54), channel_id=1, source_target_pairs={{1,2},{3,4},{5,6},{7,8},{9,10},{11,12},{13,14},{15,16},{17,18},{19... | collective-permute-start | bytes 1572872 | tf_op jit(solution)/shard_map/ppermute | solution.py:501
  30.6 8.7 %collective-permute-start.3 = (f32[16,4,2,8,128]{4,3,2,1,0:T(8,128)}, f32[16,4,2,8,128]{4,3,2,1,0:T(8,128)S(1)}, u32[]{:S(2)}, u32[]{:S(2)}) collective-permute-start(f32[16,4,2,8,128]{4,3,2,1,0:T(8,128)} %get-tuple-element.55), channel_id=1, source_target_pairs={{0,1},{1,0},{2,3},{3,2},{4,5},{5,4},{6,7},{7,6},{8,9},{9,8},{10,11... | collective-permute-start | bytes 1572872 | tf_op jit(solution)/shard_map/ppermute | solution.py:502
  74.5 8.3 %collective-permute-start.6 = (f32[4,128]{1,0:T(4,128)S(1)}, f32[4,128]{1,0:T(4,128)S(1)}, u32[]{:S(2)}, u32[]{:S(2)}) collective-permute-start(f32[4,128]{1,0:T(4,128)S(1)} %get-tuple-element.57.refs_0_), channel_id=1, source_target_pairs={{0,9},{1,8},{2,11},{3,10},{4,13},{5,12},{6,15},{7,14},{8,1},{9,0},... | collective-permute-start | bytes 6152 | tf_op jit(solution)/shard_map/ppermute | solution.py:566
  76.2 6.6 %collective-permute-start.5 = (f32[4,128]{1,0:T(4,128)S(1)}, f32[4,128]{1,0:T(4,128)S(1)}, u32[]{:S(2)}, u32[]{:S(2)}) collective-permute-start(f32[4,128]{1,0:T(4,128)S(1)} %get-tuple-element.57.refs_0_), channel_id=1, source_target_pairs={{0,8},{1,9},{2,10},{3,11},{4,12},{5,13},{6,14},{7,15},{8,0},{9,1},... | collective-permute-start | bytes 6152 | tf_op jit(solution)/shard_map/ppermute | solution.py:566
  76.6 6.2 %collective-permute-start.4 = (f32[4,128]{1,0:T(4,128)S(1)}, f32[4,128]{1,0:T(4,128)S(1)}, u32[]{:S(2)}, u32[]{:S(2)}) collective-permute-start(f32[4,128]{1,0:T(4,128)S(1)} %get-tuple-element.57.refs_0_), channel_id=1, source_target_pairs={{0,1},{1,0},{2,3},{3,2},{4,5},{5,4},{6,7},{7,6},{8,9},{9,8},{10,11... | collective-permute-start | bytes 6152 | tf_op jit(solution)/shard_map/ppermute | solution.py:566
  82.8 21.4 %collective-permute-start.10 = (f32[16,2,8,128]{3,2,1,0:T(8,128)}, f32[16,2,8,128]{3,2,1,0:T(8,128)S(1)}, u32[]{:S(2)}, u32[]{:S(2)}) collective-permute-start(f32[16,2,8,128]{3,2,1,0:T(8,128)} %get-tuple-element.70), channel_id=1, source_target_pairs={{0,64},{64,128},{128,192},{192,0},{1,65},{65,129},{129,193},{193,1... | collective-permute-start | bytes 393224 | tf_op jit(solution)/shard_map/ppermute | solution.py:560
  86.2 18.1 %collective-permute-start.11 = (f32[16,2,8,128]{3,2,1,0:T(8,128)}, f32[16,2,8,128]{3,2,1,0:T(8,128)S(1)}, u32[]{:S(2)}, u32[]{:S(2)}) collective-permute-start(f32[16,2,8,128]{3,2,1,0:T(8,128)} %get-tuple-element.71), channel_id=1, source_target_pairs={{0,128},{64,192},{128,0},{192,64},{1,129},{65,193},{129,1},{193,65... | collective-permute-start | bytes 393224 | tf_op jit(solution)/shard_map/ppermute | solution.py:560
  91.4 13.0 %collective-permute-start.12 = (f32[16,2,8,128]{3,2,1,0:T(8,128)}, f32[16,2,8,128]{3,2,1,0:T(8,128)S(1)}, u32[]{:S(2)}, u32[]{:S(2)}) collective-permute-start(f32[16,2,8,128]{3,2,1,0:T(8,128)} %get-tuple-element.72), channel_id=1, source_target_pairs={{0,192},{64,0},{128,64},{192,128},{1,193},{65,1},{129,65},{193,129... | collective-permute-start | bytes 393224 | tf_op jit(solution)/shard_map/ppermute | solution.py:560
  94.1 5.2 %collective-permute-start.9 = (f32[4,128]{1,0:T(4,128)S(1)}, f32[4,128]{1,0:T(4,128)S(1)}, u32[]{:S(2)}, u32[]{:S(2)}) collective-permute-start(f32[4,128]{1,0:T(4,128)S(1)} %add.8.refs_0_), channel_id=1, source_target_pairs={{0,6},{1,7},{2,4},{3,5},{4,2},{5,3},{6,0},{7,1},{8,14},{9,15},{10,... | collective-permute-start | bytes 6152 | tf_op jit(solution)/shard_map/ppermute | solution.py:566
  95.4 8.9 %collective-permute-start.8 = (f32[4,128]{1,0:T(4,128)S(1)}, f32[4,128]{1,0:T(4,128)S(1)}, u32[]{:S(2)}, u32[]{:S(2)}) collective-permute-start(f32[4,128]{1,0:T(4,128)S(1)} %add.8.refs_0_), channel_id=1, source_target_pairs={{0,4},{1,5},{2,6},{3,7},{4,0},{5,1},{6,2},{7,3},{8,12},{9,13},{10,... | collective-permute-start | bytes 6152 | tf_op jit(solution)/shard_map/ppermute | solution.py:566
  99.2 5.0 %collective-permute-start.7 = (f32[4,128]{1,0:T(4,128)S(1)}, f32[4,128]{1,0:T(4,128)S(1)}, u32[]{:S(2)}, u32[]{:S(2)}) collective-permute-start(f32[4,128]{1,0:T(4,128)S(1)} %add.8.refs_0_), channel_id=1, source_target_pairs={{0,2},{1,3},{2,0},{3,1},{4,6},{5,7},{6,4},{7,5},{8,10},{9,11},{10,... | collective-permute-start | bytes 6152 | tf_op jit(solution)/shard_map/ppermute | solution.py:566
  104.2 5.8 %copy-start.5 = (f32[16,2,8,128]{3,2,1,0:T(8,128)}, f32[16,2,8,128]{3,2,1,0:T(8,128)S(1)}, u32[]{:S(2)}) copy-start(f32[16,2,8,128]{3,2,1,0:T(8,128)S(1)} %collective-permute-done.10.b) | copy-start | bytes 393220
  104.3 5.7 %copy-start.6 = (f32[16,2,8,128]{3,2,1,0:T(8,128)}, f32[16,2,8,128]{3,2,1,0:T(8,128)S(1)}, u32[]{:S(2)}) copy-start(f32[16,2,8,128]{3,2,1,0:T(8,128)S(1)} %collective-permute-done.11.c) | copy-start | bytes 393220
  104.5 5.6 %copy-start.7 = (f32[16,2,8,128]{3,2,1,0:T(8,128)}, f32[16,2,8,128]{3,2,1,0:T(8,128)S(1)}, u32[]{:S(2)}) copy-start(f32[16,2,8,128]{3,2,1,0:T(8,128)S(1)} %collective-permute-done.12.d) | copy-start | bytes 393220
  104.5 7.3 %collective-permute-start.15 = (f32[4,128]{1,0:T(4,128)S(1)}, f32[4,128]{1,0:T(4,128)S(1)}, u32[]{:S(2)}, u32[]{:S(2)}) collective-permute-start(f32[4,128]{1,0:T(4,128)S(1)} %add.9.refs_0_), channel_id=1, source_target_pairs={{0,48},{1,49},{2,50},{3,51},{4,52},{5,53},{6,54},{7,55},{8,56},{9,... | collective-permute-start | bytes 6152 | tf_op jit(solution)/shard_map/ppermute | solution.py:566
  109.0 5.1 %collective-permute-start.14 = (f32[4,128]{1,0:T(4,128)S(1)}, f32[4,128]{1,0:T(4,128)S(1)}, u32[]{:S(2)}, u32[]{:S(2)}) collective-permute-start(f32[4,128]{1,0:T(4,128)S(1)} %add.9.refs_0_), channel_id=1, source_target_pairs={{0,32},{1,33},{2,34},{3,35},{4,36},{5,37},{6,38},{7,39},{8,40},{9,... | collective-permute-start | bytes 6152 | tf_op jit(solution)/shard_map/ppermute | solution.py:566
  109.5 4.6 %collective-permute-start.13 = (f32[4,128]{1,0:T(4,128)S(1)}, f32[4,128]{1,0:T(4,128)S(1)}, u32[]{:S(2)}, u32[]{:S(2)}) collective-permute-start(f32[4,128]{1,0:T(4,128)S(1)} %add.9.refs_0_), channel_id=1, source_target_pairs={{0,16},{1,17},{2,18},{3,19},{4,20},{5,21},{6,22},{7,23},{8,24},{9,... | collective-permute-start | bytes 6152 | tf_op jit(solution)/shard_map/ppermute | solution.py:566

commit v6 on v5

--- a/solution.py
+++ b/solution.py
@@ -17,7 +17,8 @@
 WIDTH = 16
 SLAB = 4
 HALF = 2
-DEPTH = STEPS // 2
+ROUND = STEPS // 2
+DEPTH = ROUND // 2
 FREQS = 2
 CELLS = (SLAB, HALF, 8, 128)
 
@@ -130,9 +131,13 @@
     return lax.dot_general(pick, values, (((1,), (1,)), ((), ())), preferred_element_type=jnp.float32)
 
 
-def free_planes(ea, ha, eb, hb, coef):
+def free_run(ea, ha, eb, hb, coef, faces):
     m = masks()
     half = WIDTH // 2
+    to_left, to_right = faces.at[0], faces.at[1]
+    for e, h in ((ea, ha), (eb, hb)):
+        e[:, half] = jnp.zeros((3,) + CELLS, jnp.float32)
+        h[:, 0] = jnp.zeros((3,) + CELLS, jnp.float32)
 
     def low(x):
         update_plane(ea.at[:, x], ea.at[:, x + 1], ha.at[:, x + 1], ha.at[:, x], coef.at[x], ea.at[:, x], m)
@@ -140,7 +145,19 @@
     def high(x):
         update_plane(eb.at[:, x], eb.at[:, x + 1], hb.at[:, x + 1], hb.at[:, x], coef.at[half + x], eb.at[:, x], m)
 
-    return low, high
+    def step(s, _):
+        to_left[pl.ds(2 * s - 2, 2)] = ea[1:3, 0]
+        blocks = (ROUND + 2 - s) // 2
+        first = half - 2 * blocks
+        sweep(
+            blocks,
+            lambda i: [(low, 2 * i), (high, first + 2 * i), (low, 2 * i + 1), (high, first + 2 * i + 1)],
+            lambda job: job[0](job[1]),
+        )
+        to_right[pl.ds(2 * s - 2, 2)] = hb[1:3, half]
+        return 0
+
+    lax.fori_loop(1, ROUND + 1, step, 0)
 
 
 def swaps(info, faces, inter_far, intra_far, sems):
@@ -153,8 +170,8 @@
 
 def free_kernel(
     info, table, mat_far, des_far, dens_far, e_far, h_far,
-    coef, inter_far, intra_far, ea, ha, eb, hb,
-    mat, des, dens, e_in, h_in, faces, sems, sent,
+    coef, inter_far, intra_far,
+    ea, ha, eb, hb, mat, des, dens, e_in, h_in, faces, sems, sent,
 ):
     to_left, to_right = faces.at[0], faces.at[1]
     pairs = ((mat_far, mat), (des_far, des), (dens_far, dens), (e_far, e_in), (h_far, h_in))
@@ -176,8 +193,8 @@
                 d = jnp.broadcast_to(flag[:, at : at + 1], (8, 128))
                 eps = b + d * dens[x, strided(z, v), :]
                 coef[x, z, v] = (COEF_E * COEF_H) / eps
-    to_left[STEPS:] = coef[:DEPTH]
-    to_right[STEPS:] = coef[WIDTH - DEPTH :]
+    to_left[2 * ROUND :] = coef[:DEPTH]
+    to_right[2 * ROUND :] = coef[WIDTH - DEPTH :]
 
     half = WIDTH // 2
     fetch[3].wait()
@@ -186,20 +203,7 @@
     load_rows(e_in, eb, 1.0, half, half)
     load_rows(h_in, ha, 1.0 / COEF_H, 0, half, 1)
     load_rows(h_in, hb, 1.0 / COEF_H, half, half, 1)
-    eb[:, half] = jnp.zeros((3,) + CELLS, jnp.float32)
-    ha[:, 0] = jnp.zeros((3,) + CELLS, jnp.float32)
-    low, high = free_planes(ea, ha, eb, hb, coef)
-
-    def early(s, _):
-        to_left[pl.ds(2 * s - 2, 2)] = ea[1:3, 0]
-        ea[1:3, half] = eb[1:3, 0]
-        sweep(half // 4, lambda i: [4 * i + k for k in range(4)], low)
-        hb[1:3, 0] = ha[1:3, half]
-        sweep(half // 4, lambda i: [4 * i + k for k in range(4)], high)
-        to_right[pl.ds(2 * s - 2, 2)] = hb[1:3, half]
-        return 0
-
-    lax.fori_loop(1, DEPTH + 1, early, 0)
+    free_run(ea, ha, eb, hb, coef, faces)
     sends = swaps(info, faces, inter_far, intra_far, sent)
     for copy in sends:
         copy.start()
@@ -207,46 +211,9 @@
         copy.wait()
 
 
-def late_kernel(
-    info, coef, ea_in, ha_in, eb_in, hb_in,
-    inter_far, intra_far,
-    ea, ha, eb, hb, faces, sent,
-):
-    to_left, to_right = faces.at[0], faces.at[1]
-    half = WIDTH // 2
-
-    def place(x, _):
-        for comp in range(3):
-            for src, dst in ((ea_in, ea), (ha_in, ha), (eb_in, eb), (hb_in, hb)):
-                dst[comp, x] = src[comp, x]
-        return 0
-
-    lax.fori_loop(0, half + 1, place, 0)
-    low, high = free_planes(ea, ha, eb, hb, coef)
-
-    def late(s, _):
-        to_left[pl.ds(2 * (s - DEPTH - 1), 2)] = ea[1:3, 0]
-        blocks = (STEPS + 2 - s) // 2
-        first = half - 2 * blocks
-        sweep(
-            blocks,
-            lambda i: [(low, 2 * i), (high, first + 2 * i), (low, 2 * i + 1), (high, first + 2 * i + 1)],
-            lambda job: job[0](job[1]),
-        )
-        to_right[pl.ds(2 * (s - DEPTH - 1), 2)] = hb[1:3, half]
-        return 0
-
-    lax.fori_loop(DEPTH + 1, STEPS + 1, late, 0)
-    sends = swaps(info, faces, inter_far, intra_far, sent)
-    for copy in sends:
-        copy.start()
-    for copy in sends:
-        copy.wait()
-
-
 def angles():
     omegas = [OMEGA * (f + 1) for f in range(FREQS)]
-    mid = (STEPS + 1) / 2
+    mid = (ROUND + 1) / 2
     return omegas, [float(np.cos(w * mid)) for w in omegas], [float(np.sin(w * mid)) for w in omegas]
 
 
@@ -260,7 +227,7 @@
                 at = x * SLAB + z
                 mask[x, z, v] = jnp.broadcast_to(flag[:, at : at + 1], (8, 128)) * (1.0 / STEPS)
     load_rows(e_in, e_all, 1.0)
-    load_rows(h_in, h_all, 1.0 / COEF_H)
+    load_rows(h_in, h_all, 1.0 / COEF_H, base=1)
 
     def one(x, _):
         for f in range(FREQS):
@@ -284,31 +251,44 @@
     lax.fori_loop(0, WIDTH, one, 0)
 
 
-def terms(away, info, e, turned, grad):
+def terms(e, turned, x, z, v):
     omegas, _, _ = angles()
-    z = lax.rem(info[1] + away, SLAB)
+    total = None
+    for comp in range(3):
+        plus, minus = [], []
+        for i in range(ROUND // 2):
+            lo = e[ROUND // 2 - 1 - i, comp, x, z, v]
+            hi = e[ROUND // 2 + i, comp, x, z, v]
+            plus.append(hi + lo)
+            minus.append(hi - lo)
+        for f in range(FREQS):
+            even = odd = None
+            for i in range(ROUND // 2):
+                c = float(np.cos(omegas[f] * (i + 0.5)))
+                s = float(np.sin(omegas[f] * (i + 0.5)))
+                even = c * plus[i] if even is None else even + c * plus[i]
+                odd = s * minus[i] if odd is None else odd + s * minus[i]
+            term = even * turned[f, 0, comp, z, x, v] + odd * turned[f, 1, comp, z, x, v]
+            total = term if total is None else total + term
+    return total
+
+
+def first_kernel(e, turned, grad, later):
+    omegas, _, _ = angles()
 
     def one(x, _):
-        for v in range(HALF):
-            total = None
-            for comp in range(3):
-                plus, minus = [], []
-                for i in range(STEPS // 2):
-                    lo = e[STEPS // 2 - 1 - i, comp, x, z, v]
-                    hi = e[STEPS // 2 + i, comp, x, z, v]
-                    plus.append(hi + lo)
-                    minus.append(hi - lo)
+        def at_z(z, _):
+            for v in range(HALF):
+                grad[z, x, v] = terms(e, turned, x, z, v)
                 for f in range(FREQS):
-                    even = odd = None
-                    for i in range(STEPS // 2):
-                        c = float(np.cos(omegas[f] * (i + 0.5)))
-                        s = float(np.sin(omegas[f] * (i + 0.5)))
-                        even = c * plus[i] if even is None else even + c * plus[i]
-                        odd = s * minus[i] if odd is None else odd + s * minus[i]
-                    term = even * turned[f, 0, comp, z, x, v] + odd * turned[f, 1, comp, z, x, v]
-                    total = term if total is None else total + term
-            grad[x, v] = total
-        return 0
+                    c, s = float(np.cos(omegas[f] * ROUND)), float(np.sin(omegas[f] * ROUND))
+                    for comp in range(3):
+                        re, im = turned[f, 0, comp, z, x, v], turned[f, 1, comp, z, x, v]
+                        later[f, 0, comp, z, x, v] = c * re + s * im
+                        later[f, 1, comp, z, x, v] = c * im - s * re
+            return 0
+
+        return lax.fori_loop(0, SLAB, at_z, 0)
 
     lax.fori_loop(0, WIDTH, one, 0)
 
@@ -325,30 +305,29 @@
     lax.fori_loop(0, WIDTH, one, 0)
 
 
-def steps_kernel(
-    scale, info, e_all, h_all, coef, inter, intra, late_inter, late_intra, profile,
-    e, now, h, over,
-    el, hl, er, hr, sums, got, sems,
-):
+def round_kernel(final, scale, info, e_in, h_in, coef, inter, intra, *rest):
+    if final:
+        (late_inter, late_intra, profile, sums_before), rest = rest[:4], rest[4:]
+        (e, now, h, over), (el, hl, er, hr, got, sems, sums) = rest[:4], rest[4:]
+    else:
+        (e, now, h, sums, inter_far, intra_far), rest = rest[:6], rest[6:]
+        el, hl, er, hr, got, sems, ea, ha, eb, hb, faces, sent = rest
+        late_inter, late_intra = inter, intra
     m = masks()
     odd = lax.rem(info[0], 2)
-    hist, tail = pl.ds(0, STEPS), pl.ds(STEPS, DEPTH)
+    hist, tail = pl.ds(0, 2 * ROUND), pl.ds(2 * ROUND, DEPTH)
     fetch = []
     for side, early, late in ((odd, inter, late_inter), (1 - odd, intra, late_intra)):
-        for src, dst in (
-            (early.at[hist], got.at[side, hist]),
-            (early.at[tail], got.at[side, pl.ds(2 * STEPS, DEPTH)]),
-            (late, got.at[side, pl.ds(STEPS, STEPS)]),
-        ):
-            fetch.append(pltpu.make_async_copy(src, dst, sems.at[len(fetch)]))
+        for src, part in ((late, hist), (early, tail)):
+            fetch.append(pltpu.make_async_copy(src.at[part], got.at[side, part], sems.at[len(fetch)]))
     for copy in fetch:
         copy.start()
     from_left, from_right = got.at[0], got.at[1]
 
     def place(x, _):
         for comp in range(3):
-            now[comp, x] = e_all[comp, x]
-            h[comp, x + 1] = h_all[comp, x]
+            now[comp, x] = e_in[comp, x]
+            h[comp, x + 1] = h_in[comp, x + 1]
         return 0
 
     lax.fori_loop(0, WIDTH, place, 0)
@@ -360,18 +339,18 @@
     def left(x):
         update_plane(
             el.at[:, x + 1], el.at[:, x + 2], hl.at[:, x + 1], hl.at[:, x],
-            from_left.at[2 * STEPS + x], el.at[:, x + 1], m,
+            from_left.at[2 * ROUND + x], el.at[:, x + 1], m,
         )
 
     def right(x):
         update_plane(
             er.at[:, x], er.at[:, x + 1], hr.at[:, x + 1], hr.at[:, x],
-            from_right.at[2 * STEPS + x], er.at[:, x], m,
+            from_right.at[2 * ROUND + x], er.at[:, x], m,
         )
 
     def halos(s):
         el[1:3, DEPTH + 1] = now[1:3, 0]
-        blocks = (jnp.minimum(s + 1, STEPS - s) + 1) // 2
+        blocks = (jnp.minimum(s + 1, ROUND - s) + 1) // 2
         low = DEPTH - 2 * blocks
         sweep(
             blocks,
@@ -397,23 +376,53 @@
     for copy in fetch:
         copy.wait()
     halos(0)
-    lax.fori_loop(1, STEPS + 1, step, 0)
-
-    omegas = [OMEGA * (f + 1) for f in range(FREQS)]
-    profiled = [sum(sums[t, v] * profile[strided(info[2], v), :] for v in range(HALF)) for t in range(STEPS)]
+    lax.fori_loop(1, ROUND + 1, step, 0)
+
+    if not final:
+        half = WIDTH // 2
+
+        def split(x, _):
+            for comp in range(3):
+                ea[comp, x] = now[comp, x]
+                eb[comp, x] = now[comp, half + x]
+                ha[comp, x + 1] = h[comp, x + 1]
+                hb[comp, x + 1] = h[comp, half + x + 1]
+            return 0
+
+        lax.fori_loop(0, half, split, 0)
+        free_run(ea, ha, eb, hb, coef, faces)
+        sends = swaps(info, faces, inter_far, intra_far, sent)
+        for copy in sends:
+            copy.start()
+        for copy in sends:
+            copy.wait()
+        return
+
+    omegas, _, _ = angles()
+    profiled = [
+        sum(ref[t, v] * profile[strided(info[2], v), :] for v in range(HALF))
+        for ref in (sums_before, sums)
+        for t in range(ROUND)
+    ]
     for f in range(FREQS):
-        for q in range(2):
-            turn = [float(np.cos(omegas[f] * (t + 1))) if q == 0 else -float(np.sin(omegas[f] * (t + 1))) for t in range(STEPS)]
-            val = sum(turn[t] * profiled[t] for t in range(STEPS))
+        for q, turn in enumerate((np.cos, lambda angle: -np.sin(angle))):
+            val = sum(float(turn(omegas[f] * (t + 1))) * profiled[t] for t in range(STEPS))
             val = jnp.sum(jnp.sum(val, axis=0, keepdims=True), axis=1, keepdims=True)
             over[2 * f + q : 2 * f + q + 1, :] = jnp.broadcast_to(val * scale, (1, 128))
 
 
-def finish_kernel(info, e, turned, g0, g1, g2, g3, *scratch):
+def finish_kernel(info, e, turned, before, g0, g1, g2, g3, *scratch):
     grads_far, (*grads, sems) = (g0, g1, g2, g3), scratch
     copies = []
     for away in (1, 2, 3, 0):
-        terms(away, info, e, turned, grads[away])
+        z = lax.rem(info[1] + away, SLAB)
+
+        def one(x, _, grad=grads[away], z=z):
+            for v in range(HALF):
+                grad[x, v] = before[z, x, v] + terms(e, turned, x, z, v)
+            return 0
+
+        lax.fori_loop(0, WIDTH, one, 0)
         copies.append(pltpu.make_async_copy(grads[away], grads_far[away], sems.at[away]))
         copies[-1].start()
     for copy in copies:
@@ -433,6 +442,16 @@
     refs[-1][...] = total
 
 
+def last_kernel(*refs):
+    total = refs[0][...]
+    for ref in refs[1:-1]:
+        total = total + ref[...]
+    lane = lax.broadcasted_iota(jnp.int32, (1, 128), 1)
+    for f in range(FREQS):
+        both = jnp.where(lane == 0, total[2 * f : 2 * f + 1], total[2 * f + 1 : 2 * f + 2])
+        refs[-1][0, f : f + 1, :] = both[:, :2]
+
+
 def f32(*shape):
     return jax.ShapeDtypeStruct(shape, jnp.float32)
 
@@ -466,29 +485,30 @@
     port = lax.axis_index("port")
 
     e_rows, h_rows = rows(e_start[0]), rows(h_start[0])
-    planes = 2 * STEPS + DEPTH
+    planes = 2 * ROUND + DEPTH
     half = (3, WIDTH // 2 + 1) + CELLS
 
     def sent(count):
         return (pltpu.HBM((count, *CELLS), jnp.float32),) * 2
 
     info = jnp.stack([tile.astype(jnp.int32), port.astype(jnp.int32), port_mode[0]])
-    coef, inter, intra, *state = pl.pallas_call(
+    coef, inter, intra = pl.pallas_call(
         free_kernel,
-        out_shape=(held(WIDTH, *CELLS),) + sent(STEPS + DEPTH) + (held(*half),) * 4,
+        out_shape=(f32(WIDTH, *CELLS),) + sent(planes),
         in_specs=[SMEM] * 2 + [FAR] * 5,
-        out_specs=(VMEM,) + (FAR,) * 2 + (VMEM,) * 4,
-        scratch_shapes=[
+        out_specs=(VMEM,) + (FAR,) * 2,
+        scratch_shapes=[held(*half)] * 4
+        + [
             pltpu.VMEM((64, 16), jnp.int32),
             pltpu.VMEM((64, 16), jnp.int32),
             held(WIDTH, 64, 128),
             held(3, WIDTH, 64, 128),
             held(3, WIDTH, 64, 128),
-            held(2, STEPS + DEPTH, *CELLS),
+            held(2, planes, *CELLS),
             pltpu.SemaphoreType.DMA((5,)),
             pltpu.SemaphoreType.DMA((2,)),
         ],
-        compiler_params=room(10),
+        compiler_params=room(12),
         name="free",
     )(
         info, far(eps_table), far(material.reshape(64, 16)), far(design.reshape(64, 16)), far(rows(density)),
@@ -502,23 +522,14 @@
             lax.ppermute(intra, "tile", [(i, i ^ 1) for i in range(tiles)]),
         )
 
+    blocks, inter, intra = lax.optimization_barrier((design.reshape(64, 16), inter, intra))
     inter, intra = swap(inter, intra)
-    late_inter, late_intra = pl.pallas_call(
-        late_kernel,
-        out_shape=sent(STEPS),
-        in_specs=[SMEM] + [VMEM] * 5,
-        out_specs=(FAR,) * 2,
-        scratch_shapes=[held(*half)] * 4 + [held(2, STEPS, *CELLS), pltpu.SemaphoreType.DMA((2,))],
-        compiler_params=room(8),
-        name="late",
-    )(info, here(coef), *[here(x) for x in state])
-    blocks, late_inter, late_intra = lax.optimization_barrier((design.reshape(64, 16), late_inter, late_intra))
-    late_inter, late_intra = swap(late_inter, late_intra)
-
-    fields = held(3, WIDTH, *CELLS)
+
+    fields = held(3, WIDTH + 1, *CELLS)
+    turned_shape = held(FREQS, 2, 3, SLAB, WIDTH, HALF, 8, 128)
     turned, profile, e_all, h_all = pl.pallas_call(
         wide_kernel,
-        out_shape=(held(FREQS, 2, 3, SLAB, WIDTH, HALF, 8, 128), f32(64, 128), fields, fields),
+        out_shape=(turned_shape, f32(64, 128), fields, fields),
         in_specs=[VMEM] * 5,
         out_specs=(VMEM,) * 4,
         scratch_shapes=[held(4 * 3, 64, 128), held(WIDTH, *CELLS)],
@@ -528,45 +539,66 @@
 
     scale = 1.0 / math.sqrt(WIDTH * tiles * SLAB * 2048)
     edge = (3, DEPTH + 1) + CELLS
-    wider = held(3, WIDTH + 1, *CELLS)
-    e_hist, e_last, h_last, over = pl.pallas_call(
-        functools.partial(steps_kernel, scale),
-        out_shape=(held(STEPS, 3, WIDTH, *CELLS), wider, wider, f32(2 * FREQS, 128)),
-        in_specs=[SMEM] + [VMEM] * 3 + [ANY] * 4 + [VMEM],
+    history = held(ROUND, 3, WIDTH, *CELLS)
+    halos = [
+        held(3, DEPTH + 2, *CELLS),
+        held(*edge),
+        held(*edge),
+        held(*edge),
+        held(2, planes, *CELLS),
+        pltpu.SemaphoreType.DMA((4,)),
+    ]
+    e_first, e_mid, h_mid, sums, late_inter, late_intra = pl.pallas_call(
+        functools.partial(round_kernel, False, scale),
+        out_shape=(history, fields, fields, f32(ROUND, HALF, 8, 128)) + sent(2 * ROUND),
+        in_specs=[SMEM] + [VMEM] * 3 + [ANY] * 2,
+        out_specs=(VMEM,) * 4 + (FAR,) * 2,
+        scratch_shapes=halos
+        + [held(*half)] * 4
+        + [held(2, 2 * ROUND, *CELLS), pltpu.SemaphoreType.DMA((2,))],
+        compiler_params=room(12),
+        name="round",
+    )(info, here(e_all), here(h_all), coef, inter, intra)
+    late_inter, late_intra = swap(late_inter, late_intra)
+    grad_first, turned = pl.pallas_call(
+        first_kernel,
+        out_shape=(f32(SLAB, WIDTH, HALF, 8, 128), turned_shape),
+        in_specs=[VMEM] * 2,
+        out_specs=(VMEM,) * 2,
+        compiler_params=room(2),
+        name="first",
+    )(here(e_first), here(turned))
+    sums, grad_first = lax.optimization_barrier((sums, grad_first))
+    e_second, e_last, h_last, over = pl.pallas_call(
+        functools.partial(round_kernel, True, scale),
+        out_shape=(history, fields, fields, f32(2 * FREQS, 128)),
+        in_specs=[SMEM] + [VMEM] * 3 + [ANY] * 4 + [VMEM] * 2,
         out_specs=(VMEM,) * 4,
-        scratch_shapes=[
-            held(3, DEPTH + 2, *CELLS),
-            held(*edge),
-            held(*edge),
-            held(*edge),
-            held(STEPS, HALF, 8, 128),
-            held(2, planes, *CELLS),
-            pltpu.SemaphoreType.DMA((6,)),
-        ],
-        compiler_params=room(9),
-        name="steps",
-    )(info, here(e_all), here(h_all), here(coef), inter, intra, late_inter, late_intra, profile)
+        scratch_shapes=halos + [held(ROUND, HALF, 8, 128)],
+        compiler_params=room(8),
+        name="round",
+    )(info, here(e_mid), here(h_mid), coef, inter, intra, late_inter, late_intra, profile, sums)
     parts = pl.pallas_call(
         finish_kernel,
         out_shape=(pltpu.HBM((WIDTH, HALF, 8, 128), jnp.float32),) * SLAB,
-        in_specs=[SMEM, VMEM, VMEM],
+        in_specs=[SMEM] + [VMEM] * 3,
         out_specs=(FAR,) * SLAB,
         scratch_shapes=[held(WIDTH, HALF, 8, 128)] * SLAB + [pltpu.SemaphoreType.DMA((SLAB,))],
         compiler_params=room(4),
         name="finish",
-    )(info, here(e_hist), here(turned))
+    )(info, here(e_second), here(turned), grad_first)
 
     def to_port(x, d):
         return lax.ppermute(x, "port", [(i, (i + d) % ports) for i in range(ports)])
 
-    def stage(total, steps):
+    def stage(total, steps, kernel=add_kernel, shape=(2 * FREQS, 128)):
         got = []
         for mask in range(1, 1 << len(steps)):
             flip = sum(by for bit, by in enumerate(steps) if mask >> bit & 1)
             got.append(lax.ppermute(total, "tile", [(i, i ^ flip) for i in range(tiles)]))
         return pl.pallas_call(
-            add_kernel,
-            out_shape=f32(*total.shape),
+            kernel,
+            out_shape=f32(*shape),
             in_specs=[VMEM] * (1 + len(got)),
             out_specs=VMEM,
             compiler_params=room(1),
@@ -587,7 +619,7 @@
         parts[d] = to_port(parts[d], d)
     total = stage(total, (2, 4))
     total, e_out, h_out, *parts = lax.optimization_barrier((total, e_out, h_out, *parts))
-    total = stage(total, (16, 32))
+    intersections = stage(total, (16, 32), last_kernel, (1, FREQS, 2))
     gradient = pl.pallas_call(
         sum_kernel,
         out_shape=f32(WIDTH, 16, 128),
@@ -599,7 +631,7 @@
         unrows(e_out)[None],
         unrows(h_out)[None],
         gradient.reshape(WIDTH, 1, 2048),
-        total[:, 0].reshape(1, FREQS, 2),
+        intersections,
     )
 
 

time: 117 us -> 116 us (level)
  Pallas kernels: 72.9 us -> 66.5 us
  waiting for transfers between devices: 5.81 us -> 8.45 us
  starting transfers between devices: 33.9 us -> 35.8 us
    pallas_call x7 -> x8, Pallas kernels: 62.7 us -> 58.3 us  [the longest x1 23.1 us: body(): pl.pallas_call(functools.partial(round_kernel, False, scale), out_shape=(...]
    ppermute x2, waiting for transfers between devices: 3.25 us -> 6.07 us  [swap(): lax.ppermute(inter, 'tile', across + [(j, i) for i, j in across])]
    pallas_call x1, Pallas kernels: 6.15 us -> 4.2 us  [body(): pl.pallas_call(finish_kernel, out_shape=(pltpu.HBM((WIDTH, HALF, 8, 128),...]
    unnamed x16, local copies, waits for them, and re-layouts: 0.03 us -> 1.91 us
    ppermute x9, starting transfers between devices: 15.5 us -> 17.2 us  [stage(): lax.ppermute(total, 'tile', [(i, i ^ flip) for i in range(tiles)])]
  transfers between devices with their start and end apart: 16 -> 16, of which waited for: 3 -> 3; matrix products, arithmetic and copies ran while one was open for 0% -> 0% of each run, Pallas kernels for 19% -> 14%
where the time goes in v6:
time: 116 us; the launch traced here: 114 us
  Pallas kernels  66.5 us (57%)
  starting transfers between devices  35.8 us (31%)
  waiting for transfers between devices  8.45 us (7%)
  local copies, waits for them, and re-layouts  1.91 us (2%)
  between operations  1.46 us (1%)
    pallas_call x1, Pallas kernels, body(): pl.pallas_call(functools.partial(round_kernel, False, scale), out_shape=(...  23.1 us
    ppermute x9, starting transfers between devices, stage(): lax.ppermute(total, 'tile', [(i, i ^ flip) for i in range(tiles)])  17.2 us
    pallas_call x1, Pallas kernels, body(): pl.pallas_call(functools.partial(round_kernel, True, scale), out_shape=(h...  16.1 us
    ppermute x3, starting transfers between devices, to_port(): return lax.ppermute(x, 'port', [(i, (i + d) % ports) for i in range(ports)])  11.2 us
    pallas_call x1, Pallas kernels, body(): pl.pallas_call(free_kernel, out_shape=(f32(WIDTH, *CELLS),) + sent(planes...  11.1 us
    ppermute x2, waiting for transfers between devices, swap(): lax.ppermute(inter, 'tile', across + [(j, i) for i, j in across])  6.07 us
    pallas_call x1, Pallas kernels, body(): pl.pallas_call(finish_kernel, out_shape=(pltpu.HBM((WIDTH, HALF, 8, 128),...  4.2 us
    pallas_call x1, Pallas kernels, body(): pl.pallas_call(wide_kernel, out_shape=(turned_shape, f32(64, 128), fields...  4.02 us
  transfers between devices with their start and end apart: 16, of which 3 were waited for; matrix products, arithmetic and copies ran while one was open for 0% of the time, Pallas kernels for 14%

profile of v6, /device:TPU:8, one launch (start us, length us, event | category | flops | bytes accessed | tf_op | source)
XLA Modules:
  0.0 114.2 jit_solution(3896174820475611915)
XLA Ops:
  1.3 0.1 pad_add_fusion.info
  1.4 11.1 %free.1 = (f32[16,4,2,8,128]{4,3,2,1,0:T(8,128)S(1)}, f32[20,4,2,8,128]{4,3,2,1,0:T(8,128)}, f32[20,4,2,8,128]{4,3,2,1,0:T(8,128)}) custom-call(s32[3]{0:T(128)S(1)} %pad_add_fusion.info, f32[4]{0:T(128)} %table.1, s32[64,16]{1,0:T(8,128)} %bitcast.50, s32[64,16]{1,0:T(8,128)} %bitcast.45, f32[16,64,128]{2,1,0:T(8,128)} %bitcast.48, ...), custom_call_target="tpu_custom_call" | custom-call | tf_op jit(solution)/shard_map/free/pallas_call | solution.py:495
  12.4 1.9 %collective-permute-start = (f32[20,4,2,8,128]{4,3,2,1,0:T(8,128)}, f32[20,4,2,8,128]{4,3,2,1,0:T(8,128)S(1)}, u32[]{:S(2)}, u32[]{:S(2)}) collective-permute-start(f32[20,4,2,8,128]{4,3,2,1,0:T(8,128)} %get-tuple-element.52), channel_id=1, source_target_pairs={{1,2},{3,4},{5,6},{7,8},{9,10},{11,12},{13,14},{15,16},{17,18},{19... | collective-permute-start | bytes 1966088 | tf_op jit(solution)/shard_map/ppermute | solution.py:521
  14.4 1.8 %collective-permute-start.1 = (f32[20,4,2,8,128]{4,3,2,1,0:T(8,128)}, f32[20,4,2,8,128]{4,3,2,1,0:T(8,128)S(1)}, u32[]{:S(2)}, u32[]{:S(2)}) collective-permute-start(f32[20,4,2,8,128]{4,3,2,1,0:T(8,128)} %get-tuple-element.53), channel_id=1, source_target_pairs={{0,1},{1,0},{2,3},{3,2},{4,5},{5,4},{6,7},{7,6},{8,9},{9,8},{10,11... | collective-permute-start | bytes 1966088 | tf_op jit(solution)/shard_map/ppermute | solution.py:522
  16.1 0.0 copy-done
  16.1 0.0 copy-done.1
  16.1 0.0 copy-start.2
  16.2 1.9 %copy-done.2 = bf16[1,2,2,3,16,4,2048]{6,5,4,3,2,1,0:T(4,128)(2,1)S(1)} copy-done((bf16[1,2,2,3,16,4,2048]{6,5,4,3,2,1,0:T(4,128)(2,1)S(1)}, bf16[1,2,2,3,16,4,2048]{6,5,4,3,2,1,0:T(4,128)(2,1)}, u32[]{:S(2)}) %copy-start.2) | copy-done | bytes 3145752
  18.0 4.0 %wide.1 = (f32[2,2,3,4,16,2,8,128]{7,6,5,4,3,2,1,0:T(8,128)S(1)}, f32[64,128]{1,0:T(8,128)S(1)}, f32[3,17,4,2,8,128]{5,4,3,2,1,0:T(8,128)S(1)}, f32[3,17,4,2,8,128]{5,4,3,2,1,0:T(8,128)S(1)}) custom-call(bf16[2,2,3,16,64,128]{5,4,3,2,1,0:T(8,128)(2,1)S(1)} %bitcast.44, s32[64,16]{1,0:T(8,128)S(1)} %bitcast.46, f32[64,128]{1,0:T(8,128)S(1)} %bitcast.47, ...), custom_call_target="tpu_custom_call" | custom-call | tf_op jit(solution)/shard_map/wide/pallas_call | solution.py:530
  22.1 2.5 %collective-permute-done.inter = f32[20,4,2,8,128]{4,3,2,1,0:T(8,128)S(1)} collective-permute-done((f32[20,4,2,8,128]{4,3,2,1,0:T(8,128)}, f32[20,4,2,8,128]{4,3,2,1,0:T(8,128)S(1)}, u32[]{:S(2)}, u32[]{:S(2)}) %collective-permute-start) | collective-permute-done | bytes 655392 | tf_op jit(solution)/shard_map/ppermute | solution.py:521
  24.6 0.0 collective-permute-done.1.intra
  24.6 23.1 %round.2 = (f32[8,3,16,4,2,8,128]{6,5,4,3,2,1,0:T(8,128)S(1)}, f32[3,17,4,2,8,128]{5,4,3,2,1,0:T(8,128)S(1)}, f32[3,17,4,2,8,128]{5,4,3,2,1,0:T(8,128)S(1)}, f32...) custom-call(s32[3]{0:T(128)S(1)} %pad_add_fusion.info, ...), custom_call_target="tpu_custom_call" | custom-call | tf_op jit(solution)/shard_map/round/pallas_call | solution.py:551
  47.7 1.9 %collective-permute-start.2 = (f32[16,4,2,8,128]{4,3,2,1,0:T(8,128)}, f32[16,4,2,8,128]{4,3,2,1,0:T(8,128)S(1)}, u32[]{:S(2)}, u32[]{:S(2)}) collective-permute-start(f32[16,4,2,8,128]{4,3,2,1,0:T(8,128)} %get-tuple-element.56), channel_id=1, source_target_pairs={{1,2},{3,4},{5,6},{7,8},{9,10},{11,12},{13,14},{15,16},{17,18},{19... | collective-permute-start | bytes 1572872 | tf_op jit(solution)/shard_map/ppermute | solution.py:521
  49.6 1.8 %collective-permute-start.3 = (f32[16,4,2,8,128]{4,3,2,1,0:T(8,128)}, f32[16,4,2,8,128]{4,3,2,1,0:T(8,128)S(1)}, u32[]{:S(2)}, u32[]{:S(2)}) collective-permute-start(f32[16,4,2,8,128]{4,3,2,1,0:T(8,128)} %get-tuple-element.57), channel_id=1, source_target_pairs={{0,1},{1,0},{2,3},{3,2},{4,5},{5,4},{6,7},{7,6},{8,9},{9,8},{10,11... | collective-permute-start | bytes 1572872 | tf_op jit(solution)/shard_map/ppermute | solution.py:522
  51.4 3.4 %first.1 = (f32[4,16,2,8,128]{4,3,2,1,0:T(8,128)S(1)}, f32[2,2,3,4,16,2,8,128]{7,6,5,4,3,2,1,0:T(8,128)S(1)}) custom-call(f32[8,3,16,4,2,8,128]{6,5,4,3,2,1,0:T(8,128)S(1)} %get-tuple-element.60.e, f32[2,2,3,4,16,2,8,128]{7,6,5,4,3,2,1,0:T(8,128)S(1)} %get-tuple-element.61.turned), custom_call_target="tpu_custom_call" | custom-call | tf_op jit(solution)/shard_map/first/pallas_call | solution.py:563
  54.8 3.6 %collective-permute-done.2.rest_0_ = f32[16,4,2,8,128]{4,3,2,1,0:T(8,128)S(1)} collective-permute-done((f32[16,4,2,8,128]{4,3,2,1,0:T(8,128)}, f32[16,4,2,8,128]{4,3,2,1,0:T(8,128)S(1)}, u32[]{:S(2)}, u32[]{:S(2)}) %collective-permute-start.2) | collective-permute-done | bytes 524320 | tf_op jit(solution)/shard_map/ppermute | solution.py:521
  58.4 0.0 collective-permute-done.3.rest_1_
  58.4 16.1 %round.3 = (f32[8,3,16,4,2,8,128]{6,5,4,3,2,1,0:T(8,128)S(1)}, f32[3,17,4,2,8,128]{5,4,3,2,1,0:T(8,128)S(1)}, f32[3,17,4,2,8,128]{5,4,3,2,1,0:T(8,128)S(1)}, f32[4,128]{1,0:T(4,128)S(1)}) custom-call(s32[3]{0:T(128)S(1)} %pad_add_fusion.info, f32[3,17,4,2,8,128]{5,4,3,2,1,0:T(8,128)S(1)} %get-tuple-element.54.e_in, ...), custom_call_target="tpu_custom_call" | custom-call | tf_op jit(solution)/shard_map/round/pallas_call | solution.py:572
  74.5 1.7 %collective-permute-start.6 = (f32[4,128]{1,0:T(4,128)S(1)}, f32[4,128]{1,0:T(4,128)S(1)}, u32[]{:S(2)}, u32[]{:S(2)}) collective-permute-start(f32[4,128]{1,0:T(4,128)S(1)} %get-tuple-element.64.refs_0_), channel_id=1, source_target_pairs={{0,9},{1,8},{2,11},{3,10},{4,13},{5,12},{6,15},{7,14},{8,1},{9,0},... | collective-permute-start | bytes 6152 | tf_op jit(solution)/shard_map/ppermute | solution.py:598
  76.2 0.4 collective-permute-start.5
  76.6 0.0 collective-permute-start.4
  76.6 4.2 %finish.1 = (f32[16,2,8,128]{3,2,1,0:T(8,128)}, f32[16,2,8,128]{3,2,1,0:T(8,128)}, f32[16,2,8,128]{3,2,1,0:T(8,128)}, f32[16,2,8,128]{3,2,1,0:T(8,128)}) custom-call(s32[3]{0:T(128)S(1)} %pad_add_fusion.info, f32[8,3,16,4,2,8,128]{6,5,4,3,2,1,0:T(8,128)S(1)} %get-tuple-element.65.e, f32[2,2,3,4,16,2,8,128]{7,6,5,4,3,2,1,0:T(8,128)S(1)} %get-tuple-element.66.turned, ...), custom_call_target="tpu_custom_call" | custom-call | tf_op jit(solution)/shard_map/finish/pallas_call | solution.py:581
  80.8 0.0 collective-permute-done.6.refs_3_
  80.8 0.0 collective-permute-done.5.refs_2_
  80.8 0.0 collective-permute-done.4.refs_1_
  80.8 3.3 %collective-permute-start.10 = (f32[16,2,8,128]{3,2,1,0:T(8,128)}, f32[16,2,8,128]{3,2,1,0:T(8,128)S(1)}, u32[]{:S(2)}, u32[]{:S(2)}) collective-permute-start(f32[16,2,8,128]{3,2,1,0:T(8,128)} %get-tuple-element.78), channel_id=1, source_target_pairs={{0,64},{64,128},{128,192},{192,0},{1,65},{65,129},{129,193},{193,1... | collective-permute-start | bytes 393224 | tf_op jit(solution)/shard_map/ppermute | solution.py:592
  84.2 5.2 %collective-permute-start.11 = (f32[16,2,8,128]{3,2,1,0:T(8,128)}, f32[16,2,8,128]{3,2,1,0:T(8,128)S(1)}, u32[]{:S(2)}, u32[]{:S(2)}) collective-permute-start(f32[16,2,8,128]{3,2,1,0:T(8,128)} %get-tuple-element.79), channel_id=1, source_target_pairs={{0,128},{64,192},{128,0},{192,64},{1,129},{65,193},{129,1},{193,65... | collective-permute-start | bytes 393224 | tf_op jit(solution)/shard_map/ppermute | solution.py:592
  89.4 2.7 %collective-permute-start.12 = (f32[16,2,8,128]{3,2,1,0:T(8,128)}, f32[16,2,8,128]{3,2,1,0:T(8,128)S(1)}, u32[]{:S(2)}, u32[]{:S(2)}) collective-permute-start(f32[16,2,8,128]{3,2,1,0:T(8,128)} %get-tuple-element.80), channel_id=1, source_target_pairs={{0,192},{64,0},{128,64},{192,128},{1,193},{65,1},{129,65},{193,129... | collective-permute-start | bytes 393224 | tf_op jit(solution)/shard_map/ppermute | solution.py:592
  92.1 1.6 %collective-permute-start.9 = (f32[4,128]{1,0:T(4,128)S(1)}, f32[4,128]{1,0:T(4,128)S(1)}, u32[]{:S(2)}, u32[]{:S(2)}) collective-permute-start(f32[4,128]{1,0:T(4,128)S(1)} %add.7.refs_0_), channel_id=1, source_target_pairs={{0,6},{1,7},{2,4},{3,5},{4,2},{5,3},{6,0},{7,1},{8,14},{9,15},{10,... | collective-permute-start | bytes 6152 | tf_op jit(solution)/shard_map/ppermute | solution.py:598
  93.6 5.5 %collective-permute-start.8 = (f32[4,128]{1,0:T(4,128)S(1)}, f32[4,128]{1,0:T(4,128)S(1)}, u32[]{:S(2)}, u32[]{:S(2)}) collective-permute-start(f32[4,128]{1,0:T(4,128)S(1)} %add.7.refs_0_), channel_id=1, source_target_pairs={{0,4},{1,5},{2,6},{3,7},{4,0},{5,1},{6,2},{7,3},{8,12},{9,13},{10,... | collective-permute-start | bytes 6152 | tf_op jit(solution)/shard_map/ppermute | solution.py:598
  99.2 0.0 collective-permute-done.9.refs_3_
  99.2 2.7 %collective-permute-start.7 = (f32[4,128]{1,0:T(4,128)S(1)}, f32[4,128]{1,0:T(4,128)S(1)}, u32[]{:S(2)}, u32[]{:S(2)}) collective-permute-start(f32[4,128]{1,0:T(4,128)S(1)} %add.7.refs_0_), channel_id=1, source_target_pairs={{0,2},{1,3},{2,0},{3,1},{4,6},{5,7},{6,4},{7,5},{8,10},{9,11},{10,... | collective-permute-start | bytes 6152 | tf_op jit(solution)/shard_map/ppermute | solution.py:598
  101.9 2.3 %out.1 = (f32[3,16,64,128]{3,2,1,0:T(8,128)}, f32[3,16,64,128]{3,2,1,0:T(8,128)}) custom-call(f32[3,17,4,2,8,128]{5,4,3,2,1,0:T(8,128)S(1)} %get-tuple-element.73.e, f32[3,17,4,2,8,128]{5,4,3,2,1,0:T(8,128)S(1)} %get-tuple-element.74.h), custom_call_target="tpu_custom_call" | custom-call | tf_op jit(solution)/shard_map/out/pallas_call | solution.py:608
  104.2 0.0 collective-permute-done.8.refs_2_
  104.2 0.0 collective-permute-done.7.refs_1_
  104.2 0.0 collective-permute-done.10.b
  104.2 0.0 collective-permute-done.11.c
  104.2 0.0 collective-permute-done.12.d
  104.2 0.0 copy-start.7
  104.3 4.3 %collective-permute-start.15 = (f32[4,128]{1,0:T(4,128)S(1)}, f32[4,128]{1,0:T(4,128)S(1)}, u32[]{:S(2)}, u32[]{:S(2)}) collective-permute-start(f32[4,128]{1,0:T(4,128)S(1)} %add.8.refs_0_), channel_id=1, source_target_pairs={{0,48},{1,49},{2,50},{3,51},{4,52},{5,53},{6,54},{7,55},{8,56},{9,... | collective-permute-start | bytes 6152 | tf_op jit(solution)/shard_map/ppermute | solution.py:598
  108.5 0.8 collective-permute-start.14
  109.3 0.2 collective-permute-start.13
  109.5 0.0 copy-done.6
  109.5 1.8 %total.1 = f32[16,16,128]{2,1,0:T(8,128)} custom-call(f32[16,2,8,128]{3,2,1,0:T(8,128)} %get-tuple-element.83.a, f32[16,2,8,128]{3,2,1,0:T(8,128)} %copy-done.5, f32[16,2,8,128]{3,2,1,0:T(8,128)} %copy-done.6, f32[16,2,8,128]{3,2,1,0:T(8,128)} %copy-done.7), custom_call_target="tpu_custom_call" | custom-call | tf_op jit(solution)/shard_map/total/pallas_call | solution.py:623
  111.2 0.0 collective-permute-done.15.refs_3_
  111.3 2.3 %collective-permute-done.14.refs_2_ = f32[4,128]{1,0:T(4,128)S(1)} collective-permute-done((f32[4,128]{1,0:T(4,128)S(1)}, f32[4,128]{1,0:T(4,128)S(1)}, u32[]{:S(2)}, u32[]{:S(2)}) %collective-permute-start.14) | collective-permute-done | bytes 2080 | tf_op jit(solution)/shard_map/ppermute | solution.py:598
  113.6 0.0 collective-permute-done.13.refs_1_
  113.6 0.6 add.9
  (12 shorter events, 0.0 us)
Async XLA Ops:
  1.4 14.8 %copy-start = (f32[1,3,16,4,2048]{4,3,2,1,0:T(4,128)S(1)}, f32[1,3,16,4,2048]{4,3,2,1,0:T(4,128)}, u32[]{:S(2)}) copy-start(f32[1,3,16,4,2048]{4,3,2,1,0:T(4,128)} %param.9) | copy-start | bytes 4718596
  1.4 14.8 %copy-start.1 = (f32[1,3,16,4,2048]{4,3,2,1,0:T(4,128)S(1)}, f32[1,3,16,4,2048]{4,3,2,1,0:T(4,128)}, u32[]{:S(2)}) copy-start(f32[1,3,16,4,2048]{4,3,2,1,0:T(4,128)} %param.10) | copy-start | bytes 4718596
  1.4 14.8 %copy-start.3 = (s32[16,4,16]{2,1,0:T(4,128)S(1)}, s32[16,4,16]{2,1,0:T(4,128)}, u32[]{:S(2)}) copy-start(s32[16,4,16]{2,1,0:T(4,128)} %param.14) | copy-start | bytes 12292
  1.4 14.8 %copy-start.4 = (f32[4,2048]{1,0:T(4,128)S(1)}, f32[4,2048]{1,0:T(4,128)}, u32[]{:S(2)}) copy-start(f32[4,2048]{1,0:T(4,128)} %param.16) | copy-start | bytes 98308
  12.4 12.1 %collective-permute-start = (f32[20,4,2,8,128]{4,3,2,1,0:T(8,128)}, f32[20,4,2,8,128]{4,3,2,1,0:T(8,128)S(1)}, u32[]{:S(2)}, u32[]{:S(2)}) collective-permute-start(f32[20,4,2,8,128]{4,3,2,1,0:T(8,128)} %get-tuple-element.52), channel_id=1, source_target_pairs={{1,2},{3,4},{5,6},{7,8},{9,10},{11,12},{13,14},{15,16},{17,18},{19... | collective-permute-start | bytes 1966088 | tf_op jit(solution)/shard_map/ppermute | solution.py:521
  14.4 10.2 %collective-permute-start.1 = (f32[20,4,2,8,128]{4,3,2,1,0:T(8,128)}, f32[20,4,2,8,128]{4,3,2,1,0:T(8,128)S(1)}, u32[]{:S(2)}, u32[]{:S(2)}) collective-permute-start(f32[20,4,2,8,128]{4,3,2,1,0:T(8,128)} %get-tuple-element.53), channel_id=1, source_target_pairs={{0,1},{1,0},{2,3},{3,2},{4,5},{5,4},{6,7},{7,6},{8,9},{9,8},{10,11... | collective-permute-start | bytes 1966088 | tf_op jit(solution)/shard_map/ppermute | solution.py:522
  16.1 1.9 %copy-start.2 = (bf16[1,2,2,3,16,4,2048]{6,5,4,3,2,1,0:T(4,128)(2,1)S(1)}, bf16[1,2,2,3,16,4,2048]{6,5,4,3,2,1,0:T(4,128)(2,1)}, u32[]{:S(2)}) copy-start(bf16[1,2,2,3,16,4,2048]{6,5,4,3,2,1,0:T(4,128)(2,1)} %param.11) | copy-start | bytes 9437188
  47.7 10.7 %collective-permute-start.2 = (f32[16,4,2,8,128]{4,3,2,1,0:T(8,128)}, f32[16,4,2,8,128]{4,3,2,1,0:T(8,128)S(1)}, u32[]{:S(2)}, u32[]{:S(2)}) collective-permute-start(f32[16,4,2,8,128]{4,3,2,1,0:T(8,128)} %get-tuple-element.56), channel_id=1, source_target_pairs={{1,2},{3,4},{5,6},{7,8},{9,10},{11,12},{13,14},{15,16},{17,18},{19... | collective-permute-start | bytes 1572872 | tf_op jit(solution)/shard_map/ppermute | solution.py:521
  49.6 8.8 %collective-permute-start.3 = (f32[16,4,2,8,128]{4,3,2,1,0:T(8,128)}, f32[16,4,2,8,128]{4,3,2,1,0:T(8,128)S(1)}, u32[]{:S(2)}, u32[]{:S(2)}) collective-permute-start(f32[16,4,2,8,128]{4,3,2,1,0:T(8,128)} %get-tuple-element.57), channel_id=1, source_target_pairs={{0,1},{1,0},{2,3},{3,2},{4,5},{5,4},{6,7},{7,6},{8,9},{9,8},{10,11... | collective-permute-start | bytes 1572872 | tf_op jit(solution)/shard_map/ppermute | solution.py:522
  74.5 6.3 %collective-permute-start.6 = (f32[4,128]{1,0:T(4,128)S(1)}, f32[4,128]{1,0:T(4,128)S(1)}, u32[]{:S(2)}, u32[]{:S(2)}) collective-permute-start(f32[4,128]{1,0:T(4,128)S(1)} %get-tuple-element.64.refs_0_), channel_id=1, source_target_pairs={{0,9},{1,8},{2,11},{3,10},{4,13},{5,12},{6,15},{7,14},{8,1},{9,0},... | collective-permute-start | bytes 6152 | tf_op jit(solution)/shard_map/ppermute | solution.py:598
  76.2 4.6 %collective-permute-start.5 = (f32[4,128]{1,0:T(4,128)S(1)}, f32[4,128]{1,0:T(4,128)S(1)}, u32[]{:S(2)}, u32[]{:S(2)}) collective-permute-start(f32[4,128]{1,0:T(4,128)S(1)} %get-tuple-element.64.refs_0_), channel_id=1, source_target_pairs={{0,8},{1,9},{2,10},{3,11},{4,12},{5,13},{6,14},{7,15},{8,0},{9,1},... | collective-permute-start | bytes 6152 | tf_op jit(solution)/shard_map/ppermute | solution.py:598
  76.6 4.2 %collective-permute-start.4 = (f32[4,128]{1,0:T(4,128)S(1)}, f32[4,128]{1,0:T(4,128)S(1)}, u32[]{:S(2)}, u32[]{:S(2)}) collective-permute-start(f32[4,128]{1,0:T(4,128)S(1)} %get-tuple-element.64.refs_0_), channel_id=1, source_target_pairs={{0,1},{1,0},{2,3},{3,2},{4,5},{5,4},{6,7},{7,6},{8,9},{9,8},{10,11... | collective-permute-start | bytes 6152 | tf_op jit(solution)/shard_map/ppermute | solution.py:598
  80.8 23.4 %collective-permute-start.10 = (f32[16,2,8,128]{3,2,1,0:T(8,128)}, f32[16,2,8,128]{3,2,1,0:T(8,128)S(1)}, u32[]{:S(2)}, u32[]{:S(2)}) collective-permute-start(f32[16,2,8,128]{3,2,1,0:T(8,128)} %get-tuple-element.78), channel_id=1, source_target_pairs={{0,64},{64,128},{128,192},{192,0},{1,65},{65,129},{129,193},{193,1... | collective-permute-start | bytes 393224 | tf_op jit(solution)/shard_map/ppermute | solution.py:592
  84.2 20.0 %collective-permute-start.11 = (f32[16,2,8,128]{3,2,1,0:T(8,128)}, f32[16,2,8,128]{3,2,1,0:T(8,128)S(1)}, u32[]{:S(2)}, u32[]{:S(2)}) collective-permute-start(f32[16,2,8,128]{3,2,1,0:T(8,128)} %get-tuple-element.79), channel_id=1, source_target_pairs={{0,128},{64,192},{128,0},{192,64},{1,129},{65,193},{129,1},{193,65... | collective-permute-start | bytes 393224 | tf_op jit(solution)/shard_map/ppermute | solution.py:592
  89.4 14.8 %collective-permute-start.12 = (f32[16,2,8,128]{3,2,1,0:T(8,128)}, f32[16,2,8,128]{3,2,1,0:T(8,128)S(1)}, u32[]{:S(2)}, u32[]{:S(2)}) collective-permute-start(f32[16,2,8,128]{3,2,1,0:T(8,128)} %get-tuple-element.80), channel_id=1, source_target_pairs={{0,192},{64,0},{128,64},{192,128},{1,193},{65,1},{129,65},{193,129... | collective-permute-start | bytes 393224 | tf_op jit(solution)/shard_map/ppermute | solution.py:592
  92.1 7.1 %collective-permute-start.9 = (f32[4,128]{1,0:T(4,128)S(1)}, f32[4,128]{1,0:T(4,128)S(1)}, u32[]{:S(2)}, u32[]{:S(2)}) collective-permute-start(f32[4,128]{1,0:T(4,128)S(1)} %add.7.refs_0_), channel_id=1, source_target_pairs={{0,6},{1,7},{2,4},{3,5},{4,2},{5,3},{6,0},{7,1},{8,14},{9,15},{10,... | collective-permute-start | bytes 6152 | tf_op jit(solution)/shard_map/ppermute | solution.py:598
  93.6 10.5 %collective-permute-start.8 = (f32[4,128]{1,0:T(4,128)S(1)}, f32[4,128]{1,0:T(4,128)S(1)}, u32[]{:S(2)}, u32[]{:S(2)}) collective-permute-start(f32[4,128]{1,0:T(4,128)S(1)} %add.7.refs_0_), channel_id=1, source_target_pairs={{0,4},{1,5},{2,6},{3,7},{4,0},{5,1},{6,2},{7,3},{8,12},{9,13},{10,... | collective-permute-start | bytes 6152 | tf_op jit(solution)/shard_map/ppermute | solution.py:598
  99.2 5.0 %collective-permute-start.7 = (f32[4,128]{1,0:T(4,128)S(1)}, f32[4,128]{1,0:T(4,128)S(1)}, u32[]{:S(2)}, u32[]{:S(2)}) collective-permute-start(f32[4,128]{1,0:T(4,128)S(1)} %add.7.refs_0_), channel_id=1, source_target_pairs={{0,2},{1,3},{2,0},{3,1},{4,6},{5,7},{6,4},{7,5},{8,10},{9,11},{10,... | collective-permute-start | bytes 6152 | tf_op jit(solution)/shard_map/ppermute | solution.py:598
  104.2 5.3 %copy-start.5 = (f32[16,2,8,128]{3,2,1,0:T(8,128)}, f32[16,2,8,128]{3,2,1,0:T(8,128)S(1)}, u32[]{:S(2)}) copy-start(f32[16,2,8,128]{3,2,1,0:T(8,128)S(1)} %collective-permute-done.10.b) | copy-start | bytes 393220
  104.2 5.2 %copy-start.6 = (f32[16,2,8,128]{3,2,1,0:T(8,128)}, f32[16,2,8,128]{3,2,1,0:T(8,128)S(1)}, u32[]{:S(2)}) copy-start(f32[16,2,8,128]{3,2,1,0:T(8,128)S(1)} %collective-permute-done.11.c) | copy-start | bytes 393220
  104.2 5.2 %copy-start.7 = (f32[16,2,8,128]{3,2,1,0:T(8,128)}, f32[16,2,8,128]{3,2,1,0:T(8,128)S(1)}, u32[]{:S(2)}) copy-start(f32[16,2,8,128]{3,2,1,0:T(8,128)S(1)} %collective-permute-done.12.d) | copy-start | bytes 393220
  104.3 7.0 %collective-permute-start.15 = (f32[4,128]{1,0:T(4,128)S(1)}, f32[4,128]{1,0:T(4,128)S(1)}, u32[]{:S(2)}, u32[]{:S(2)}) collective-permute-start(f32[4,128]{1,0:T(4,128)S(1)} %add.8.refs_0_), channel_id=1, source_target_pairs={{0,48},{1,49},{2,50},{3,51},{4,52},{5,53},{6,54},{7,55},{8,56},{9,... | collective-permute-start | bytes 6152 | tf_op jit(solution)/shard_map/ppermute | solution.py:598
  108.5 5.1 %collective-permute-start.14 = (f32[4,128]{1,0:T(4,128)S(1)}, f32[4,128]{1,0:T(4,128)S(1)}, u32[]{:S(2)}, u32[]{:S(2)}) collective-permute-start(f32[4,128]{1,0:T(4,128)S(1)} %add.8.refs_0_), channel_id=1, source_target_pairs={{0,32},{1,33},{2,34},{3,35},{4,36},{5,37},{6,38},{7,39},{8,40},{9,... | collective-permute-start | bytes 6152 | tf_op jit(solution)/shard_map/ppermute | solution.py:598
  109.3 4.3 %collective-permute-start.13 = (f32[4,128]{1,0:T(4,128)S(1)}, f32[4,128]{1,0:T(4,128)S(1)}, u32[]{:S(2)}, u32[]{:S(2)}) collective-permute-start(f32[4,128]{1,0:T(4,128)S(1)} %add.8.refs_0_), channel_id=1, source_target_pairs={{0,16},{1,17},{2,18},{3,19},{4,20},{5,21},{6,22},{7,23},{8,24},{9,... | collective-permute-start | bytes 6152 | tf_op jit(solution)/shard_map/ppermute | solution.py:598

commit v7 on v6

--- a/solution.py
+++ b/solution.py
@@ -131,7 +131,7 @@
     return lax.dot_general(pick, values, (((1,), (1,)), ((), ())), preferred_element_type=jnp.float32)
 
 
-def free_run(ea, ha, eb, hb, coef, faces):
+def free_run(ea, ha, eb, hb, coef, faces, sends):
     m = masks()
     half = WIDTH // 2
     to_left, to_right = faces.at[0], faces.at[1]
@@ -157,15 +157,23 @@
         to_right[pl.ds(2 * s - 2, 2)] = hb[1:3, half]
         return 0
 
-    lax.fori_loop(1, ROUND + 1, step, 0)
+    lax.fori_loop(1, ROUND // 2 + 1, step, 0)
+    for copy in sends[:2]:
+        copy.start()
+    lax.fori_loop(ROUND // 2 + 1, ROUND + 1, step, 0)
+    for copy in sends[2:]:
+        copy.start()
+    for copy in sends:
+        copy.wait()
 
 
 def swaps(info, faces, inter_far, intra_far, sems):
     odd = lax.rem(info[0], 2)
-    return [
-        pltpu.make_async_copy(faces.at[side], far, sems.at[i])
-        for i, (side, far) in enumerate(((odd, inter_far), (1 - odd, intra_far)))
-    ]
+    copies = []
+    for part in (pl.ds(0, ROUND), pl.ds(ROUND, faces.shape[1] - ROUND)):
+        for side, far in ((odd, inter_far), (1 - odd, intra_far)):
+            copies.append(pltpu.make_async_copy(faces.at[side, part], far.at[part], sems.at[len(copies)]))
+    return copies
 
 
 def free_kernel(
@@ -203,12 +211,7 @@
     load_rows(e_in, eb, 1.0, half, half)
     load_rows(h_in, ha, 1.0 / COEF_H, 0, half, 1)
     load_rows(h_in, hb, 1.0 / COEF_H, half, half, 1)
-    free_run(ea, ha, eb, hb, coef, faces)
-    sends = swaps(info, faces, inter_far, intra_far, sent)
-    for copy in sends:
-        copy.start()
-    for copy in sends:
-        copy.wait()
+    free_run(ea, ha, eb, hb, coef, faces, swaps(info, faces, inter_far, intra_far, sent))
 
 
 def angles():
@@ -390,12 +393,7 @@
             return 0
 
         lax.fori_loop(0, half, split, 0)
-        free_run(ea, ha, eb, hb, coef, faces)
-        sends = swaps(info, faces, inter_far, intra_far, sent)
-        for copy in sends:
-            copy.start()
-        for copy in sends:
-            copy.wait()
+        free_run(ea, ha, eb, hb, coef, faces, swaps(info, faces, inter_far, intra_far, sent))
         return
 
     omegas, _, _ = angles()
@@ -506,7 +504,7 @@
             held(3, WIDTH, 64, 128),
             held(2, planes, *CELLS),
             pltpu.SemaphoreType.DMA((5,)),
-            pltpu.SemaphoreType.DMA((2,)),
+            pltpu.SemaphoreType.DMA((4,)),
         ],
         compiler_params=room(12),
         name="free",
@@ -555,7 +553,7 @@
         out_specs=(VMEM,) * 4 + (FAR,) * 2,
         scratch_shapes=halos
         + [held(*half)] * 4
-        + [held(2, 2 * ROUND, *CELLS), pltpu.SemaphoreType.DMA((2,))],
+        + [held(2, 2 * ROUND, *CELLS), pltpu.SemaphoreType.DMA((4,))],
         compiler_params=room(12),
         name="round",
     )(info, here(e_all), here(h_all), coef, inter, intra)
@@ -618,7 +616,7 @@
     for d in range(1, ports):
         parts[d] = to_port(parts[d], d)
     total = stage(total, (2, 4))
-    total, e_out, h_out, *parts = lax.optimization_barrier((total, e_out, h_out, *parts))
+    total, e_out, h_out, parts[1], parts[2] = lax.optimization_barrier((total, e_out, h_out, parts[1], parts[2]))
     intersections = stage(total, (16, 32), last_kernel, (1, FREQS, 2))
     gradient = pl.pallas_call(
         sum_kernel,

time: 116 us -> 114 us (0.983); the launches traced: 114 us -> 114 us
  no operation moved by 1% of the time
where the time goes in v7:
time: 114 us
  Pallas kernels  66.2 us (58%)
  starting transfers between devices  35.8 us (31%)
  waiting for transfers between devices  7.79 us (7%)
  local copies, waits for them, and re-layouts  2.55 us (2%)
  between operations  1.46 us (1%)
    pallas_call x1, Pallas kernels, body(): pl.pallas_call(functools.partial(round_kernel, False, scale), out_shape=(...  23 us
    ppermute x9, starting transfers between devices, stage(): lax.ppermute(total, 'tile', [(i, i ^ flip) for i in range(tiles)])  17.2 us
    pallas_call x1, Pallas kernels, body(): pl.pallas_call(functools.partial(round_kernel, True, scale), out_shape=(h...  16.1 us
    ppermute x3, starting transfers between devices, to_port(): return lax.ppermute(x, 'port', [(i, (i + d) % ports) for i in range(ports)])  11.2 us
    pallas_call x1, Pallas kernels, body(): pl.pallas_call(free_kernel, out_shape=(f32(WIDTH, *CELLS),) + sent(planes...  10.9 us
    ppermute x2, waiting for transfers between devices, swap(): lax.ppermute(inter, 'tile', across + [(j, i) for i, j in across])  6.07 us
    pallas_call x1, Pallas kernels, body(): pl.pallas_call(finish_kernel, out_shape=(pltpu.HBM((WIDTH, HALF, 8, 128),...  4.2 us
    pallas_call x1, Pallas kernels, body(): pl.pallas_call(wide_kernel, out_shape=(turned_shape, f32(64, 128), fields...  4.02 us
  transfers between devices with their start and end apart: 16, of which 3 were waited for; matrix products, arithmetic and copies ran while one was open for 0% of the time, Pallas kernels for 14%

profile of v7, /device:TPU:8, one launch (start us, length us, event | category | flops | bytes accessed | tf_op | source)
XLA Modules:
  0.0 113.8 jit_solution(12277066829140441679)
XLA Ops:
  1.3 0.1 pad_add_fusion.info
  1.4 10.9 %free.1 = (f32[16,4,2,8,128]{4,3,2,1,0:T(8,128)S(1)}, f32[20,4,2,8,128]{4,3,2,1,0:T(8,128)}, f32[20,4,2,8,128]{4,3,2,1,0:T(8,128)}) custom-call(s32[3]{0:T(128)S(1)} %pad_add_fusion.info, f32[4]{0:T(128)} %table.1, s32[64,16]{1,0:T(8,128)} %bitcast.50, s32[64,16]{1,0:T(8,128)} %bitcast.45, f32[16,64,128]{2,1,0:T(8,128)} %bitcast.48, ...), custom_call_target="tpu_custom_call" | custom-call | tf_op jit(solution)/shard_map/free/pallas_call | solution.py:493
  12.3 1.9 %collective-permute-start = (f32[20,4,2,8,128]{4,3,2,1,0:T(8,128)}, f32[20,4,2,8,128]{4,3,2,1,0:T(8,128)S(1)}, u32[]{:S(2)}, u32[]{:S(2)}) collective-permute-start(f32[20,4,2,8,128]{4,3,2,1,0:T(8,128)} %get-tuple-element.50), channel_id=1, source_target_pairs={{1,2},{3,4},{5,6},{7,8},{9,10},{11,12},{13,14},{15,16},{17,18},{19... | collective-permute-start | bytes 1966088 | tf_op jit(solution)/shard_map/ppermute | solution.py:519
  14.2 1.8 %collective-permute-start.1 = (f32[20,4,2,8,128]{4,3,2,1,0:T(8,128)}, f32[20,4,2,8,128]{4,3,2,1,0:T(8,128)S(1)}, u32[]{:S(2)}, u32[]{:S(2)}) collective-permute-start(f32[20,4,2,8,128]{4,3,2,1,0:T(8,128)} %get-tuple-element.51), channel_id=1, source_target_pairs={{0,1},{1,0},{2,3},{3,2},{4,5},{5,4},{6,7},{7,6},{8,9},{9,8},{10,11... | collective-permute-start | bytes 1966088 | tf_op jit(solution)/shard_map/ppermute | solution.py:520
  16.0 0.0 copy-done
  16.0 0.0 copy-done.1
  16.0 0.0 copy-done.3
  16.0 0.0 copy-start.2
  16.0 1.9 %copy-done.2 = bf16[1,2,2,3,16,4,2048]{6,5,4,3,2,1,0:T(4,128)(2,1)S(1)} copy-done((bf16[1,2,2,3,16,4,2048]{6,5,4,3,2,1,0:T(4,128)(2,1)S(1)}, bf16[1,2,2,3,16,4,2048]{6,5,4,3,2,1,0:T(4,128)(2,1)}, u32[]{:S(2)}) %copy-start.2) | copy-done | bytes 3145752
  17.9 4.0 %wide.1 = (f32[2,2,3,4,16,2,8,128]{7,6,5,4,3,2,1,0:T(8,128)S(1)}, f32[64,128]{1,0:T(8,128)S(1)}, f32[3,17,4,2,8,128]{5,4,3,2,1,0:T(8,128)S(1)}, f32[3,17,4,2,8,128]{5,4,3,2,1,0:T(8,128)S(1)}) custom-call(bf16[2,2,3,16,64,128]{5,4,3,2,1,0:T(8,128)(2,1)S(1)} %bitcast.44, s32[64,16]{1,0:T(8,128)S(1)} %bitcast.46, f32[64,128]{1,0:T(8,128)S(1)} %bitcast.47, ...), custom_call_target="tpu_custom_call" | custom-call | tf_op jit(solution)/shard_map/wide/pallas_call | solution.py:528
  21.9 2.5 %collective-permute-done.inter = f32[20,4,2,8,128]{4,3,2,1,0:T(8,128)S(1)} collective-permute-done((f32[20,4,2,8,128]{4,3,2,1,0:T(8,128)}, f32[20,4,2,8,128]{4,3,2,1,0:T(8,128)S(1)}, u32[]{:S(2)}, u32[]{:S(2)}) %collective-permute-start) | collective-permute-done | bytes 655392 | tf_op jit(solution)/shard_map/ppermute | solution.py:519
  24.4 0.0 collective-permute-done.1.intra
  24.4 23.0 %round.2 = (f32[8,3,16,4,2,8,128]{6,5,4,3,2,1,0:T(8,128)S(1)}, f32[3,17,4,2,8,128]{5,4,3,2,1,0:T(8,128)S(1)}, f32[3,17,4,2,8,128]{5,4,3,2,1,0:T(8,128)S(1)}, f32...) custom-call(s32[3]{0:T(128)S(1)} %pad_add_fusion.info, ...), custom_call_target="tpu_custom_call" | custom-call | tf_op jit(solution)/shard_map/round/pallas_call | solution.py:549
  47.4 1.9 %collective-permute-start.2 = (f32[16,4,2,8,128]{4,3,2,1,0:T(8,128)}, f32[16,4,2,8,128]{4,3,2,1,0:T(8,128)S(1)}, u32[]{:S(2)}, u32[]{:S(2)}) collective-permute-start(f32[16,4,2,8,128]{4,3,2,1,0:T(8,128)} %get-tuple-element.54), channel_id=1, source_target_pairs={{1,2},{3,4},{5,6},{7,8},{9,10},{11,12},{13,14},{15,16},{17,18},{19... | collective-permute-start | bytes 1572872 | tf_op jit(solution)/shard_map/ppermute | solution.py:519
  49.3 1.8 %collective-permute-start.3 = (f32[16,4,2,8,128]{4,3,2,1,0:T(8,128)}, f32[16,4,2,8,128]{4,3,2,1,0:T(8,128)S(1)}, u32[]{:S(2)}, u32[]{:S(2)}) collective-permute-start(f32[16,4,2,8,128]{4,3,2,1,0:T(8,128)} %get-tuple-element.55), channel_id=1, source_target_pairs={{0,1},{1,0},{2,3},{3,2},{4,5},{5,4},{6,7},{7,6},{8,9},{9,8},{10,11... | collective-permute-start | bytes 1572872 | tf_op jit(solution)/shard_map/ppermute | solution.py:520
  51.1 3.4 %first.1 = (f32[4,16,2,8,128]{4,3,2,1,0:T(8,128)S(1)}, f32[2,2,3,4,16,2,8,128]{7,6,5,4,3,2,1,0:T(8,128)S(1)}) custom-call(f32[8,3,16,4,2,8,128]{6,5,4,3,2,1,0:T(8,128)S(1)} %get-tuple-element.58.e, f32[2,2,3,4,16,2,8,128]{7,6,5,4,3,2,1,0:T(8,128)S(1)} %get-tuple-element.59.turned), custom_call_target="tpu_custom_call" | custom-call | tf_op jit(solution)/shard_map/first/pallas_call | solution.py:561
  54.5 3.6 %collective-permute-done.2.rest_0_ = f32[16,4,2,8,128]{4,3,2,1,0:T(8,128)S(1)} collective-permute-done((f32[16,4,2,8,128]{4,3,2,1,0:T(8,128)}, f32[16,4,2,8,128]{4,3,2,1,0:T(8,128)S(1)}, u32[]{:S(2)}, u32[]{:S(2)}) %collective-permute-start.2) | collective-permute-done | bytes 524320 | tf_op jit(solution)/shard_map/ppermute | solution.py:519
  58.1 0.0 collective-permute-done.3.rest_1_
  58.1 16.1 %round.3 = (f32[8,3,16,4,2,8,128]{6,5,4,3,2,1,0:T(8,128)S(1)}, f32[3,17,4,2,8,128]{5,4,3,2,1,0:T(8,128)S(1)}, f32[3,17,4,2,8,128]{5,4,3,2,1,0:T(8,128)S(1)}, f32[4,128]{1,0:T(4,128)S(1)}) custom-call(s32[3]{0:T(128)S(1)} %pad_add_fusion.info, f32[3,17,4,2,8,128]{5,4,3,2,1,0:T(8,128)S(1)} %get-tuple-element.52.e_in, ...), custom_call_target="tpu_custom_call" | custom-call | tf_op jit(solution)/shard_map/round/pallas_call | solution.py:570
  74.1 1.7 %collective-permute-start.6 = (f32[4,128]{1,0:T(4,128)S(1)}, f32[4,128]{1,0:T(4,128)S(1)}, u32[]{:S(2)}, u32[]{:S(2)}) collective-permute-start(f32[4,128]{1,0:T(4,128)S(1)} %get-tuple-element.62.refs_0_), channel_id=1, source_target_pairs={{0,9},{1,8},{2,11},{3,10},{4,13},{5,12},{6,15},{7,14},{8,1},{9,0},... | collective-permute-start | bytes 6152 | tf_op jit(solution)/shard_map/ppermute | solution.py:596
  75.9 0.4 collective-permute-start.5
  76.2 0.0 collective-permute-start.4
  76.3 4.2 %finish.1 = (f32[16,2,8,128]{3,2,1,0:T(8,128)}, f32[16,2,8,128]{3,2,1,0:T(8,128)}, f32[16,2,8,128]{3,2,1,0:T(8,128)}, f32[16,2,8,128]{3,2,1,0:T(8,128)}) custom-call(s32[3]{0:T(128)S(1)} %pad_add_fusion.info, f32[8,3,16,4,2,8,128]{6,5,4,3,2,1,0:T(8,128)S(1)} %get-tuple-element.63.e, f32[2,2,3,4,16,2,8,128]{7,6,5,4,3,2,1,0:T(8,128)S(1)} %get-tuple-element.64.turned, ...), custom_call_target="tpu_custom_call" | custom-call | tf_op jit(solution)/shard_map/finish/pallas_call | solution.py:579
  80.5 0.0 collective-permute-done.6.refs_3_
  80.5 0.0 collective-permute-done.5.refs_2_
  80.5 0.0 collective-permute-done.4.refs_1_
  80.5 3.3 %collective-permute-start.10 = (f32[16,2,8,128]{3,2,1,0:T(8,128)}, f32[16,2,8,128]{3,2,1,0:T(8,128)S(1)}, u32[]{:S(2)}, u32[]{:S(2)}) collective-permute-start(f32[16,2,8,128]{3,2,1,0:T(8,128)} %get-tuple-element.75), channel_id=1, source_target_pairs={{0,64},{64,128},{128,192},{192,0},{1,65},{65,129},{129,193},{193,1... | collective-permute-start | bytes 393224 | tf_op jit(solution)/shard_map/ppermute | solution.py:590
  83.9 5.2 %collective-permute-start.11 = (f32[16,2,8,128]{3,2,1,0:T(8,128)}, f32[16,2,8,128]{3,2,1,0:T(8,128)S(1)}, u32[]{:S(2)}, u32[]{:S(2)}) collective-permute-start(f32[16,2,8,128]{3,2,1,0:T(8,128)} %get-tuple-element.76), channel_id=1, source_target_pairs={{0,128},{64,192},{128,0},{192,64},{1,129},{65,193},{129,1},{193,65... | collective-permute-start | bytes 393224 | tf_op jit(solution)/shard_map/ppermute | solution.py:590
  89.1 2.7 %collective-permute-start.12 = (f32[16,2,8,128]{3,2,1,0:T(8,128)}, f32[16,2,8,128]{3,2,1,0:T(8,128)S(1)}, u32[]{:S(2)}, u32[]{:S(2)}) collective-permute-start(f32[16,2,8,128]{3,2,1,0:T(8,128)} %get-tuple-element.82), channel_id=1, source_target_pairs={{0,192},{64,0},{128,64},{192,128},{1,193},{65,1},{129,65},{193,129... | collective-permute-start | bytes 393224 | tf_op jit(solution)/shard_map/ppermute | solution.py:590
  91.7 1.6 %collective-permute-start.9 = (f32[4,128]{1,0:T(4,128)S(1)}, f32[4,128]{1,0:T(4,128)S(1)}, u32[]{:S(2)}, u32[]{:S(2)}) collective-permute-start(f32[4,128]{1,0:T(4,128)S(1)} %add.7.refs_0_), channel_id=1, source_target_pairs={{0,6},{1,7},{2,4},{3,5},{4,2},{5,3},{6,0},{7,1},{8,14},{9,15},{10,... | collective-permute-start | bytes 6152 | tf_op jit(solution)/shard_map/ppermute | solution.py:596
  93.3 5.5 %collective-permute-start.8 = (f32[4,128]{1,0:T(4,128)S(1)}, f32[4,128]{1,0:T(4,128)S(1)}, u32[]{:S(2)}, u32[]{:S(2)}) collective-permute-start(f32[4,128]{1,0:T(4,128)S(1)} %add.7.refs_0_), channel_id=1, source_target_pairs={{0,4},{1,5},{2,6},{3,7},{4,0},{5,1},{6,2},{7,3},{8,12},{9,13},{10,... | collective-permute-start | bytes 6152 | tf_op jit(solution)/shard_map/ppermute | solution.py:596
  98.9 0.0 collective-permute-done.9.refs_3_
  98.9 2.7 %collective-permute-start.7 = (f32[4,128]{1,0:T(4,128)S(1)}, f32[4,128]{1,0:T(4,128)S(1)}, u32[]{:S(2)}, u32[]{:S(2)}) collective-permute-start(f32[4,128]{1,0:T(4,128)S(1)} %add.7.refs_0_), channel_id=1, source_target_pairs={{0,2},{1,3},{2,0},{3,1},{4,6},{5,7},{6,4},{7,5},{8,10},{9,11},{10,... | collective-permute-start | bytes 6152 | tf_op jit(solution)/shard_map/ppermute | solution.py:596
  101.6 2.3 %out.1 = (f32[3,16,64,128]{3,2,1,0:T(8,128)}, f32[3,16,64,128]{3,2,1,0:T(8,128)}) custom-call(f32[3,17,4,2,8,128]{5,4,3,2,1,0:T(8,128)S(1)} %get-tuple-element.71.e, f32[3,17,4,2,8,128]{5,4,3,2,1,0:T(8,128)S(1)} %get-tuple-element.72.h), custom_call_target="tpu_custom_call" | custom-call | tf_op jit(solution)/shard_map/out/pallas_call | solution.py:606
  103.9 0.0 collective-permute-done.8.refs_2_
  103.9 0.0 collective-permute-done.7.refs_1_
  103.9 0.0 collective-permute-done.10.b
  103.9 0.0 collective-permute-done.11.c
  103.9 4.3 %collective-permute-start.15 = (f32[4,128]{1,0:T(4,128)S(1)}, f32[4,128]{1,0:T(4,128)S(1)}, u32[]{:S(2)}, u32[]{:S(2)}) collective-permute-start(f32[4,128]{1,0:T(4,128)S(1)} %add.8.refs_0_), channel_id=1, source_target_pairs={{0,48},{1,49},{2,50},{3,51},{4,52},{5,53},{6,54},{7,55},{8,56},{9,... | collective-permute-start | bytes 6152 | tf_op jit(solution)/shard_map/ppermute | solution.py:596
  108.2 0.8 collective-permute-start.14
  109.0 0.2 collective-permute-start.13
  109.1 0.0 collective-permute-done.12.d
  109.1 0.6 copy-done.7
  109.8 1.8 %total.1 = f32[16,16,128]{2,1,0:T(8,128)} custom-call(f32[16,2,8,128]{3,2,1,0:T(8,128)} %get-tuple-element.79.a, f32[16,2,8,128]{3,2,1,0:T(8,128)} %copy-done.5, f32[16,2,8,128]{3,2,1,0:T(8,128)} %copy-done.6, f32[16,2,8,128]{3,2,1,0:T(8,128)} %copy-done.7), custom_call_target="tpu_custom_call" | custom-call | tf_op jit(solution)/shard_map/total/pallas_call | solution.py:621
  111.6 0.0 collective-permute-done.15.refs_3_
  111.6 1.7 %collective-permute-done.14.refs_2_ = f32[4,128]{1,0:T(4,128)S(1)} collective-permute-done((f32[4,128]{1,0:T(4,128)S(1)}, f32[4,128]{1,0:T(4,128)S(1)}, u32[]{:S(2)}, u32[]{:S(2)}) %collective-permute-start.14) | collective-permute-done | bytes 2080 | tf_op jit(solution)/shard_map/ppermute | solution.py:596
  113.3 0.0 collective-permute-done.13.refs_1_
  113.3 0.6 add.9
  (12 shorter events, 0.0 us)
Async XLA Ops:
  1.4 14.6 %copy-start = (f32[1,3,16,4,2048]{4,3,2,1,0:T(4,128)S(1)}, f32[1,3,16,4,2048]{4,3,2,1,0:T(4,128)}, u32[]{:S(2)}) copy-start(f32[1,3,16,4,2048]{4,3,2,1,0:T(4,128)} %param.9) | copy-start | bytes 4718596
  1.4 14.6 %copy-start.1 = (f32[1,3,16,4,2048]{4,3,2,1,0:T(4,128)S(1)}, f32[1,3,16,4,2048]{4,3,2,1,0:T(4,128)}, u32[]{:S(2)}) copy-start(f32[1,3,16,4,2048]{4,3,2,1,0:T(4,128)} %param.10) | copy-start | bytes 4718596
  1.4 14.6 %copy-start.3 = (s32[16,4,16]{2,1,0:T(4,128)S(1)}, s32[16,4,16]{2,1,0:T(4,128)}, u32[]{:S(2)}) copy-start(s32[16,4,16]{2,1,0:T(4,128)} %param.14) | copy-start | bytes 12292
  1.4 14.6 %copy-start.4 = (f32[4,2048]{1,0:T(4,128)S(1)}, f32[4,2048]{1,0:T(4,128)}, u32[]{:S(2)}) copy-start(f32[4,2048]{1,0:T(4,128)} %param.16) | copy-start | bytes 98308
  12.3 12.1 %collective-permute-start = (f32[20,4,2,8,128]{4,3,2,1,0:T(8,128)}, f32[20,4,2,8,128]{4,3,2,1,0:T(8,128)S(1)}, u32[]{:S(2)}, u32[]{:S(2)}) collective-permute-start(f32[20,4,2,8,128]{4,3,2,1,0:T(8,128)} %get-tuple-element.50), channel_id=1, source_target_pairs={{1,2},{3,4},{5,6},{7,8},{9,10},{11,12},{13,14},{15,16},{17,18},{19... | collective-permute-start | bytes 1966088 | tf_op jit(solution)/shard_map/ppermute | solution.py:519
  14.2 10.2 %collective-permute-start.1 = (f32[20,4,2,8,128]{4,3,2,1,0:T(8,128)}, f32[20,4,2,8,128]{4,3,2,1,0:T(8,128)S(1)}, u32[]{:S(2)}, u32[]{:S(2)}) collective-permute-start(f32[20,4,2,8,128]{4,3,2,1,0:T(8,128)} %get-tuple-element.51), channel_id=1, source_target_pairs={{0,1},{1,0},{2,3},{3,2},{4,5},{5,4},{6,7},{7,6},{8,9},{9,8},{10,11... | collective-permute-start | bytes 1966088 | tf_op jit(solution)/shard_map/ppermute | solution.py:520
  16.0 1.9 %copy-start.2 = (bf16[1,2,2,3,16,4,2048]{6,5,4,3,2,1,0:T(4,128)(2,1)S(1)}, bf16[1,2,2,3,16,4,2048]{6,5,4,3,2,1,0:T(4,128)(2,1)}, u32[]{:S(2)}) copy-start(bf16[1,2,2,3,16,4,2048]{6,5,4,3,2,1,0:T(4,128)(2,1)} %param.11) | copy-start | bytes 9437188
  47.4 10.7 %collective-permute-start.2 = (f32[16,4,2,8,128]{4,3,2,1,0:T(8,128)}, f32[16,4,2,8,128]{4,3,2,1,0:T(8,128)S(1)}, u32[]{:S(2)}, u32[]{:S(2)}) collective-permute-start(f32[16,4,2,8,128]{4,3,2,1,0:T(8,128)} %get-tuple-element.54), channel_id=1, source_target_pairs={{1,2},{3,4},{5,6},{7,8},{9,10},{11,12},{13,14},{15,16},{17,18},{19... | collective-permute-start | bytes 1572872 | tf_op jit(solution)/shard_map/ppermute | solution.py:519
  49.3 8.8 %collective-permute-start.3 = (f32[16,4,2,8,128]{4,3,2,1,0:T(8,128)}, f32[16,4,2,8,128]{4,3,2,1,0:T(8,128)S(1)}, u32[]{:S(2)}, u32[]{:S(2)}) collective-permute-start(f32[16,4,2,8,128]{4,3,2,1,0:T(8,128)} %get-tuple-element.55), channel_id=1, source_target_pairs={{0,1},{1,0},{2,3},{3,2},{4,5},{5,4},{6,7},{7,6},{8,9},{9,8},{10,11... | collective-permute-start | bytes 1572872 | tf_op jit(solution)/shard_map/ppermute | solution.py:520
  74.1 6.3 %collective-permute-start.6 = (f32[4,128]{1,0:T(4,128)S(1)}, f32[4,128]{1,0:T(4,128)S(1)}, u32[]{:S(2)}, u32[]{:S(2)}) collective-permute-start(f32[4,128]{1,0:T(4,128)S(1)} %get-tuple-element.62.refs_0_), channel_id=1, source_target_pairs={{0,9},{1,8},{2,11},{3,10},{4,13},{5,12},{6,15},{7,14},{8,1},{9,0},... | collective-permute-start | bytes 6152 | tf_op jit(solution)/shard_map/ppermute | solution.py:596
  75.9 4.6 %collective-permute-start.5 = (f32[4,128]{1,0:T(4,128)S(1)}, f32[4,128]{1,0:T(4,128)S(1)}, u32[]{:S(2)}, u32[]{:S(2)}) collective-permute-start(f32[4,128]{1,0:T(4,128)S(1)} %get-tuple-element.62.refs_0_), channel_id=1, source_target_pairs={{0,8},{1,9},{2,10},{3,11},{4,12},{5,13},{6,14},{7,15},{8,0},{9,1},... | collective-permute-start | bytes 6152 | tf_op jit(solution)/shard_map/ppermute | solution.py:596
  76.2 4.2 %collective-permute-start.4 = (f32[4,128]{1,0:T(4,128)S(1)}, f32[4,128]{1,0:T(4,128)S(1)}, u32[]{:S(2)}, u32[]{:S(2)}) collective-permute-start(f32[4,128]{1,0:T(4,128)S(1)} %get-tuple-element.62.refs_0_), channel_id=1, source_target_pairs={{0,1},{1,0},{2,3},{3,2},{4,5},{5,4},{6,7},{7,6},{8,9},{9,8},{10,11... | collective-permute-start | bytes 6152 | tf_op jit(solution)/shard_map/ppermute | solution.py:596
  80.5 23.4 %collective-permute-start.10 = (f32[16,2,8,128]{3,2,1,0:T(8,128)}, f32[16,2,8,128]{3,2,1,0:T(8,128)S(1)}, u32[]{:S(2)}, u32[]{:S(2)}) collective-permute-start(f32[16,2,8,128]{3,2,1,0:T(8,128)} %get-tuple-element.75), channel_id=1, source_target_pairs={{0,64},{64,128},{128,192},{192,0},{1,65},{65,129},{129,193},{193,1... | collective-permute-start | bytes 393224 | tf_op jit(solution)/shard_map/ppermute | solution.py:590
  83.9 20.0 %collective-permute-start.11 = (f32[16,2,8,128]{3,2,1,0:T(8,128)}, f32[16,2,8,128]{3,2,1,0:T(8,128)S(1)}, u32[]{:S(2)}, u32[]{:S(2)}) collective-permute-start(f32[16,2,8,128]{3,2,1,0:T(8,128)} %get-tuple-element.76), channel_id=1, source_target_pairs={{0,128},{64,192},{128,0},{192,64},{1,129},{65,193},{129,1},{193,65... | collective-permute-start | bytes 393224 | tf_op jit(solution)/shard_map/ppermute | solution.py:590
  89.1 20.1 %collective-permute-start.12 = (f32[16,2,8,128]{3,2,1,0:T(8,128)}, f32[16,2,8,128]{3,2,1,0:T(8,128)S(1)}, u32[]{:S(2)}, u32[]{:S(2)}) collective-permute-start(f32[16,2,8,128]{3,2,1,0:T(8,128)} %get-tuple-element.82), channel_id=1, source_target_pairs={{0,192},{64,0},{128,64},{192,128},{1,193},{65,1},{129,65},{193,129... | collective-permute-start | bytes 393224 | tf_op jit(solution)/shard_map/ppermute | solution.py:590
  91.7 7.1 %collective-permute-start.9 = (f32[4,128]{1,0:T(4,128)S(1)}, f32[4,128]{1,0:T(4,128)S(1)}, u32[]{:S(2)}, u32[]{:S(2)}) collective-permute-start(f32[4,128]{1,0:T(4,128)S(1)} %add.7.refs_0_), channel_id=1, source_target_pairs={{0,6},{1,7},{2,4},{3,5},{4,2},{5,3},{6,0},{7,1},{8,14},{9,15},{10,... | collective-permute-start | bytes 6152 | tf_op jit(solution)/shard_map/ppermute | solution.py:596
  93.3 10.5 %collective-permute-start.8 = (f32[4,128]{1,0:T(4,128)S(1)}, f32[4,128]{1,0:T(4,128)S(1)}, u32[]{:S(2)}, u32[]{:S(2)}) collective-permute-start(f32[4,128]{1,0:T(4,128)S(1)} %add.7.refs_0_), channel_id=1, source_target_pairs={{0,4},{1,5},{2,6},{3,7},{4,0},{5,1},{6,2},{7,3},{8,12},{9,13},{10,... | collective-permute-start | bytes 6152 | tf_op jit(solution)/shard_map/ppermute | solution.py:596
  98.9 5.0 %collective-permute-start.7 = (f32[4,128]{1,0:T(4,128)S(1)}, f32[4,128]{1,0:T(4,128)S(1)}, u32[]{:S(2)}, u32[]{:S(2)}) collective-permute-start(f32[4,128]{1,0:T(4,128)S(1)} %add.7.refs_0_), channel_id=1, source_target_pairs={{0,2},{1,3},{2,0},{3,1},{4,6},{5,7},{6,4},{7,5},{8,10},{9,11},{10,... | collective-permute-start | bytes 6152 | tf_op jit(solution)/shard_map/ppermute | solution.py:596
  103.9 5.2 %copy-start.5 = (f32[16,2,8,128]{3,2,1,0:T(8,128)}, f32[16,2,8,128]{3,2,1,0:T(8,128)S(1)}, u32[]{:S(2)}) copy-start(f32[16,2,8,128]{3,2,1,0:T(8,128)S(1)} %collective-permute-done.10.b) | copy-start | bytes 393220
  103.9 5.2 %copy-start.6 = (f32[16,2,8,128]{3,2,1,0:T(8,128)}, f32[16,2,8,128]{3,2,1,0:T(8,128)S(1)}, u32[]{:S(2)}) copy-start(f32[16,2,8,128]{3,2,1,0:T(8,128)S(1)} %collective-permute-done.11.c) | copy-start | bytes 393220
  103.9 7.7 %collective-permute-start.15 = (f32[4,128]{1,0:T(4,128)S(1)}, f32[4,128]{1,0:T(4,128)S(1)}, u32[]{:S(2)}, u32[]{:S(2)}) collective-permute-start(f32[4,128]{1,0:T(4,128)S(1)} %add.8.refs_0_), channel_id=1, source_target_pairs={{0,48},{1,49},{2,50},{3,51},{4,52},{5,53},{6,54},{7,55},{8,56},{9,... | collective-permute-start | bytes 6152 | tf_op jit(solution)/shard_map/ppermute | solution.py:596
  108.2 5.1 %collective-permute-start.14 = (f32[4,128]{1,0:T(4,128)S(1)}, f32[4,128]{1,0:T(4,128)S(1)}, u32[]{:S(2)}, u32[]{:S(2)}) collective-permute-start(f32[4,128]{1,0:T(4,128)S(1)} %add.8.refs_0_), channel_id=1, source_target_pairs={{0,32},{1,33},{2,34},{3,35},{4,36},{5,37},{6,38},{7,39},{8,40},{9,... | collective-permute-start | bytes 6152 | tf_op jit(solution)/shard_map/ppermute | solution.py:596
  109.0 4.3 %collective-permute-start.13 = (f32[4,128]{1,0:T(4,128)S(1)}, f32[4,128]{1,0:T(4,128)S(1)}, u32[]{:S(2)}, u32[]{:S(2)}) collective-permute-start(f32[4,128]{1,0:T(4,128)S(1)} %add.8.refs_0_), channel_id=1, source_target_pairs={{0,16},{1,17},{2,18},{3,19},{4,20},{5,21},{6,22},{7,23},{8,24},{9,... | collective-permute-start | bytes 6152 | tf_op jit(solution)/shard_map/ppermute | solution.py:596
  109.1 0.7 copy-start.7

commit v8 on v7

--- a/solution.py
+++ b/solution.py
@@ -206,9 +206,9 @@
 
     half = WIDTH // 2
     fetch[3].wait()
-    fetch[4].wait()
     load_rows(e_in, ea, 1.0, 0, half)
     load_rows(e_in, eb, 1.0, half, half)
+    fetch[4].wait()
     load_rows(h_in, ha, 1.0 / COEF_H, 0, half, 1)
     load_rows(h_in, hb, 1.0 / COEF_H, half, half, 1)
     free_run(ea, ha, eb, hb, coef, faces, swaps(info, faces, inter_far, intra_far, sent))
@@ -613,7 +613,7 @@
     )(here(e_last), here(h_last))
     total = stage(over, (1, 8))
     total, *parts = lax.optimization_barrier((total, *parts))
-    for d in range(1, ports):
+    for d in (2, 1, 3):
         parts[d] = to_port(parts[d], d)
     total = stage(total, (2, 4))
     total, e_out, h_out, parts[1], parts[2] = lax.optimization_barrier((total, e_out, h_out, parts[1], parts[2]))

time: 114 us -> 114 us (level)
  no operation moved by 1% of the time
where the time goes in v8:
time: 114 us
  Pallas kernels  65.8 us (58%)
  starting transfers between devices  35.8 us (31%)
  waiting for transfers between devices  7.79 us (7%)
  local copies, waits for them, and re-layouts  2.55 us (2%)
  between operations  1.46 us (1%)
    pallas_call x1, Pallas kernels, body(): pl.pallas_call(functools.partial(round_kernel, False, scale), out_shape=(...  23 us
    ppermute x9, starting transfers between devices, stage(): lax.ppermute(total, 'tile', [(i, i ^ flip) for i in range(tiles)])  17.2 us
    pallas_call x1, Pallas kernels, body(): pl.pallas_call(functools.partial(round_kernel, True, scale), out_shape=(h...  16.1 us
    ppermute x3, starting transfers between devices, to_port(): return lax.ppermute(x, 'port', [(i, (i + d) % ports) for i in range(ports)])  11.2 us
    pallas_call x1, Pallas kernels, body(): pl.pallas_call(free_kernel, out_shape=(f32(WIDTH, *CELLS),) + sent(planes...  10.6 us
    ppermute x2, waiting for transfers between devices, swap(): lax.ppermute(inter, 'tile', across + [(j, i) for i, j in across])  6.07 us
    pallas_call x1, Pallas kernels, body(): pl.pallas_call(finish_kernel, out_shape=(pltpu.HBM((WIDTH, HALF, 8, 128),...  4.2 us
    pallas_call x1, Pallas kernels, body(): pl.pallas_call(wide_kernel, out_shape=(turned_shape, f32(64, 128), fields...  4.02 us
  transfers between devices with their start and end apart: 16, of which 3 were waited for; matrix products, arithmetic and copies ran while one was open for 0% of the time, Pallas kernels for 14%

profile of v8, /device:TPU:8, one launch (start us, length us, event | category | flops | bytes accessed | tf_op | source)
XLA Modules:
  0.0 113.5 jit_solution(11229853899432302828)
XLA Ops:
  1.3 0.1 pad_add_fusion.info
  1.4 10.6 %free.1 = (f32[16,4,2,8,128]{4,3,2,1,0:T(8,128)S(1)}, f32[20,4,2,8,128]{4,3,2,1,0:T(8,128)}, f32[20,4,2,8,128]{4,3,2,1,0:T(8,128)}) custom-call(s32[3]{0:T(128)S(1)} %pad_add_fusion.info, f32[4]{0:T(128)} %table.1, s32[64,16]{1,0:T(8,128)} %bitcast.50, s32[64,16]{1,0:T(8,128)} %bitcast.45, f32[16,64,128]{2,1,0:T(8,128)} %bitcast.48, ...), custom_call_target="tpu_custom_call" | custom-call | tf_op jit(solution)/shard_map/free/pallas_call | solution.py:493
  12.0 1.9 %collective-permute-start = (f32[20,4,2,8,128]{4,3,2,1,0:T(8,128)}, f32[20,4,2,8,128]{4,3,2,1,0:T(8,128)S(1)}, u32[]{:S(2)}, u32[]{:S(2)}) collective-permute-start(f32[20,4,2,8,128]{4,3,2,1,0:T(8,128)} %get-tuple-element.50), channel_id=1, source_target_pairs={{1,2},{3,4},{5,6},{7,8},{9,10},{11,12},{13,14},{15,16},{17,18},{19... | collective-permute-start | bytes 1966088 | tf_op jit(solution)/shard_map/ppermute | solution.py:519
  13.9 1.8 %collective-permute-start.1 = (f32[20,4,2,8,128]{4,3,2,1,0:T(8,128)}, f32[20,4,2,8,128]{4,3,2,1,0:T(8,128)S(1)}, u32[]{:S(2)}, u32[]{:S(2)}) collective-permute-start(f32[20,4,2,8,128]{4,3,2,1,0:T(8,128)} %get-tuple-element.51), channel_id=1, source_target_pairs={{0,1},{1,0},{2,3},{3,2},{4,5},{5,4},{6,7},{7,6},{8,9},{9,8},{10,11... | collective-permute-start | bytes 1966088 | tf_op jit(solution)/shard_map/ppermute | solution.py:520
  15.6 0.0 copy-done
  15.7 0.0 copy-done.1
  15.7 0.0 copy-start.2
  15.7 1.9 %copy-done.2 = bf16[1,2,2,3,16,4,2048]{6,5,4,3,2,1,0:T(4,128)(2,1)S(1)} copy-done((bf16[1,2,2,3,16,4,2048]{6,5,4,3,2,1,0:T(4,128)(2,1)S(1)}, bf16[1,2,2,3,16,4,2048]{6,5,4,3,2,1,0:T(4,128)(2,1)}, u32[]{:S(2)}) %copy-start.2) | copy-done | bytes 3145752
  17.6 4.0 %wide.1 = (f32[2,2,3,4,16,2,8,128]{7,6,5,4,3,2,1,0:T(8,128)S(1)}, f32[64,128]{1,0:T(8,128)S(1)}, f32[3,17,4,2,8,128]{5,4,3,2,1,0:T(8,128)S(1)}, f32[3,17,4,2,8,128]{5,4,3,2,1,0:T(8,128)S(1)}) custom-call(bf16[2,2,3,16,64,128]{5,4,3,2,1,0:T(8,128)(2,1)S(1)} %bitcast.44, s32[64,16]{1,0:T(8,128)S(1)} %bitcast.46, f32[64,128]{1,0:T(8,128)S(1)} %bitcast.47, ...), custom_call_target="tpu_custom_call" | custom-call | tf_op jit(solution)/shard_map/wide/pallas_call | solution.py:528
  21.6 2.5 %collective-permute-done.inter = f32[20,4,2,8,128]{4,3,2,1,0:T(8,128)S(1)} collective-permute-done((f32[20,4,2,8,128]{4,3,2,1,0:T(8,128)}, f32[20,4,2,8,128]{4,3,2,1,0:T(8,128)S(1)}, u32[]{:S(2)}, u32[]{:S(2)}) %collective-permute-start) | collective-permute-done | bytes 655392 | tf_op jit(solution)/shard_map/ppermute | solution.py:519
  24.1 0.0 collective-permute-done.1.intra
  24.1 23.0 %round.2 = (f32[8,3,16,4,2,8,128]{6,5,4,3,2,1,0:T(8,128)S(1)}, f32[3,17,4,2,8,128]{5,4,3,2,1,0:T(8,128)S(1)}, f32[3,17,4,2,8,128]{5,4,3,2,1,0:T(8,128)S(1)}, f32...) custom-call(s32[3]{0:T(128)S(1)} %pad_add_fusion.info, ...), custom_call_target="tpu_custom_call" | custom-call | tf_op jit(solution)/shard_map/round/pallas_call | solution.py:549
  47.0 1.9 %collective-permute-start.2 = (f32[16,4,2,8,128]{4,3,2,1,0:T(8,128)}, f32[16,4,2,8,128]{4,3,2,1,0:T(8,128)S(1)}, u32[]{:S(2)}, u32[]{:S(2)}) collective-permute-start(f32[16,4,2,8,128]{4,3,2,1,0:T(8,128)} %get-tuple-element.54), channel_id=1, source_target_pairs={{1,2},{3,4},{5,6},{7,8},{9,10},{11,12},{13,14},{15,16},{17,18},{19... | collective-permute-start | bytes 1572872 | tf_op jit(solution)/shard_map/ppermute | solution.py:519
  49.0 1.8 %collective-permute-start.3 = (f32[16,4,2,8,128]{4,3,2,1,0:T(8,128)}, f32[16,4,2,8,128]{4,3,2,1,0:T(8,128)S(1)}, u32[]{:S(2)}, u32[]{:S(2)}) collective-permute-start(f32[16,4,2,8,128]{4,3,2,1,0:T(8,128)} %get-tuple-element.55), channel_id=1, source_target_pairs={{0,1},{1,0},{2,3},{3,2},{4,5},{5,4},{6,7},{7,6},{8,9},{9,8},{10,11... | collective-permute-start | bytes 1572872 | tf_op jit(solution)/shard_map/ppermute | solution.py:520
  50.7 3.4 %first.1 = (f32[4,16,2,8,128]{4,3,2,1,0:T(8,128)S(1)}, f32[2,2,3,4,16,2,8,128]{7,6,5,4,3,2,1,0:T(8,128)S(1)}) custom-call(f32[8,3,16,4,2,8,128]{6,5,4,3,2,1,0:T(8,128)S(1)} %get-tuple-element.58.e, f32[2,2,3,4,16,2,8,128]{7,6,5,4,3,2,1,0:T(8,128)S(1)} %get-tuple-element.59.turned), custom_call_target="tpu_custom_call" | custom-call | tf_op jit(solution)/shard_map/first/pallas_call | solution.py:561
  54.2 3.6 %collective-permute-done.2.rest_0_ = f32[16,4,2,8,128]{4,3,2,1,0:T(8,128)S(1)} collective-permute-done((f32[16,4,2,8,128]{4,3,2,1,0:T(8,128)}, f32[16,4,2,8,128]{4,3,2,1,0:T(8,128)S(1)}, u32[]{:S(2)}, u32[]{:S(2)}) %collective-permute-start.2) | collective-permute-done | bytes 524320 | tf_op jit(solution)/shard_map/ppermute | solution.py:519
  57.7 0.0 collective-permute-done.3.rest_1_
  57.7 16.1 %round.3 = (f32[8,3,16,4,2,8,128]{6,5,4,3,2,1,0:T(8,128)S(1)}, f32[3,17,4,2,8,128]{5,4,3,2,1,0:T(8,128)S(1)}, f32[3,17,4,2,8,128]{5,4,3,2,1,0:T(8,128)S(1)}, f32[4,128]{1,0:T(4,128)S(1)}) custom-call(s32[3]{0:T(128)S(1)} %pad_add_fusion.info, f32[3,17,4,2,8,128]{5,4,3,2,1,0:T(8,128)S(1)} %get-tuple-element.52.e_in, ...), custom_call_target="tpu_custom_call" | custom-call | tf_op jit(solution)/shard_map/round/pallas_call | solution.py:570
  73.8 1.7 %collective-permute-start.6 = (f32[4,128]{1,0:T(4,128)S(1)}, f32[4,128]{1,0:T(4,128)S(1)}, u32[]{:S(2)}, u32[]{:S(2)}) collective-permute-start(f32[4,128]{1,0:T(4,128)S(1)} %get-tuple-element.62.refs_0_), channel_id=1, source_target_pairs={{0,9},{1,8},{2,11},{3,10},{4,13},{5,12},{6,15},{7,14},{8,1},{9,0},... | collective-permute-start | bytes 6152 | tf_op jit(solution)/shard_map/ppermute | solution.py:596
  75.5 0.4 collective-permute-start.5
  75.9 0.0 collective-permute-start.4
  75.9 4.2 %finish.1 = (f32[16,2,8,128]{3,2,1,0:T(8,128)}, f32[16,2,8,128]{3,2,1,0:T(8,128)}, f32[16,2,8,128]{3,2,1,0:T(8,128)}, f32[16,2,8,128]{3,2,1,0:T(8,128)}) custom-call(s32[3]{0:T(128)S(1)} %pad_add_fusion.info, f32[8,3,16,4,2,8,128]{6,5,4,3,2,1,0:T(8,128)S(1)} %get-tuple-element.63.e, f32[2,2,3,4,16,2,8,128]{7,6,5,4,3,2,1,0:T(8,128)S(1)} %get-tuple-element.64.turned, ...), custom_call_target="tpu_custom_call" | custom-call | tf_op jit(solution)/shard_map/finish/pallas_call | solution.py:579
  80.1 0.0 collective-permute-done.6.refs_3_
  80.2 0.0 collective-permute-done.5.refs_2_
  80.2 0.0 collective-permute-done.4.refs_1_
  80.2 3.3 %collective-permute-start.10 = (f32[16,2,8,128]{3,2,1,0:T(8,128)}, f32[16,2,8,128]{3,2,1,0:T(8,128)S(1)}, u32[]{:S(2)}, u32[]{:S(2)}) collective-permute-start(f32[16,2,8,128]{3,2,1,0:T(8,128)} %get-tuple-element.75), channel_id=1, source_target_pairs={{0,64},{64,128},{128,192},{192,0},{1,65},{65,129},{129,193},{193,1... | collective-permute-start | bytes 393224 | tf_op jit(solution)/shard_map/ppermute | solution.py:590
  83.5 5.2 %collective-permute-start.11 = (f32[16,2,8,128]{3,2,1,0:T(8,128)}, f32[16,2,8,128]{3,2,1,0:T(8,128)S(1)}, u32[]{:S(2)}, u32[]{:S(2)}) collective-permute-start(f32[16,2,8,128]{3,2,1,0:T(8,128)} %get-tuple-element.76), channel_id=1, source_target_pairs={{0,128},{64,192},{128,0},{192,64},{1,129},{65,193},{129,1},{193,65... | collective-permute-start | bytes 393224 | tf_op jit(solution)/shard_map/ppermute | solution.py:590
  88.8 2.7 %collective-permute-start.12 = (f32[16,2,8,128]{3,2,1,0:T(8,128)}, f32[16,2,8,128]{3,2,1,0:T(8,128)S(1)}, u32[]{:S(2)}, u32[]{:S(2)}) collective-permute-start(f32[16,2,8,128]{3,2,1,0:T(8,128)} %get-tuple-element.82), channel_id=1, source_target_pairs={{0,192},{64,0},{128,64},{192,128},{1,193},{65,1},{129,65},{193,129... | collective-permute-start | bytes 393224 | tf_op jit(solution)/shard_map/ppermute | solution.py:590
  91.4 1.6 %collective-permute-start.9 = (f32[4,128]{1,0:T(4,128)S(1)}, f32[4,128]{1,0:T(4,128)S(1)}, u32[]{:S(2)}, u32[]{:S(2)}) collective-permute-start(f32[4,128]{1,0:T(4,128)S(1)} %add.7.refs_0_), channel_id=1, source_target_pairs={{0,6},{1,7},{2,4},{3,5},{4,2},{5,3},{6,0},{7,1},{8,14},{9,15},{10,... | collective-permute-start | bytes 6152 | tf_op jit(solution)/shard_map/ppermute | solution.py:596
  93.0 5.5 %collective-permute-start.8 = (f32[4,128]{1,0:T(4,128)S(1)}, f32[4,128]{1,0:T(4,128)S(1)}, u32[]{:S(2)}, u32[]{:S(2)}) collective-permute-start(f32[4,128]{1,0:T(4,128)S(1)} %add.7.refs_0_), channel_id=1, source_target_pairs={{0,4},{1,5},{2,6},{3,7},{4,0},{5,1},{6,2},{7,3},{8,12},{9,13},{10,... | collective-permute-start | bytes 6152 | tf_op jit(solution)/shard_map/ppermute | solution.py:596
  98.5 0.0 collective-permute-done.9.refs_3_
  98.5 2.7 %collective-permute-start.7 = (f32[4,128]{1,0:T(4,128)S(1)}, f32[4,128]{1,0:T(4,128)S(1)}, u32[]{:S(2)}, u32[]{:S(2)}) collective-permute-start(f32[4,128]{1,0:T(4,128)S(1)} %add.7.refs_0_), channel_id=1, source_target_pairs={{0,2},{1,3},{2,0},{3,1},{4,6},{5,7},{6,4},{7,5},{8,10},{9,11},{10,... | collective-permute-start | bytes 6152 | tf_op jit(solution)/shard_map/ppermute | solution.py:596
  101.3 2.3 %out.1 = (f32[3,16,64,128]{3,2,1,0:T(8,128)}, f32[3,16,64,128]{3,2,1,0:T(8,128)}) custom-call(f32[3,17,4,2,8,128]{5,4,3,2,1,0:T(8,128)S(1)} %get-tuple-element.71.e, f32[3,17,4,2,8,128]{5,4,3,2,1,0:T(8,128)S(1)} %get-tuple-element.72.h), custom_call_target="tpu_custom_call" | custom-call | tf_op jit(solution)/shard_map/out/pallas_call | solution.py:606
  103.5 0.0 collective-permute-done.8.refs_2_
  103.5 0.0 collective-permute-done.7.refs_1_
  103.5 0.0 collective-permute-done.10.b
  103.6 0.0 collective-permute-done.11.c
  103.6 0.0 copy-start.6
  103.6 4.3 %collective-permute-start.15 = (f32[4,128]{1,0:T(4,128)S(1)}, f32[4,128]{1,0:T(4,128)S(1)}, u32[]{:S(2)}, u32[]{:S(2)}) collective-permute-start(f32[4,128]{1,0:T(4,128)S(1)} %add.8.refs_0_), channel_id=1, source_target_pairs={{0,48},{1,49},{2,50},{3,51},{4,52},{5,53},{6,54},{7,55},{8,56},{9,... | collective-permute-start | bytes 6152 | tf_op jit(solution)/shard_map/ppermute | solution.py:596
  107.8 0.8 collective-permute-start.14
  108.6 0.2 collective-permute-start.13
  108.8 0.0 collective-permute-done.12.d
  108.8 0.6 copy-done.7
  109.5 1.8 %total.1 = f32[16,16,128]{2,1,0:T(8,128)} custom-call(f32[16,2,8,128]{3,2,1,0:T(8,128)} %get-tuple-element.79.a, f32[16,2,8,128]{3,2,1,0:T(8,128)} %copy-done.5, f32[16,2,8,128]{3,2,1,0:T(8,128)} %copy-done.6, f32[16,2,8,128]{3,2,1,0:T(8,128)} %copy-done.7), custom_call_target="tpu_custom_call" | custom-call | tf_op jit(solution)/shard_map/total/pallas_call | solution.py:621
  111.2 0.0 collective-permute-done.15.refs_3_
  111.2 1.7 %collective-permute-done.14.refs_2_ = f32[4,128]{1,0:T(4,128)S(1)} collective-permute-done((f32[4,128]{1,0:T(4,128)S(1)}, f32[4,128]{1,0:T(4,128)S(1)}, u32[]{:S(2)}, u32[]{:S(2)}) %collective-permute-start.14) | collective-permute-done | bytes 2080 | tf_op jit(solution)/shard_map/ppermute | solution.py:596
  112.9 0.0 collective-permute-done.13.refs_1_
  112.9 0.6 add.9
  (12 shorter events, 0.0 us)
Async XLA Ops:
  1.4 14.3 %copy-start = (f32[1,3,16,4,2048]{4,3,2,1,0:T(4,128)S(1)}, f32[1,3,16,4,2048]{4,3,2,1,0:T(4,128)}, u32[]{:S(2)}) copy-start(f32[1,3,16,4,2048]{4,3,2,1,0:T(4,128)} %param.9) | copy-start | bytes 4718596
  1.4 14.3 %copy-start.1 = (f32[1,3,16,4,2048]{4,3,2,1,0:T(4,128)S(1)}, f32[1,3,16,4,2048]{4,3,2,1,0:T(4,128)}, u32[]{:S(2)}) copy-start(f32[1,3,16,4,2048]{4,3,2,1,0:T(4,128)} %param.10) | copy-start | bytes 4718596
  1.4 14.3 %copy-start.3 = (s32[16,4,16]{2,1,0:T(4,128)S(1)}, s32[16,4,16]{2,1,0:T(4,128)}, u32[]{:S(2)}) copy-start(s32[16,4,16]{2,1,0:T(4,128)} %param.14) | copy-start | bytes 12292
  1.4 14.3 %copy-start.4 = (f32[4,2048]{1,0:T(4,128)S(1)}, f32[4,2048]{1,0:T(4,128)}, u32[]{:S(2)}) copy-start(f32[4,2048]{1,0:T(4,128)} %param.16) | copy-start | bytes 98308
  12.0 12.1 %collective-permute-start = (f32[20,4,2,8,128]{4,3,2,1,0:T(8,128)}, f32[20,4,2,8,128]{4,3,2,1,0:T(8,128)S(1)}, u32[]{:S(2)}, u32[]{:S(2)}) collective-permute-start(f32[20,4,2,8,128]{4,3,2,1,0:T(8,128)} %get-tuple-element.50), channel_id=1, source_target_pairs={{1,2},{3,4},{5,6},{7,8},{9,10},{11,12},{13,14},{15,16},{17,18},{19... | collective-permute-start | bytes 1966088 | tf_op jit(solution)/shard_map/ppermute | solution.py:519
  13.9 10.2 %collective-permute-start.1 = (f32[20,4,2,8,128]{4,3,2,1,0:T(8,128)}, f32[20,4,2,8,128]{4,3,2,1,0:T(8,128)S(1)}, u32[]{:S(2)}, u32[]{:S(2)}) collective-permute-start(f32[20,4,2,8,128]{4,3,2,1,0:T(8,128)} %get-tuple-element.51), channel_id=1, source_target_pairs={{0,1},{1,0},{2,3},{3,2},{4,5},{5,4},{6,7},{7,6},{8,9},{9,8},{10,11... | collective-permute-start | bytes 1966088 | tf_op jit(solution)/shard_map/ppermute | solution.py:520
  15.7 1.9 %copy-start.2 = (bf16[1,2,2,3,16,4,2048]{6,5,4,3,2,1,0:T(4,128)(2,1)S(1)}, bf16[1,2,2,3,16,4,2048]{6,5,4,3,2,1,0:T(4,128)(2,1)}, u32[]{:S(2)}) copy-start(bf16[1,2,2,3,16,4,2048]{6,5,4,3,2,1,0:T(4,128)(2,1)} %param.11) | copy-start | bytes 9437188
  47.0 10.7 %collective-permute-start.2 = (f32[16,4,2,8,128]{4,3,2,1,0:T(8,128)}, f32[16,4,2,8,128]{4,3,2,1,0:T(8,128)S(1)}, u32[]{:S(2)}, u32[]{:S(2)}) collective-permute-start(f32[16,4,2,8,128]{4,3,2,1,0:T(8,128)} %get-tuple-element.54), channel_id=1, source_target_pairs={{1,2},{3,4},{5,6},{7,8},{9,10},{11,12},{13,14},{15,16},{17,18},{19... | collective-permute-start | bytes 1572872 | tf_op jit(solution)/shard_map/ppermute | solution.py:519
  49.0 8.8 %collective-permute-start.3 = (f32[16,4,2,8,128]{4,3,2,1,0:T(8,128)}, f32[16,4,2,8,128]{4,3,2,1,0:T(8,128)S(1)}, u32[]{:S(2)}, u32[]{:S(2)}) collective-permute-start(f32[16,4,2,8,128]{4,3,2,1,0:T(8,128)} %get-tuple-element.55), channel_id=1, source_target_pairs={{0,1},{1,0},{2,3},{3,2},{4,5},{5,4},{6,7},{7,6},{8,9},{9,8},{10,11... | collective-permute-start | bytes 1572872 | tf_op jit(solution)/shard_map/ppermute | solution.py:520
  73.8 6.3 %collective-permute-start.6 = (f32[4,128]{1,0:T(4,128)S(1)}, f32[4,128]{1,0:T(4,128)S(1)}, u32[]{:S(2)}, u32[]{:S(2)}) collective-permute-start(f32[4,128]{1,0:T(4,128)S(1)} %get-tuple-element.62.refs_0_), channel_id=1, source_target_pairs={{0,9},{1,8},{2,11},{3,10},{4,13},{5,12},{6,15},{7,14},{8,1},{9,0},... | collective-permute-start | bytes 6152 | tf_op jit(solution)/shard_map/ppermute | solution.py:596
  75.5 4.6 %collective-permute-start.5 = (f32[4,128]{1,0:T(4,128)S(1)}, f32[4,128]{1,0:T(4,128)S(1)}, u32[]{:S(2)}, u32[]{:S(2)}) collective-permute-start(f32[4,128]{1,0:T(4,128)S(1)} %get-tuple-element.62.refs_0_), channel_id=1, source_target_pairs={{0,8},{1,9},{2,10},{3,11},{4,12},{5,13},{6,14},{7,15},{8,0},{9,1},... | collective-permute-start | bytes 6152 | tf_op jit(solution)/shard_map/ppermute | solution.py:596
  75.9 4.2 %collective-permute-start.4 = (f32[4,128]{1,0:T(4,128)S(1)}, f32[4,128]{1,0:T(4,128)S(1)}, u32[]{:S(2)}, u32[]{:S(2)}) collective-permute-start(f32[4,128]{1,0:T(4,128)S(1)} %get-tuple-element.62.refs_0_), channel_id=1, source_target_pairs={{0,1},{1,0},{2,3},{3,2},{4,5},{5,4},{6,7},{7,6},{8,9},{9,8},{10,11... | collective-permute-start | bytes 6152 | tf_op jit(solution)/shard_map/ppermute | solution.py:596
  80.2 23.4 %collective-permute-start.10 = (f32[16,2,8,128]{3,2,1,0:T(8,128)}, f32[16,2,8,128]{3,2,1,0:T(8,128)S(1)}, u32[]{:S(2)}, u32[]{:S(2)}) collective-permute-start(f32[16,2,8,128]{3,2,1,0:T(8,128)} %get-tuple-element.75), channel_id=1, source_target_pairs={{0,64},{64,128},{128,192},{192,0},{1,65},{65,129},{129,193},{193,1... | collective-permute-start | bytes 393224 | tf_op jit(solution)/shard_map/ppermute | solution.py:590
  83.5 20.0 %collective-permute-start.11 = (f32[16,2,8,128]{3,2,1,0:T(8,128)}, f32[16,2,8,128]{3,2,1,0:T(8,128)S(1)}, u32[]{:S(2)}, u32[]{:S(2)}) collective-permute-start(f32[16,2,8,128]{3,2,1,0:T(8,128)} %get-tuple-element.76), channel_id=1, source_target_pairs={{0,128},{64,192},{128,0},{192,64},{1,129},{65,193},{129,1},{193,65... | collective-permute-start | bytes 393224 | tf_op jit(solution)/shard_map/ppermute | solution.py:590
  88.8 20.1 %collective-permute-start.12 = (f32[16,2,8,128]{3,2,1,0:T(8,128)}, f32[16,2,8,128]{3,2,1,0:T(8,128)S(1)}, u32[]{:S(2)}, u32[]{:S(2)}) collective-permute-start(f32[16,2,8,128]{3,2,1,0:T(8,128)} %get-tuple-element.82), channel_id=1, source_target_pairs={{0,192},{64,0},{128,64},{192,128},{1,193},{65,1},{129,65},{193,129... | collective-permute-start | bytes 393224 | tf_op jit(solution)/shard_map/ppermute | solution.py:590
  91.4 7.1 %collective-permute-start.9 = (f32[4,128]{1,0:T(4,128)S(1)}, f32[4,128]{1,0:T(4,128)S(1)}, u32[]{:S(2)}, u32[]{:S(2)}) collective-permute-start(f32[4,128]{1,0:T(4,128)S(1)} %add.7.refs_0_), channel_id=1, source_target_pairs={{0,6},{1,7},{2,4},{3,5},{4,2},{5,3},{6,0},{7,1},{8,14},{9,15},{10,... | collective-permute-start | bytes 6152 | tf_op jit(solution)/shard_map/ppermute | solution.py:596
  93.0 10.5 %collective-permute-start.8 = (f32[4,128]{1,0:T(4,128)S(1)}, f32[4,128]{1,0:T(4,128)S(1)}, u32[]{:S(2)}, u32[]{:S(2)}) collective-permute-start(f32[4,128]{1,0:T(4,128)S(1)} %add.7.refs_0_), channel_id=1, source_target_pairs={{0,4},{1,5},{2,6},{3,7},{4,0},{5,1},{6,2},{7,3},{8,12},{9,13},{10,... | collective-permute-start | bytes 6152 | tf_op jit(solution)/shard_map/ppermute | solution.py:596
  98.5 5.0 %collective-permute-start.7 = (f32[4,128]{1,0:T(4,128)S(1)}, f32[4,128]{1,0:T(4,128)S(1)}, u32[]{:S(2)}, u32[]{:S(2)}) collective-permute-start(f32[4,128]{1,0:T(4,128)S(1)} %add.7.refs_0_), channel_id=1, source_target_pairs={{0,2},{1,3},{2,0},{3,1},{4,6},{5,7},{6,4},{7,5},{8,10},{9,11},{10,... | collective-permute-start | bytes 6152 | tf_op jit(solution)/shard_map/ppermute | solution.py:596
  103.6 5.2 %copy-start.5 = (f32[16,2,8,128]{3,2,1,0:T(8,128)}, f32[16,2,8,128]{3,2,1,0:T(8,128)S(1)}, u32[]{:S(2)}) copy-start(f32[16,2,8,128]{3,2,1,0:T(8,128)S(1)} %collective-permute-done.10.b) | copy-start | bytes 393220
  103.6 5.2 %copy-start.6 = (f32[16,2,8,128]{3,2,1,0:T(8,128)}, f32[16,2,8,128]{3,2,1,0:T(8,128)S(1)}, u32[]{:S(2)}) copy-start(f32[16,2,8,128]{3,2,1,0:T(8,128)S(1)} %collective-permute-done.11.c) | copy-start | bytes 393220
  103.6 7.7 %collective-permute-start.15 = (f32[4,128]{1,0:T(4,128)S(1)}, f32[4,128]{1,0:T(4,128)S(1)}, u32[]{:S(2)}, u32[]{:S(2)}) collective-permute-start(f32[4,128]{1,0:T(4,128)S(1)} %add.8.refs_0_), channel_id=1, source_target_pairs={{0,48},{1,49},{2,50},{3,51},{4,52},{5,53},{6,54},{7,55},{8,56},{9,... | collective-permute-start | bytes 6152 | tf_op jit(solution)/shard_map/ppermute | solution.py:596
  107.8 5.1 %collective-permute-start.14 = (f32[4,128]{1,0:T(4,128)S(1)}, f32[4,128]{1,0:T(4,128)S(1)}, u32[]{:S(2)}, u32[]{:S(2)}) collective-permute-start(f32[4,128]{1,0:T(4,128)S(1)} %add.8.refs_0_), channel_id=1, source_target_pairs={{0,32},{1,33},{2,34},{3,35},{4,36},{5,37},{6,38},{7,39},{8,40},{9,... | collective-permute-start | bytes 6152 | tf_op jit(solution)/shard_map/ppermute | solution.py:596
  108.6 4.3 %collective-permute-start.13 = (f32[4,128]{1,0:T(4,128)S(1)}, f32[4,128]{1,0:T(4,128)S(1)}, u32[]{:S(2)}, u32[]{:S(2)}) collective-permute-start(f32[4,128]{1,0:T(4,128)S(1)} %add.8.refs_0_), channel_id=1, source_target_pairs={{0,16},{1,17},{2,18},{3,19},{4,20},{5,21},{6,22},{7,23},{8,24},{9,... | collective-permute-start | bytes 6152 | tf_op jit(solution)/shard_map/ppermute | solution.py:596
  108.8 0.7 copy-start.7
